TPU v7x, 32 devices: a whole 2x2x4 slice. The times are simulated.
32 devices in a mesh: expert: 8 (over y, x, core), tensor: 4 (over z).
Axes of the slice: x: 2, y: 2, z: 4, core: 2. Of those that a mesh axis runs over, the one named last changes fastest.
Arguments:
- residual: bfloat16 [512, 7168], P('expert', 'tensor'), may hold values from -40 to 40
- attn_parts: bfloat16 [4, 512, 7168], P('tensor', 'expert'), may hold values from -2 to 2
- norm_gain: bfloat16 [7168], P('tensor'), may hold values from 0.099609375 to 1.8984375
- routes: int32 [512, 2], P('expert'), may hold values from 0 to 7, all different within a row; in each aligned block of 64 rows (0 to 63, 64 to 127, ...) at most 24 rows name the same one
- route_weights: float32 [512, 2], P('expert'), may hold values from 0.05 to 0.6
- w_gate: bfloat16 [8, 7168, 2048], P('expert', None, 'tensor'), may hold values from -0.06023809 to 0.06023809
- w_gate_q: bfloat16 [8, 7168, 2048], P('expert', None, 'tensor'), may hold values from -0.09567226 to 0.09567226
Outputs:
- token_error: float32 [512], P('expert')
- expert_error: float32 [8], P('expert')
- hess_diag: float32 [8, 7168], P('expert', 'tensor')
Inputs may be any that keep to these rules, and one draw needn't show every extreme that they name: `routes`: no expert is named by more than 24 of the rows of one device, and in every draw some expert is named by exactly 24 of them; the 2 experts of a token are distinct; every expert is named by some token.
All inputs are finite; a program needn't handle non-finite values.
Results may differ from a plain program's by a relative error of at most 0.0023.
Values may be sent and summed in bfloat16 or wider, within the bound.
No kernel may reach another device: no remote copies, remote signals or barrier semaphores. Data moves between devices by JAX's collectives and lax.ppermute only.
A program may use at most 64 MiB of HBM per device.

v0:
```python
import jax
import jax.numpy as jnp
from jax import lax
from jax.sharding import PartitionSpec as P

D = 7168
FF = 2048
CAP = 24


epsilon = 1e-06


def per_device(residual, attn_parts, norm_gain, routes, route_weights, w_gate, w_gate_q):
    n_expert = lax.axis_size("expert")
    tok_count = residual.shape[0]
    local_cols = residual.shape[1]
    top_count = routes.shape[1]
    gain_wide = norm_gain.astype(jnp.float32)[None, :]
    summed = lax.psum_scatter(
        attn_parts[0].astype(jnp.float32).astype(jnp.bfloat16),
        "tensor",
        scatter_dimension=1,
        tiled=True,
    ).astype(jnp.float32)
    hidden = residual.astype(jnp.float32) + summed
    squares = lax.psum(jnp.sum(hidden * hidden, axis=1), "tensor")
    scaling = lax.rsqrt(squares / D + epsilon)
    normed = (hidden * scaling[:, None] * gain_wide).astype(jnp.bfloat16)
    expert_ids = jnp.arange(n_expert, dtype=jnp.int32)
    flat_routes = routes.reshape(-1)
    one_hot = (flat_routes[:, None] == expert_ids[None, :]).astype(jnp.int32)
    earlier = jnp.cumsum(one_hot, axis=0) - one_hot
    slot_index = jnp.sum(earlier * one_hot, axis=1)
    target = flat_routes * CAP + slot_index
    load_counts = jnp.sum(one_hot, axis=0)
    slot_ids = jnp.arange(n_expert * CAP, dtype=jnp.int32)
    placing = (slot_ids[:, None] == target[None, :]).reshape(n_expert * CAP, tok_count, top_count)
    dispatch = jnp.sum(placing.astype(jnp.int32), axis=2).astype(jnp.bfloat16)
    count_send = load_counts.astype(jnp.bfloat16).reshape(n_expert, 1)
    weight_full = w_gate[0]
    weight_quant = w_gate_q[0]
    outgoing = jnp.dot(dispatch, normed, preferred_element_type=jnp.float32).astype(jnp.bfloat16)
    outgoing = outgoing.reshape(n_expert, CAP, local_cols)
    arrived, arrived_counts = (
        lax.all_to_all(outgoing, "expert", split_axis=0, concat_axis=0, tiled=True),
        lax.all_to_all(count_send, "expert", split_axis=0, concat_axis=0, tiled=True),
    )
    own_block = arrived.reshape(n_expert * CAP, local_cols)
    column_block = lax.all_gather(own_block, "tensor", axis=1, tiled=True)
    full_acc = jnp.dot(column_block, weight_full, preferred_element_type=jnp.float32)
    quant_acc = jnp.dot(column_block, weight_quant, preferred_element_type=jnp.float32)
    block_squares = jnp.einsum("rc,rc->c", own_block, own_block, preferred_element_type=jnp.float32)
    total_load = jnp.sum(arrived_counts.astype(jnp.float32))
    hess_local = 2.0 * block_squares / total_load
    difference = full_acc - quant_acc
    err_part = (jnp.sum(difference * difference, axis=1) / FF).reshape(n_expert, CAP)
    pow_part = (jnp.sum(full_acc * full_acc, axis=1) / FF).reshape(n_expert, CAP)
    err_slots, pow_slots = lax.psum((err_part, pow_part), "tensor")
    expert_total = jnp.sum(err_slots) / (jnp.sum(pow_slots) + epsilon)
    back_err, back_pow = (
        lax.all_to_all(err_slots, "expert", split_axis=0, concat_axis=0, tiled=True),
        lax.all_to_all(pow_slots, "expert", split_axis=0, concat_axis=0, tiled=True),
    )
    token_err = jnp.take(back_err.reshape(-1), target).reshape(tok_count, top_count)
    token_pow = jnp.take(back_pow.reshape(-1), target).reshape(tok_count, top_count)
    ratios = token_err / (token_pow + epsilon)
    token_error = jnp.sum(route_weights * ratios, axis=1)
    return (token_error, expert_total.reshape(1), hess_local.reshape(1, local_cols))


def solution(mesh):
    placed = (
        P("expert", "tensor"),
        P("tensor", "expert", None),
        P("tensor"),
        P("expert", None),
        P("expert", None),
        P("expert", None, "tensor"),
        P("expert", None, "tensor"),
    )
    return jax.shard_map(
        per_device,
        mesh=mesh,
        in_specs=placed,
        out_specs=(P("expert"), P("expert"), P("expert", "tensor")),
        check_vma=False,
    )
```

profile of v0, /device:TPU:0, one launch (start us, length us, event | category | flops | bytes accessed | tf_op | source)
XLA Modules:
  0.0 170.2 jit_solution(7307798527935969382)
XLA Ops:
  7.2 0.0 copy-start.1
  7.2 0.0 reduce-scatter.2.cloned.1.call-start
  7.2 0.7 reduce-scatter.2.cloned.1.call-update
  7.9 0.0 all-gather.2.cloned.1.call-start
  8.0 0.7 convert_element_type.57
  8.6 0.8 copy.29
  9.4 0.1 eq.30
  9.6 0.1 fusion.16
  9.6 0.2 reduce_window_sum.11
  9.8 0.2 fusion.17
  10.0 0.1 reduce_sum.93
  10.1 0.1 copy.30
  10.2 0.7 multiply_add_fusion
  10.9 0.1 convert_reduce_fusion
  11.0 27.1 %reduce-scatter.2.cloned.1.call-done = bf16[64,1792]{1,0:T(8,128)(2,1)} async-done(((bf16[64,7168]{1,0:T(8,128)(2,1)}), bf16[64,1792]{1,0:T(8,128)(2,1)}) %reduce-scatter.2.cloned.1.call-update) | async-done | bytes 229392 | tf_op jit(solution)/shard_map/reduce_scatter | solution.py:20
  38.2 1.2 multiply_reduce_fusion
  39.4 9.7 %psum.21 = f32[64]{0:T(128)S(1)} all-reduce(f32[64]{0:T(128)S(1)} %multiply_reduce_fusion), channel_id=1, replica_groups=mesh['expert'=8,'tensor'=4] {'tensor'}, use_global_device_ids=true, to_apply=%region_5.6 | all-reduce | flops 64 | bytes 512 | tf_op jit(solution)/shard_map/psum | solution.py:27
  49.1 1.5 convolution_convert_fusion
  50.6 15.1 %all_to_all.29 = bf16[8,24,1792]{2,1,0:T(8,128)(2,1)} all-to-all(bf16[8,24,1792]{2,1,0:T(8,128)(2,1)S(1)} %bitcast.30), channel_id=1, replica_groups=mesh['expert'=8,'tensor'=4] {'expert'}, dimensions={0} | all-to-all | bytes 1376256 | tf_op jit(solution)/shard_map/all_to_all | solution.py:46
  65.6 0.0 all-gather.2.cloned.1.call-update
  65.7 0.7 copy.32
  66.4 3.3 %all-to-all-start.3 = ((bf16[8,1,1]{2,1,0:T(2,128)(2,1)}), bf16[8,1,1]{2,1,0:T(2,128)(2,1)S(1)}, u32[]{:S(2)}, u32[]{:S(2)}) async-start(bf16[8,1,1]{2,1,0:T(2,128)(2,1)} %copy.32), calls=%async_computation.4 | async-start | bytes 8192 | tf_op jit(solution)/shard_map/all_to_all | solution.py:47
  69.7 0.0 copy-done.1
  69.7 0.1 copy.31
  69.8 4.4 %all-to-all-done.3 = bf16[8,1,1]{2,1,0:T(2,128)(2,1)S(1)} async-done(((bf16[8,1,1]{2,1,0:T(2,128)(2,1)}), bf16[8,1,1]{2,1,0:T(2,128)(2,1)S(1)}, u32[]{:S(2)}, u32[]{:S(2)}) %all-to-all-start.3) | async-done | bytes 48 | tf_op jit(solution)/shard_map/all_to_all | solution.py:47
  74.2 0.6 convert_reduce_fusion.1
  74.8 44.4 %all-gather.2.cloned.1.call-done = bf16[192,7168]{1,0:T(8,128)(2,1)} async-done(((bf16[192,1792]{1,0:T(8,128)(2,1)}), bf16[192,7168]{1,0:T(8,128)(2,1)}) %all-gather.2.cloned.1.call-update) | async-done | bytes 2752528 | tf_op jit(solution)/shard_map/all_gather | solution.py:50
  119.2 0.0 copy-start.2
  119.2 5.8 %multiply_reduce_fusion.1 = (f32[192]{0:T(256)S(1)}, f32[192,512]{1,0:T(8,128)S(1)}) fusion(bf16[192,7168]{1,0:T(8,128)(2,1)} %all-gather.2.cloned.1.call-done, bf16[1,7168,512]{2,1,0:T(8,128)(2,1)} %param.14), kind=kOutput, calls=%fused_computation.15 | convolution fusion | flops 1409482496 | bytes 10486528 | tf_op jit(solution)/shard_map/dot_general | solution.py:51
  125.0 0.0 copy-done.2
  125.0 0.0 copy-start
  125.0 4.8 %fusion.11 = f32[192]{0:T(256)S(1)} fusion(f32[192,512]{1,0:T(8,128)S(1)} %get-tuple-element.9, bf16[192,7168]{1,0:T(8,128)(2,1)S(1)} %copy-done.2, bf16[1,7168,512]{2,1,0:T(8,128)(2,1)} %param.15), kind=kOutput, calls=%fused_computation.11 | convolution fusion | flops 1409580800 | bytes 10486528 | tf_op jit(solution)/shard_map/dot_general | solution.py:52
  129.8 0.1 div.34
  129.9 0.1 div.36
  130.0 9.9 %all-reduce = (f32[8,24]{1,0:T(8,128)}, f32[8,24]{1,0:T(8,128)}) all-reduce(f32[8,24]{1,0:T(8,128)S(1)} %div.36, f32[8,24]{1,0:T(8,128)S(1)} %div.34), channel_id=1, replica_groups=mesh['expert'=8,'tensor'=4] {'tensor'}, use_global_device_ids=true, to_apply=%region_9.11 | all-reduce | flops 384 | bytes 3072 | tf_op jit(solution)/shard_map/psum | solution.py:59
  139.9 3.9 %all-to-all-start.1 = ((f32[8,1,24]{2,1,0:T(1,128)}), f32[8,1,24]{2,1,0:T(1,128)S(1)}, u32[]{:S(2)}, u32[]{:S(2)}) async-start(f32[8,1,24]{2,1,0:T(1,128)} %bitcast.7), calls=%async_computation.2 | async-start | bytes 8192 | tf_op jit(solution)/shard_map/all_to_all | solution.py:62
  143.8 0.0 copy-done
  143.8 0.2 fusion.4
  144.0 4.5 %all-to-all-done.1 = f32[8,1,24]{2,1,0:T(1,128)S(1)} async-done(((f32[8,1,24]{2,1,0:T(1,128)}), f32[8,1,24]{2,1,0:T(1,128)S(1)}, u32[]{:S(2)}, u32[]{:S(2)}) %all-to-all-start.1) | async-done | bytes 800 | tf_op jit(solution)/shard_map/all_to_all | solution.py:62
  148.4 3.3 %all-to-all-start.2 = ((f32[8,1,24]{2,1,0:T(1,128)}), f32[8,1,24]{2,1,0:T(1,128)S(1)}, u32[]{:S(2)}, u32[]{:S(2)}) async-start(f32[8,1,24]{2,1,0:T(1,128)} %bitcast.8), calls=%async_computation.3 | async-start | bytes 8192 | tf_op jit(solution)/shard_map/all_to_all | solution.py:63
  151.8 0.7 multiply_divide_fusion
  152.4 0.6 reshape.99
  153.0 1.3 reduce_sum.99
  154.3 1.3 reduce_sum.100
  156.9 0.5 broadcast.46
  157.4 0.7 reduce.10
  158.1 0.1 reshape.96
  158.2 0.0 all-to-all-done.2
  158.2 0.7 reduce.9
  158.9 0.1 reshape.97
  158.9 1.3 gather_fusion
  160.2 1.3 gather_fusion.1
  161.5 0.1 div.38
  161.6 0.6 multiply_reduce_fusion.2
  (7 shorter events, 0.0 us)
Async XLA Ops:
  7.2 62.5 %copy-start.1 = (f32[64,2]{0,1:T(2,128)S(1)}, f32[64,2]{0,1:T(2,128)}, u32[]{:S(2)}) copy-start(f32[64,2]{0,1:T(2,128)} %param.13) | copy-start | bytes 1540
  7.2 31.0 %reduce-scatter.2.cloned.1.call-start = ((), (), s32[]{:S(2)}) async-start(), calls=%async_computation.5 | async-start | bytes 1146880 | tf_op jit(solution)/shard_map/reduce_scatter | solution.py:20
  7.9 111.3 %all-gather.2.cloned.1.call-start = ((), (), s32[]{:S(2)}) async-start(), calls=%async_computation.6 | async-start | bytes 3440640 | tf_op jit(solution)/shard_map/all_gather | solution.py:50
  66.4 7.8 %all-to-all-start.3 = ((bf16[8,1,1]{2,1,0:T(2,128)(2,1)}), bf16[8,1,1]{2,1,0:T(2,128)(2,1)S(1)}, u32[]{:S(2)}, u32[]{:S(2)}) async-start(bf16[8,1,1]{2,1,0:T(2,128)(2,1)} %copy.32), calls=%async_computation.4 | async-start | bytes 8192 | tf_op jit(solution)/shard_map/all_to_all | solution.py:47
  119.2 5.8 %copy-start.2 = (bf16[192,7168]{1,0:T(8,128)(2,1)S(1)}, bf16[192,7168]{1,0:T(8,128)(2,1)}, u32[]{:S(2)}) copy-start(bf16[192,7168]{1,0:T(8,128)(2,1)} %all-gather.2.cloned.1.call-done) | copy-start | bytes 8257540
  125.0 18.8 %copy-start = (bf16[8,24,1792]{2,1,0:T(8,128)(2,1)S(1)}, bf16[8,24,1792]{2,1,0:T(8,128)(2,1)}, u32[]{:S(2)}) copy-start(bf16[8,24,1792]{2,1,0:T(8,128)(2,1)} %all_to_all.29) | copy-start | bytes 2064388
  139.9 8.5 %all-to-all-start.1 = ((f32[8,1,24]{2,1,0:T(1,128)}), f32[8,1,24]{2,1,0:T(1,128)S(1)}, u32[]{:S(2)}, u32[]{:S(2)}) async-start(f32[8,1,24]{2,1,0:T(1,128)} %bitcast.7), calls=%async_computation.2 | async-start | bytes 8192 | tf_op jit(solution)/shard_map/all_to_all | solution.py:62
  148.4 9.7 %all-to-all-start.2 = ((f32[8,1,24]{2,1,0:T(1,128)}), f32[8,1,24]{2,1,0:T(1,128)S(1)}, u32[]{:S(2)}, u32[]{:S(2)}) async-start(f32[8,1,24]{2,1,0:T(1,128)} %bitcast.8), calls=%async_computation.3 | async-start | bytes 8192 | tf_op jit(solution)/shard_map/all_to_all | solution.py:63
Sparse Core Ops, SparseCore 0:
  10.3 27.7 reduce-scatter.1
  65.8 53.3 all-gather.1
where the time goes:
time: 171 us; the launch traced here: 170 us
  waiting for transfers between devices  81.1 us (47%)
  blocking collectives  34.7 us (20%)
  between operations  16.7 us (10%)
  matrix products  12 us (7%)
  starting transfers between devices  10.6 us (6%)
  other arithmetic  9.16 us (5%)
  local copies, waits for them, and re-layouts  6 us (4%)
    all_gather x1, waiting for transfers between devices, per_device(): column_block = lax.all_gather(own_block, 'tensor', axis=1, tiled=True)  44.4 us
    reduce_scatter x1, waiting for transfers between devices, per_device(): lax.psum_scatter(attn_parts[0].astype(jnp.float32).astype(jnp.bfloat16),...  27.1 us
    all_to_all x1, blocking collectives, per_device(): lax.all_to_all(outgoing, 'expert', split_axis=0, concat_axis=0, tiled=True)  15.1 us
    psum x1, blocking collectives, per_device(): err_slots, pow_slots = lax.psum((err_part, pow_part), 'tensor')  9.92 us
    psum x1, blocking collectives, per_device(): squares = lax.psum(jnp.sum(hidden * hidden, axis=1), 'tensor')  9.72 us
    dot_general x1, matrix products, per_device(): jnp.dot(column_block, weight_full, preferred_element_type=jnp.float32)  5.75 us
    dot_general x1, matrix products, per_device(): jnp.dot(column_block, weight_quant, preferred_element_type=jnp.float32)  4.84 us
    all_to_all x1, waiting for transfers between devices, per_device(): lax.all_to_all(err_slots, 'expert', split_axis=0, concat_axis=0, tiled=True)  4.45 us
  transfers between devices with their start and end apart: 5, of which 4 were waited for; matrix products, arithmetic and copies ran while one was open for 6% of the time, Pallas kernels for 0%

commit v1 on v0

--- a/solution.py
+++ b/solution.py
@@ -1,17 +1,20 @@
 import jax
 import jax.numpy as jnp
 from jax import lax
+from jax.experimental import pallas as pl
+from jax.experimental.pallas import tpu as pltpu
 from jax.sharding import PartitionSpec as P
 
 D = 7168
 FF = 2048
 CAP = 24
+EXTRA = 128
 
 
 epsilon = 1e-06
 
 
-def per_device(residual, attn_parts, norm_gain, routes, route_weights, w_gate, w_gate_q):
+def general_device(residual, attn_parts, norm_gain, routes, route_weights, w_gate, w_gate_q):
     n_expert = lax.axis_size("expert")
     tok_count = residual.shape[0]
     local_cols = residual.shape[1]
@@ -38,8 +41,6 @@
     placing = (slot_ids[:, None] == target[None, :]).reshape(n_expert * CAP, tok_count, top_count)
     dispatch = jnp.sum(placing.astype(jnp.int32), axis=2).astype(jnp.bfloat16)
     count_send = load_counts.astype(jnp.bfloat16).reshape(n_expert, 1)
-    weight_full = w_gate[0]
-    weight_quant = w_gate_q[0]
     outgoing = jnp.dot(dispatch, normed, preferred_element_type=jnp.float32).astype(jnp.bfloat16)
     outgoing = outgoing.reshape(n_expert, CAP, local_cols)
     arrived, arrived_counts = (
@@ -48,8 +49,8 @@
     )
     own_block = arrived.reshape(n_expert * CAP, local_cols)
     column_block = lax.all_gather(own_block, "tensor", axis=1, tiled=True)
-    full_acc = jnp.dot(column_block, weight_full, preferred_element_type=jnp.float32)
-    quant_acc = jnp.dot(column_block, weight_quant, preferred_element_type=jnp.float32)
+    full_acc = jnp.dot(column_block, w_gate[0], preferred_element_type=jnp.float32)
+    quant_acc = jnp.dot(column_block, w_gate_q[0], preferred_element_type=jnp.float32)
     block_squares = jnp.einsum("rc,rc->c", own_block, own_block, preferred_element_type=jnp.float32)
     total_load = jnp.sum(arrived_counts.astype(jnp.float32))
     hess_local = 2.0 * block_squares / total_load
@@ -69,6 +70,252 @@
     return (token_error, expert_total.reshape(1), hess_local.reshape(1, local_cols))
 
 
+def product_kernel(first, last, *refs):
+    it = iter(refs)
+    expert_ref = next(it) if last else None
+    near_ref, far_ref, w_ref, wq_ref = next(it), next(it), next(it), next(it)
+    if not first:
+        full_in, quant_in = next(it), next(it)
+    if last:
+        stats_ref, sums = next(it), next(it)
+    else:
+        full_out, quant_out = next(it), next(it)
+    half = near_ref.shape[0]
+    depth = w_ref.shape[0]
+    step = pl.program_id(0)
+    for part, ref in enumerate((near_ref, far_ref)):
+        rows = slice(part * half, (part + 1) * half)
+        x = ref[:, :depth]
+        full = jnp.dot(x, w_ref[...], preferred_element_type=jnp.float32)
+        quant = jnp.dot(x, wq_ref[...], preferred_element_type=jnp.float32)
+        if not first:
+            full = full + full_in[rows, :]
+            quant = quant + quant_in[rows, :]
+        if not last:
+            full_out[rows, :] = full
+            quant_out[rows, :] = quant
+            continue
+        diff = full - quant
+        err = jnp.sum(diff * diff, axis=1, keepdims=True)
+        power = jnp.sum(full * full, axis=1, keepdims=True)
+        lane = lax.broadcasted_iota(jnp.int32, (half, EXTRA), 1)
+        here = jnp.where(lane == 0, err, jnp.where(lane == 1, power, 0.0))
+
+        @pl.when(step == 0)
+        def _():
+            sums[rows, :] = here
+
+        @pl.when(step == pl.num_programs(0) - 1)
+        def _():
+            total = sums[rows, :] + here
+            extra = ref[:, depth:].astype(jnp.float32)
+            squares = extra[:, 0:1] + extra[:, 1:2] + extra[:, 2:3]
+            scale = lax.rsqrt(squares / D + epsilon)
+            scale = scale * scale
+            mine = expert_ref[0].astype(jnp.float32)
+            routed = jnp.sum(
+                jnp.where((lane >= 3) & (extra == mine), 1.0, 0.0), axis=1, keepdims=True
+            )
+            out = jnp.where(
+                lane < 2,
+                total * (scale / FF),
+                jnp.where(lane == 2, routed, jnp.where(lane == 3, scale * routed, 0.0)),
+            )
+            out = jnp.where((lane == 4) | (lane == 5), 0.0, out)
+            stats_ref[:, rows] = out.T[:8, :]
+
+
+def product(near, far, w, wq, number, depth, sums, expert, last):
+    first = sums is None
+    half = near.shape[0]
+    rows = 2 * half
+    cols = w.shape[2]
+    tile = cols // 2
+    whole = lambda j: (0, 0)
+    slab = pl.BlockSpec((None, depth, tile), lambda j: (0, number, j))
+    column = pl.BlockSpec((rows, tile), lambda j: (0, j))
+    args, specs = [], []
+    if last:
+        args.append(expert)
+        specs.append(pl.BlockSpec(memory_space=pltpu.SMEM))
+    args += [near, far, w, wq]
+    specs += [pl.BlockSpec(near.shape, whole), pl.BlockSpec(far.shape, whole), slab, slab]
+    aliases = {}
+    if not first:
+        if not last:
+            aliases = {len(args): 0, len(args) + 1: 1}
+        args += list(sums)
+        specs += [column, column]
+    if last:
+        out_shape = jax.ShapeDtypeStruct((8, rows), jnp.float32)
+        out_specs = pl.BlockSpec((8, rows), whole)
+        scratch = [pltpu.VMEM((rows, EXTRA), jnp.float32)]
+    else:
+        out_shape = [jax.ShapeDtypeStruct((rows, cols), jnp.float32)] * 2
+        out_specs = [column, column]
+        scratch = []
+
+    def kernel(*refs):
+        product_kernel(first, last, *refs)
+
+    return pl.pallas_call(
+        kernel,
+        grid=(2,),
+        in_specs=specs,
+        out_specs=out_specs,
+        out_shape=out_shape,
+        scratch_shapes=scratch,
+        input_output_aliases=aliases,
+        compiler_params=pltpu.CompilerParams(vmem_limit_bytes=32 * 1024 * 1024),
+        cost_estimate=pl.CostEstimate(
+            flops=4 * rows * depth * cols, bytes_accessed=4 * depth * cols + 2 * rows * depth, transcendentals=0
+        ),
+    )(*args)
+
+
+def line_device(residual, attn_parts, norm_gain, routes, route_weights, w_gate, w_gate_q):
+    n_quarters = 4
+    z = lax.axis_index("tensor")
+    e = lax.axis_index("expert")
+    tok = residual.shape[0]
+    width = residual.shape[1]
+    is_end = (z == 0) | (z == 3)
+    low = z == 1
+    own_residual = residual.astype(jnp.float32)
+
+    def partial(k):
+        return attn_parts[0][:, k * width : (k + 1) * width].astype(jnp.float32) + jnp.where(
+            z == k, own_residual, 0.0
+        )
+
+    inward = [(0, 1), (3, 2)]
+    outward = [(1, 0), (2, 3)]
+    both = inward + outward
+    middle = [(1, 2), (2, 1)]
+    swap_x = [(i, i ^ 2) for i in range(8)]
+    swap_y = [(i, i ^ 4) for i in range(8)]
+    swap_core = [(i, i ^ 1) for i in range(8)]
+    forward = [(i, i ^ 2 if i & 1 else i ^ 4) for i in range(8)]
+
+    def gathered(x):
+        from_x = lax.ppermute(x, "expert", swap_x)
+        from_y = lax.ppermute(x, "expert", swap_y)
+        onward = jnp.where(e % 2 == 1, from_y, from_x)
+        diagonal = lax.ppermute(onward, "expert", forward)
+        near = jnp.concatenate([x, from_x, from_y, diagonal], axis=0)
+        return near, lax.ppermute(near, "expert", swap_core)
+
+    finished = [None] * n_quarters
+    sent = [None] * n_quarters
+    outer = [None] * n_quarters
+    inner = [None] * n_quarters
+    gains = None
+    squares = jnp.zeros((tok, 1), jnp.float32)
+    sums = None
+    blocks = []
+    expert = e.reshape(1).astype(jnp.int32)
+    stats = None
+    for step in range(n_quarters + 2):
+        if step < n_quarters:
+            mine = partial(step)
+            going = mine.astype(jnp.bfloat16)
+            if step == 0:
+                gain_row = jnp.concatenate(
+                    [norm_gain[None, :], jnp.zeros((15, width), jnp.bfloat16)], axis=0
+                )
+                going = jnp.concatenate([going, gain_row], axis=0)
+            if step >= 2:
+                going = jnp.where(is_end, going, sent[step - 2])
+            got = lax.ppermute(going, "tensor", both if step >= 2 else inward)
+            outer[step] = got
+            half_sum = (mine + got[:tok].astype(jnp.float32)).astype(jnp.bfloat16)
+            if step == 0:
+                outer_gain = got[tok : tok + 1]
+                half_sum = jnp.concatenate(
+                    [half_sum, norm_gain[None, :], outer_gain, jnp.zeros((14, width), jnp.bfloat16)], axis=0
+                )
+            inner[step] = lax.ppermute(half_sum, "tensor", middle)
+            if step == 0:
+                other = inner[0][tok : tok + 1], inner[0][tok + 1 : tok + 2]
+                own_gain = norm_gain[None, :]
+                gains = (
+                    jnp.where(low, outer_gain, other[1]),
+                    jnp.where(low, own_gain, other[0]),
+                    jnp.where(low, other[0], own_gain),
+                    jnp.where(low, other[1], outer_gain),
+                )
+            hidden = (mine + got[:tok].astype(jnp.float32)) + inner[step][:tok].astype(jnp.float32)
+            squares = squares + jnp.sum(hidden * hidden, axis=1, keepdims=True)
+            ready = (hidden * gains[step].astype(jnp.float32)).astype(jnp.bfloat16)
+            if step == n_quarters - 1:
+                high = lax.reduce_precision(squares, 8, 7)
+                mid = lax.reduce_precision(squares - high, 8, 7)
+                rest = squares - high - mid
+                extra = jnp.concatenate(
+                    [high, mid, rest, routes.astype(jnp.float32)]
+                    + [jnp.full((tok, EXTRA - 3 - routes.shape[1]), -1.0, jnp.float32)],
+                    axis=1,
+                ).astype(jnp.bfloat16)
+                ready = jnp.concatenate([ready, extra], axis=1)
+            sent[step] = ready
+        else:
+            outer_done = lax.ppermute(sent[step - 2], "tensor", outward)
+            outer.append(outer_done)
+        if step >= 2:
+            k = step - 2
+            rows = jnp.where(is_end, outer[step], sent[k])
+            near, far = gathered(rows)
+            blocks.append((near, far))
+            last = k == n_quarters - 1
+            result = product(near, far, w_gate, w_gate_q, k, width, sums, expert, last)
+            if last:
+                stats = result
+            else:
+                sums = result
+
+    ordered = jnp.transpose(stats.reshape(8, 2, 4, tok), (0, 2, 1, 3)).reshape(8, 8, tok)
+    routed = stats[2]
+    weight = stats[3]
+    for bit in range(3):
+        flipped = jnp.flip(ordered.reshape(8, 8 >> (bit + 1), 2, 1 << bit, tok), axis=2).reshape(8, 8, tok)
+        ordered = jnp.where((e >> bit) & 1 == 1, flipped, ordered)
+    expert_sums = jnp.sum(stats[:2] * routed[None, :], axis=1)
+    payload = jnp.concatenate(
+        [
+            ordered[0],
+            ordered[1],
+            jnp.broadcast_to(expert_sums[None, :], (8, 2)),
+            jnp.zeros((8, 126), jnp.float32),
+        ],
+        axis=1,
+    )
+    payload = jnp.broadcast_to(payload[:, None, :], (8, 4, 256)).reshape(32, 256)
+    back = lax.all_to_all(payload, ("expert", "tensor"), split_axis=0, concat_axis=0, tiled=True)
+
+    def hess_of(k):
+        def run():
+            near, far = blocks[k]
+            half = near.shape[0]
+            wide = [part[:, :width].astype(jnp.float32) for part in (near, far)]
+            return jnp.sum(wide[0] * wide[0] * weight[:half, None], axis=0) + jnp.sum(
+                wide[1] * wide[1] * weight[half:, None], axis=0
+            )
+
+        return run
+
+    hess = 2.0 * lax.switch(z, [hess_of(k) for k in range(n_quarters)]) / jnp.sum(routed)
+    back = jnp.sum(back.reshape(8, 4, 256), axis=1)
+    err, power = back[:, :tok], back[:, tok : 2 * tok]
+    ids = jnp.arange(8, dtype=jnp.int32)
+    chosen = (routes[:, :, None] == ids[None, None, :]).astype(jnp.float32)
+    token_err = jnp.sum(chosen * err.T[:, None, :], axis=2)
+    token_pow = jnp.sum(chosen * power.T[:, None, :], axis=2)
+    token_error = jnp.sum(route_weights * token_err / (token_pow + epsilon), axis=1)
+    own = jnp.sum(jnp.where((ids == e)[:, None], back[:, 2 * tok : 2 * tok + 2], 0.0), axis=0)
+    expert_total = own[0] / (own[1] + epsilon)
+    return (token_error, expert_total.reshape(1), hess.reshape(1, width))
+
+
 def solution(mesh):
     placed = (
         P("expert", "tensor"),
@@ -79,8 +326,9 @@
         P("expert", None, "tensor"),
         P("expert", None, "tensor"),
     )
+    on_line = mesh.shape["expert"] == 8 and mesh.shape["tensor"] == 4
     return jax.shard_map(
-        per_device,
+        line_device if on_line else general_device,
         mesh=mesh,
         in_specs=placed,
         out_specs=(P("expert"), P("expert"), P("expert", "tensor")),

time: 171 us -> 141 us (0.82)
  starting transfers between devices: 10.6 us -> 51.7 us
  blocking collectives: 34.7 us -> 0 us
  waiting for transfers between devices: 81.1 us -> 46.9 us
  Pallas kernels: 0 us -> 16.5 us
  between operations: 16.7 us -> 3.62 us
  matrix products: 12 us -> 0 us
  local copies, waits for them, and re-layouts: 6 us -> 9.83 us
  other arithmetic: 9.16 us -> 11.3 us
    all_gather x1 -> x0, waiting for transfers between devices: 44.4 us -> none  [per_device(): column_block = lax.all_gather(own_block, 'tensor', axis=1, tiled=True)]
    ppermute x0 -> x26, starting transfers between devices: none -> 43.6 us  [the longest x4 21.9 us: line_device(): got = lax.ppermute(going, 'tensor', both if step >= 2 else inward)]
    ppermute x0 -> x26, waiting for transfers between devices: none -> 42.6 us  [the longest x4 15.6 us: line_device(): got = lax.ppermute(going, 'tensor', both if step >= 2 else inward)]
    reduce_scatter x1 -> x0, waiting for transfers between devices: 27.1 us -> none  [per_device(): lax.psum_scatter(attn_parts[0].astype(jnp.float32).astype(jnp.bfloat16),...]
    psum x2 -> x0, blocking collectives: 19.6 us -> none  [the longest x1 9.92 us: per_device(): err_slots, pow_slots = lax.psum((err_part, pow_part), 'tensor')]
    pallas_call x0 -> x4, Pallas kernels: none -> 16.5 us  [product(): pl.pallas_call(kernel, grid=(2,), in_specs=specs, out_specs=out_specs, ou...]
    all_to_all x1 -> x0, blocking collectives: 15.1 us -> none  [per_device(): lax.all_to_all(outgoing, 'expert', split_axis=0, concat_axis=0, tiled=True)]
    dot_general x3 -> x0, matrix products: 12 us -> none  [the longest x1 5.75 us: per_device(): jnp.dot(column_block, weight_full, preferred_element_type=jnp.float32)]
  transfers between devices with their start and end apart: 5 -> 27, of which waited for: 4 -> 14; matrix products, arithmetic and copies ran while one was open for 6% -> 6% of each run, Pallas kernels for 0% -> 8%
where the time goes in v1:
time: 141 us; the launch traced here: 140 us
  starting transfers between devices  51.7 us (37%)
  waiting for transfers between devices  46.9 us (33%)
  Pallas kernels  16.5 us (12%)
  other arithmetic  11.3 us (8%)
  local copies, waits for them, and re-layouts  9.83 us (7%)
  between operations  3.62 us (3%)
    ppermute x4, starting transfers between devices, line_device(): got = lax.ppermute(going, 'tensor', both if step >= 2 else inward)  21.9 us
    pallas_call x4, Pallas kernels, product(): pl.pallas_call(kernel, grid=(2,), in_specs=specs, out_specs=out_specs, ou...  16.5 us
    ppermute x4, waiting for transfers between devices, line_device(): got = lax.ppermute(going, 'tensor', both if step >= 2 else inward)  15.6 us
    ppermute x2, waiting for transfers between devices, line_device(): outer_done = lax.ppermute(sent[step - 2], 'tensor', outward)  11.8 us
    all_to_all x1, starting transfers between devices, line_device(): lax.all_to_all(payload, ('expert', 'tensor'), split_axis=0, concat_axis=0...  8.07 us
    ppermute x4, waiting for transfers between devices, gathered(): from_x = lax.ppermute(x, 'expert', swap_x)  7.09 us
    ppermute x4, starting transfers between devices, gathered(): diagonal = lax.ppermute(onward, 'expert', forward)  6.72 us
    ppermute x4, starting transfers between devices, gathered(): from_x = lax.ppermute(x, 'expert', swap_x)  6.22 us
  transfers between devices with their start and end apart: 27, of which 14 were waited for; matrix products, arithmetic and copies ran while one was open for 6% of the time, Pallas kernels for 8%

profile of v1, /device:TPU:0, one launch (start us, length us, event | category | flops | bytes accessed | tf_op | source)
XLA Modules:
  0.0 139.9 jit_solution(1357755996285877075)
XLA Ops:
  0.7 0.8 broadcast_in_dim.38
  1.5 1.3 fusion.6
  2.8 0.1 fusion.8
  2.9 4.9 %collective-permute-start.2 = (bf16[80,1792]{1,0:T(8,128)(2,1)S(1)}, bf16[80,1792]{1,0:T(8,128)(2,1)S(1)}, u32[]{:S(2)}, u32[]{:S(2)}) collective-permute-start(bf16[80,1792]{1,0:T(8,128)(2,1)S(1)} %fusion.8), channel_id=1, source_target_pairs={{0,1},{3,2},{4,5},{7,6},{8,9},{11,10},{12,13},{15,14},{16,17},{19,... | collective-permute-start | bytes 860168 | tf_op jit(solution)/shard_map/ppermute | solution.py:229
  7.9 1.3 collective-permute-start
  9.3 5.8 %collective-permute-done.2 = bf16[80,1792]{1,0:T(8,128)(2,1)S(1)} collective-permute-done((bf16[80,1792]{1,0:T(8,128)(2,1)S(1)}, bf16[80,1792]{1,0:T(8,128)(2,1)S(1)}, u32[]{:S(2)}, u32[]{:S(2)}) %collective-permute-start.2) | collective-permute-done | bytes 286752 | tf_op jit(solution)/shard_map/ppermute | solution.py:229
  15.1 3.8 %collective-permute-done = bf16[64,1792]{1,0:T(8,128)(2,1)S(1)} collective-permute-done((bf16[64,1792]{1,0:T(8,128)(2,1)S(1)}, bf16[64,1792]{1,0:T(8,128)(2,1)S(1)}, u32[]{:S(2)}, u32[]{:S(2)}) %collective-permute-start) | collective-permute-done | bytes 229408 | tf_op jit(solution)/shard_map/ppermute | solution.py:229
  18.9 0.2 fusion.15
  19.1 0.1 fusion.10
  19.2 0.7 collective-permute-start.3
  19.9 0.7 collective-permute-start.1
  20.7 0.4 fusion.12
  21.1 15.5 %collective-permute-start.6 = (bf16[64,1792]{1,0:T(8,128)(2,1)S(1)}, bf16[64,1792]{1,0:T(8,128)(2,1)S(1)}, u32[]{:S(2)}, u32[]{:S(2)}) collective-permute-start(bf16[64,1792]{1,0:T(8,128)(2,1)S(1)} %get-tuple-element.107), channel_id=1, source_target_pairs={{0,1},{3,2},{1,0},{2,3},{4,5},{7,6},{5,4},{6,7},{8,9},{11,10},{9,8... | collective-permute-start | bytes 688136 | tf_op jit(solution)/shard_map/ppermute | solution.py:229
  36.7 0.1 copy.42
  36.9 6.0 %collective-permute-done.6 = bf16[64,1792]{1,0:T(8,128)(2,1)S(1)} collective-permute-done((bf16[64,1792]{1,0:T(8,128)(2,1)S(1)}, bf16[64,1792]{1,0:T(8,128)(2,1)S(1)}, u32[]{:S(2)}, u32[]{:S(2)}) %collective-permute-start.6) | collective-permute-done | bytes 229408 | tf_op jit(solution)/shard_map/ppermute | solution.py:229
  43.0 1.6 %collective-permute-start.22 = (bf16[64,1792]{1,0:T(8,128)(2,1)S(1)}, bf16[64,1792]{1,0:T(8,128)(2,1)S(1)}, u32[]{:S(2)}, u32[]{:S(2)}) collective-permute-start(bf16[64,1792]{1,0:T(8,128)(2,1)S(1)} %broadcast_select_fusion.5), channel_id=1, source_target_pairs={{0,8},{4,12},{8,0},{12,4},{16,24},{20,28},{24,16},{28,20},{1,9},{5... | collective-permute-start | bytes 688136 | tf_op jit(solution)/shard_map/ppermute | solution.py:201
  44.5 1.5 %collective-permute-start.23 = (bf16[64,1792]{1,0:T(8,128)(2,1)S(1)}, bf16[64,1792]{1,0:T(8,128)(2,1)S(1)}, u32[]{:S(2)}, u32[]{:S(2)}) collective-permute-start(bf16[64,1792]{1,0:T(8,128)(2,1)S(1)} %broadcast_select_fusion.5), channel_id=1, source_target_pairs={{0,16},{4,20},{8,24},{12,28},{16,0},{20,4},{24,8},{28,12},{1,17},{... | collective-permute-start | bytes 688136 | tf_op jit(solution)/shard_map/ppermute | solution.py:202
  46.1 0.9 collective-permute-start.18
  47.0 1.5 %collective-permute-start.19 = (bf16[64,1792]{1,0:T(8,128)(2,1)S(1)}, bf16[64,1792]{1,0:T(8,128)(2,1)S(1)}, u32[]{:S(2)}, u32[]{:S(2)}) collective-permute-start(bf16[64,1792]{1,0:T(8,128)(2,1)S(1)} %broadcast_select_fusion.6), channel_id=1, source_target_pairs={{0,16},{4,20},{8,24},{12,28},{16,0},{20,4},{24,8},{28,12},{1,17},{... | collective-permute-start | bytes 688136 | tf_op jit(solution)/shard_map/ppermute | solution.py:202
  48.5 0.1 fusion.16
  48.6 0.7 collective-permute-start.5
  49.3 2.2 %collective-permute-done.22 = bf16[64,1792]{1,0:T(8,128)(2,1)S(1)} collective-permute-done((bf16[64,1792]{1,0:T(8,128)(2,1)S(1)}, bf16[64,1792]{1,0:T(8,128)(2,1)S(1)}, u32[]{:S(2)}, u32[]{:S(2)}) %collective-permute-start.22) | collective-permute-done | bytes 229408 | tf_op jit(solution)/shard_map/ppermute | solution.py:201
  51.6 1.6 %collective-permute-start.24 = (bf16[64,1792]{1,0:T(8,128)(2,1)S(1)}, bf16[64,1792]{1,0:T(8,128)(2,1)S(1)}, u32[]{:S(2)}, u32[]{:S(2)}) collective-permute-start(bf16[64,1792]{1,0:T(8,128)(2,1)S(1)} %broadcast_select_fusion.2), channel_id=1, source_target_pairs={{0,16},{4,12},{8,24},{12,4},{16,0},{20,28},{24,8},{28,20},{1,17},{... | collective-permute-start | bytes 688136 | tf_op jit(solution)/shard_map/ppermute | solution.py:204
  53.2 3.2 %collective-permute-done.18 = bf16[64,1792]{1,0:T(8,128)(2,1)S(1)} collective-permute-done((bf16[64,1792]{1,0:T(8,128)(2,1)S(1)}, bf16[64,1792]{1,0:T(8,128)(2,1)S(1)}, u32[]{:S(2)}, u32[]{:S(2)}) %collective-permute-start.18) | collective-permute-done | bytes 229408 | tf_op jit(solution)/shard_map/ppermute | solution.py:201
  56.5 0.8 broadcast_select_fusion.3
  57.2 1.5 %collective-permute-start.20 = (bf16[64,1792]{1,0:T(8,128)(2,1)}, bf16[64,1792]{1,0:T(8,128)(2,1)}, u32[]{:S(2)}, u32[]{:S(2)}) collective-permute-start(bf16[64,1792]{1,0:T(8,128)(2,1)} %broadcast_select_fusion.3), channel_id=1, source_target_pairs={{0,16},{4,12},{8,24},{12,4},{16,0},{20,28},{24,8},{28,20},{1,17},{... | collective-permute-start | bytes 688136 | tf_op jit(solution)/shard_map/ppermute | solution.py:204
  58.8 0.9 fusion.17
  59.7 0.7 collective-permute-start.7
  60.6 0.7 multiply_reduce_fusion.4
  61.3 1.4 %collective-permute-start.13 = (bf16[64,1792]{1,0:T(8,128)(2,1)S(1)}, bf16[64,1792]{1,0:T(8,128)(2,1)S(1)}, u32[]{:S(2)}, u32[]{:S(2)}) collective-permute-start(bf16[64,1792]{1,0:T(8,128)(2,1)S(1)} %get-tuple-element.111), channel_id=1, source_target_pairs={{1,0},{2,3},{5,4},{6,7},{9,8},{10,11},{13,12},{14,15},{17,16},{18,... | collective-permute-start | bytes 688136 | tf_op jit(solution)/shard_map/ppermute | solution.py:262
  62.7 0.1 copy.39
  62.8 0.8 collective-permute-done.20
  63.6 1.2 pad_maximum_fusion.2.refs_0_
  64.9 0.1 copy.40
  65.0 0.1 copy.41
  65.1 0.1 concatenate.29
  65.2 1.3 collective-permute-start.8
  66.5 8.1 %collective-permute-done.13 = bf16[64,1792]{1,0:T(8,128)(2,1)S(1)} collective-permute-done((bf16[64,1792]{1,0:T(8,128)(2,1)S(1)}, bf16[64,1792]{1,0:T(8,128)(2,1)S(1)}, u32[]{:S(2)}, u32[]{:S(2)}) %collective-permute-start.13) | collective-permute-done | bytes 229408 | tf_op jit(solution)/shard_map/ppermute | solution.py:262
  74.7 1.9 %collective-permute-start.14 = (bf16[64,1792]{1,0:T(8,128)(2,1)S(1)}, bf16[64,1792]{1,0:T(8,128)(2,1)S(1)}, u32[]{:S(2)}, u32[]{:S(2)}) collective-permute-start(bf16[64,1792]{1,0:T(8,128)(2,1)S(1)} %broadcast_select_fusion.7), channel_id=1, source_target_pairs={{0,8},{4,12},{8,0},{12,4},{16,24},{20,28},{24,16},{28,20},{1,9},{5... | collective-permute-start | bytes 688136 | tf_op jit(solution)/shard_map/ppermute | solution.py:201
  76.7 3.7 %collective-permute-done.8 = bf16[64,1920]{1,0:T(8,128)(2,1)S(1)} collective-permute-done((bf16[64,1920]{1,0:T(8,128)(2,1)S(1)}, bf16[64,1920]{1,0:T(8,128)(2,1)S(1)}, u32[]{:S(2)}, u32[]{:S(2)}) %collective-permute-start.8) | collective-permute-done | bytes 245792 | tf_op jit(solution)/shard_map/ppermute | solution.py:262
  80.5 0.3 collective-permute-done.14
  80.8 1.9 %collective-permute-start.9 = (bf16[64,1920]{1,0:T(8,128)(2,1)S(1)}, bf16[64,1920]{1,0:T(8,128)(2,1)S(1)}, u32[]{:S(2)}, u32[]{:S(2)}) collective-permute-start(bf16[64,1920]{1,0:T(8,128)(2,1)S(1)} %broadcast_select_fusion.1), channel_id=1, source_target_pairs={{0,8},{4,12},{8,0},{12,4},{16,24},{20,28},{24,16},{28,20},{1,9},{5... | collective-permute-start | bytes 737288 | tf_op jit(solution)/shard_map/ppermute | solution.py:201
  82.7 1.8 %collective-permute-start.16 = (bf16[64,1792]{1,0:T(8,128)(2,1)S(1)}, bf16[64,1792]{1,0:T(8,128)(2,1)S(1)}, u32[]{:S(2)}, u32[]{:S(2)}) collective-permute-start(bf16[64,1792]{1,0:T(8,128)(2,1)S(1)} %broadcast_select_fusion.4), channel_id=1, source_target_pairs={{0,16},{4,12},{8,24},{12,4},{16,0},{20,28},{24,8},{28,20},{1,17},{... | collective-permute-start | bytes 688136 | tf_op jit(solution)/shard_map/ppermute | solution.py:204
  84.5 3.8 %collective-permute-done.10 = bf16[64,1920]{1,0:T(8,128)(2,1)S(1)} collective-permute-done((bf16[64,1920]{1,0:T(8,128)(2,1)S(1)}, bf16[64,1920]{1,0:T(8,128)(2,1)S(1)}, u32[]{:S(2)}, u32[]{:S(2)}) %collective-permute-start.10) | collective-permute-done | bytes 245792 | tf_op jit(solution)/shard_map/ppermute | solution.py:202
  88.3 1.4 collective-permute-done.9
  89.7 1.8 %collective-permute-start.11 = (bf16[64,1920]{1,0:T(8,128)(2,1)S(1)}, bf16[64,1920]{1,0:T(8,128)(2,1)S(1)}, u32[]{:S(2)}, u32[]{:S(2)}) collective-permute-start(bf16[64,1920]{1,0:T(8,128)(2,1)S(1)} %broadcast_select_fusion), channel_id=1, source_target_pairs={{0,16},{4,12},{8,24},{12,4},{16,0},{20,28},{24,8},{28,20},{1,17},{... | collective-permute-start | bytes 737288 | tf_op jit(solution)/shard_map/ppermute | solution.py:204
  91.5 1.0 pad_maximum_fusion.1.refs_0_
  92.5 3.4 %collective-permute-done.11 = bf16[64,1920]{1,0:T(8,128)(2,1)S(1)} collective-permute-done((bf16[64,1920]{1,0:T(8,128)(2,1)S(1)}, bf16[64,1920]{1,0:T(8,128)(2,1)S(1)}, u32[]{:S(2)}, u32[]{:S(2)}) %collective-permute-start.11) | collective-permute-done | bytes 245792 | tf_op jit(solution)/shard_map/ppermute | solution.py:204
  96.2 3.1 %copy-done = bf16[1,7168,512]{2,1,0:T(8,128)(2,1)S(1)} copy-done((bf16[1,7168,512]{2,1,0:T(8,128)(2,1)S(1)}, bf16[1,7168,512]{2,1,0:T(8,128)(2,1)}, u32[]{:S(2)}) %copy-start) | copy-done | bytes 7340056
  99.3 3.1 %copy-done.1 = bf16[1,7168,512]{2,1,0:T(8,128)(2,1)S(1)} copy-done((bf16[1,7168,512]{2,1,0:T(8,128)(2,1)S(1)}, bf16[1,7168,512]{2,1,0:T(8,128)(2,1)}, u32[]{:S(2)}) %copy-start.1) | copy-done | bytes 7340056
  102.4 3.7 %shard_map.94 = (f32[512,512]{1,0:T(8,128)S(1)}, f32[512,512]{1,0:T(8,128)S(1)}) custom-call(bf16[256,1792]{1,0:T(8,128)(2,1)S(1)} %pad_maximum_fusion.3.refs_0_, bf16[256,1792]{1,0:T(8,128)(2,1)} %collective-permute-done.25.refs_1_, bf16[1,7168,512]{2,1,0:T(8,128)(2,1)S(1)} %copy-done, bf16[1,7168,512]{2,1,0:T(8,128)(2,1)S(1)} %copy-done.1), custom_call_target="tpu_custom_call" | custom-call | flops 1879048192 | bytes 5505024 | tf_op jit(solution)/shard_map/pallas_call | solution.py:161
  106.1 3.8 %shard_map.95 = (f32[512,512]{1,0:T(8,128)S(1)}, f32[512,512]{1,0:T(8,128)S(1)}) custom-call(bf16[256,1792]{1,0:T(8,128)(2,1)S(1)} %pad_maximum_fusion.2.refs_0_, bf16[256,1792]{1,0:T(8,128)(2,1)} %collective-permute-done.21.refs_1_, bf16[1,7168,512]{2,1,0:T(8,128)(2,1)S(1)} %copy-done, ...), custom_call_target="tpu_custom_call", output_to_operand_aliasing={{0}: (4, {}), {1}: (5, {})} | custom-call | flops 1879048192 | bytes 5505024 | tf_op jit(solution)/shard_map/pallas_call | solution.py:161
  109.9 4.1 %shard_map.96 = (f32[512,512]{1,0:T(8,128)S(1)}, f32[512,512]{1,0:T(8,128)S(1)}) custom-call(bf16[256,1792]{1,0:T(8,128)(2,1)} %pad_maximum_fusion.1.refs_0_, bf16[256,1792]{1,0:T(8,128)(2,1)} %collective-permute-done.17.refs_1_, bf16[1,7168,512]{2,1,0:T(8,128)(2,1)S(1)} %copy-done, ...), custom_call_target="tpu_custom_call", output_to_operand_aliasing={{0}: (4, {}), {1}: (5, {})} | custom-call | flops 1879048192 | bytes 5505024 | tf_op jit(solution)/shard_map/pallas_call | solution.py:161
  114.0 4.9 %shard_map.97 = f32[8,512]{1,0:T(8,128)S(1)} custom-call(s32[1]{0:T(128)} %bitcast.refs_0_, bf16[256,1920]{1,0:T(8,128)(2,1)S(1)} %pad_maximum_fusion.refs_1_, bf16[256,1920]{1,0:T(8,128)(2,1)} %collective-permute-done.12.refs_2_, bf16[1,7168,512]{2,1,0:T(8,128)(2,1)S(1)} %copy-done, bf16[1,7168,512]{2,1,0:T(8,128)(2,1)S(1)} %copy-done.1, ...), custom_call_target="tpu_custom_call" | custom-call | flops 1879048192 | bytes 5505024 | tf_op jit(solution)/shard_map/pallas_call | solution.py:161
  118.9 0.6 slice_reduce_fusion
  119.7 0.1 fusion.27
  120.0 0.7 all_to_all.6
  120.7 8.1 %all-to-all-start = ((f32[32,1,256]{2,1,0:T(1,128)}), f32[32,1,256]{2,1,0:T(1,128)S(1)}, u32[]{:S(2)}, u32[]{:S(2)}) async-start(f32[32,1,256]{2,1,0:T(1,128)} %all_to_all.6), calls=%async_computation | async-start | bytes 65536 | tf_op jit(solution)/shard_map/all_to_all | solution.py:293
  128.7 1.7 %multiply_reduce_fusion = (f32[1792]{0:T(1024)S(1)}, f32[1792]{0:T(1024)S(1)}) fusion(f32[]{:T(128)} %get-tuple-element.91, bf16[256,1792]{1,0:T(8,128)(2,1)} %get-tuple-element.92, f32[256]{0:T(256)S(1)} %get-tuple-element.129, f32[256]{0:T(256)S(1)} %get-tuple-element.130, bf16[256,1792]{1,0:T(8,128)(2,1)S(1)} %get-tuple-element.89), kind=kLoop, calls=%fused_computation | loop fusion | flops 3666432 | bytes 1851396 | tf_op jit(solution)/shard_map/cond/branch_0_fun/reduce_sum | solution.py:300
  130.4 0.7 multiply_divide_fusion
  131.1 0.6 div.25
  131.7 4.3 %all-to-all-done = f32[32,1,256]{2,1,0:T(1,128)S(1)} async-done(((f32[32,1,256]{2,1,0:T(1,128)}), f32[32,1,256]{2,1,0:T(1,128)S(1)}, u32[]{:S(2)}, u32[]{:S(2)}) %all-to-all-start) | async-done | bytes 32800 | tf_op jit(solution)/shard_map/all_to_all | solution.py:293
  136.3 0.6 fusion.33
  138.2 0.5 fusion.28
  (85 shorter events, 1.9 us)
Async XLA Ops:
  0.6 18.2 %copy-start.2 = (bf16[1,64,7168]{2,1,0:T(8,128)(2,1)S(1)}, bf16[1,64,7168]{2,1,0:T(8,128)(2,1)}, u32[]{:S(2)}) copy-start(bf16[1,64,7168]{2,1,0:T(8,128)(2,1)} %param.12) | copy-start | bytes 2752516
  0.6 18.2 %copy-start.3 = (bf16[64,1792]{1,0:T(8,128)(2,1)S(1)}, bf16[64,1792]{1,0:T(8,128)(2,1)}, u32[]{:S(2)}) copy-start(bf16[64,1792]{1,0:T(8,128)(2,1)} %param.11) | copy-start | bytes 688132
  1.5 19.1 %copy-start.9 = (bf16[1792]{0:T(1024)(128)(2,1)S(1)}, bf16[1792]{0:T(1024)(128)(2,1)}, u32[]{:S(2)}) copy-start(bf16[1792]{0:T(1024)(128)(2,1)} %param.13) | copy-start | bytes 10756
  2.9 12.2 %collective-permute-start.2 = (bf16[80,1792]{1,0:T(8,128)(2,1)S(1)}, bf16[80,1792]{1,0:T(8,128)(2,1)S(1)}, u32[]{:S(2)}, u32[]{:S(2)}) collective-permute-start(bf16[80,1792]{1,0:T(8,128)(2,1)S(1)} %fusion.8), channel_id=1, source_target_pairs={{0,1},{3,2},{4,5},{7,6},{8,9},{11,10},{12,13},{15,14},{16,17},{19,... | collective-permute-start | bytes 860168 | tf_op jit(solution)/shard_map/ppermute | solution.py:229
  7.9 11.0 %collective-permute-start = (bf16[64,1792]{1,0:T(8,128)(2,1)S(1)}, bf16[64,1792]{1,0:T(8,128)(2,1)S(1)}, u32[]{:S(2)}, u32[]{:S(2)}) collective-permute-start(bf16[64,1792]{1,0:T(8,128)(2,1)S(1)} %get-tuple-element.118), channel_id=1, source_target_pairs={{0,1},{3,2},{4,5},{7,6},{8,9},{11,10},{12,13},{15,14},{16,17},{19,... | collective-permute-start | bytes 688136 | tf_op jit(solution)/shard_map/ppermute | solution.py:229
  19.1 17.6 %copy-start.11 = (s32[64,2]{0,1:T(2,128)S(1)}, s32[64,2]{0,1:T(2,128)}, u32[]{:S(2)}) copy-start(s32[64,2]{0,1:T(2,128)} %param.14) | copy-start | bytes 1540
  19.2 1.4 collective-permute-start.3
  19.9 0.8 collective-permute-start.1
  20.6 22.4 %copy-start.7 = (bf16[80,1792]{1,0:T(8,128)(2,1)}, bf16[80,1792]{1,0:T(8,128)(2,1)S(1)}, u32[]{:S(2)}) copy-start(bf16[80,1792]{1,0:T(8,128)(2,1)S(1)} %collective-permute-done.3) | copy-start | bytes 860164
  21.1 21.8 %collective-permute-start.6 = (bf16[64,1792]{1,0:T(8,128)(2,1)S(1)}, bf16[64,1792]{1,0:T(8,128)(2,1)S(1)}, u32[]{:S(2)}, u32[]{:S(2)}) collective-permute-start(bf16[64,1792]{1,0:T(8,128)(2,1)S(1)} %get-tuple-element.107), channel_id=1, source_target_pairs={{0,1},{3,2},{1,0},{2,3},{4,5},{7,6},{5,4},{6,7},{8,9},{11,10},{9,8... | collective-permute-start | bytes 688136 | tf_op jit(solution)/shard_map/ppermute | solution.py:229
  36.8 9.3 %collective-permute-start.4 = (bf16[64,1792]{1,0:T(8,128)(2,1)S(1)}, bf16[64,1792]{1,0:T(8,128)(2,1)S(1)}, u32[]{:S(2)}, u32[]{:S(2)}) collective-permute-start(bf16[64,1792]{1,0:T(8,128)(2,1)S(1)} %get-tuple-element.114), channel_id=1, source_target_pairs={{0,1},{3,2},{1,0},{2,3},{4,5},{7,6},{5,4},{6,7},{8,9},{11,10},{9,8... | collective-permute-start | bytes 688136 | tf_op jit(solution)/shard_map/ppermute | solution.py:229
  43.0 8.6 %collective-permute-start.22 = (bf16[64,1792]{1,0:T(8,128)(2,1)S(1)}, bf16[64,1792]{1,0:T(8,128)(2,1)S(1)}, u32[]{:S(2)}, u32[]{:S(2)}) collective-permute-start(bf16[64,1792]{1,0:T(8,128)(2,1)S(1)} %broadcast_select_fusion.5), channel_id=1, source_target_pairs={{0,8},{4,12},{8,0},{12,4},{16,24},{20,28},{24,16},{28,20},{1,9},{5... | collective-permute-start | bytes 688136 | tf_op jit(solution)/shard_map/ppermute | solution.py:201
  44.5 7.1 %collective-permute-start.23 = (bf16[64,1792]{1,0:T(8,128)(2,1)S(1)}, bf16[64,1792]{1,0:T(8,128)(2,1)S(1)}, u32[]{:S(2)}, u32[]{:S(2)}) collective-permute-start(bf16[64,1792]{1,0:T(8,128)(2,1)S(1)} %broadcast_select_fusion.5), channel_id=1, source_target_pairs={{0,16},{4,20},{8,24},{12,28},{16,0},{20,4},{24,8},{28,12},{1,17},{... | collective-permute-start | bytes 688136 | tf_op jit(solution)/shard_map/ppermute | solution.py:202
  46.1 10.4 %collective-permute-start.18 = (bf16[64,1792]{1,0:T(8,128)(2,1)S(1)}, bf16[64,1792]{1,0:T(8,128)(2,1)S(1)}, u32[]{:S(2)}, u32[]{:S(2)}) collective-permute-start(bf16[64,1792]{1,0:T(8,128)(2,1)S(1)} %broadcast_select_fusion.6), channel_id=1, source_target_pairs={{0,8},{4,12},{8,0},{12,4},{16,24},{20,28},{24,16},{28,20},{1,9},{5... | collective-permute-start | bytes 688136 | tf_op jit(solution)/shard_map/ppermute | solution.py:201
  47.0 9.5 %collective-permute-start.19 = (bf16[64,1792]{1,0:T(8,128)(2,1)S(1)}, bf16[64,1792]{1,0:T(8,128)(2,1)S(1)}, u32[]{:S(2)}, u32[]{:S(2)}) collective-permute-start(bf16[64,1792]{1,0:T(8,128)(2,1)S(1)} %broadcast_select_fusion.6), channel_id=1, source_target_pairs={{0,16},{4,20},{8,24},{12,28},{16,0},{20,4},{24,8},{28,12},{1,17},{... | collective-permute-start | bytes 688136 | tf_op jit(solution)/shard_map/ppermute | solution.py:202
  48.6 10.1 %collective-permute-start.5 = (bf16[64,1792]{1,0:T(8,128)(2,1)S(1)}, bf16[64,1792]{1,0:T(8,128)(2,1)S(1)}, u32[]{:S(2)}, u32[]{:S(2)}) collective-permute-start(bf16[64,1792]{1,0:T(8,128)(2,1)S(1)} %fusion.16), channel_id=1, source_target_pairs={{1,2},{2,1},{5,6},{6,5},{9,10},{10,9},{13,14},{14,13},{17,18},{18,... | collective-permute-start | bytes 688136 | tf_op jit(solution)/shard_map/ppermute | solution.py:237
  51.6 8.7 %collective-permute-start.24 = (bf16[64,1792]{1,0:T(8,128)(2,1)S(1)}, bf16[64,1792]{1,0:T(8,128)(2,1)S(1)}, u32[]{:S(2)}, u32[]{:S(2)}) collective-permute-start(bf16[64,1792]{1,0:T(8,128)(2,1)S(1)} %broadcast_select_fusion.2), channel_id=1, source_target_pairs={{0,16},{4,12},{8,24},{12,4},{16,0},{20,28},{24,8},{28,20},{1,17},{... | collective-permute-start | bytes 688136 | tf_op jit(solution)/shard_map/ppermute | solution.py:204
  56.4 3.9 %copy-start.4 = (bf16[64,1792]{1,0:T(8,128)(2,1)}, bf16[64,1792]{1,0:T(8,128)(2,1)S(1)}, u32[]{:S(2)}) copy-start(bf16[64,1792]{1,0:T(8,128)(2,1)S(1)} %collective-permute-done.18) | copy-start | bytes 688132
  56.4 3.9 %copy-start.5 = (bf16[64,1792]{1,0:T(8,128)(2,1)}, bf16[64,1792]{1,0:T(8,128)(2,1)S(1)}, u32[]{:S(2)}) copy-start(bf16[64,1792]{1,0:T(8,128)(2,1)S(1)} %collective-permute-done.19) | copy-start | bytes 688132
  57.2 6.3 %collective-permute-start.20 = (bf16[64,1792]{1,0:T(8,128)(2,1)}, bf16[64,1792]{1,0:T(8,128)(2,1)}, u32[]{:S(2)}, u32[]{:S(2)}) collective-permute-start(bf16[64,1792]{1,0:T(8,128)(2,1)} %broadcast_select_fusion.3), channel_id=1, source_target_pairs={{0,16},{4,12},{8,24},{12,4},{16,0},{20,28},{24,8},{28,20},{1,17},{... | collective-permute-start | bytes 688136 | tf_op jit(solution)/shard_map/ppermute | solution.py:204
  58.7 1.8 %copy-start.8 = (bf16[80,1792]{1,0:T(8,128)(2,1)S(1)}, bf16[80,1792]{1,0:T(8,128)(2,1)}, u32[]{:S(2)}) copy-start(bf16[80,1792]{1,0:T(8,128)(2,1)} %copy-done.7) | copy-start | bytes 860164
  59.7 0.9 collective-permute-start.7
  60.5 35.7 %collective-permute-start.25 = (bf16[256,1792]{1,0:T(8,128)(2,1)S(1)}, bf16[256,1792]{1,0:T(8,128)(2,1)}, u32[]{:S(2)}, u32[]{:S(2)}) collective-permute-start(bf16[256,1792]{1,0:T(8,128)(2,1)S(1)} %pad_maximum_fusion.3.refs_0_), channel_id=1, source_target_pairs={{0,4},{4,0},{8,12},{12,8},{16,20},{20,16},{24,28},{28,24},{1,5},{5... | collective-permute-start | bytes 2752520 | tf_op jit(solution)/shard_map/ppermute | solution.py:206
  61.3 3.9 %copy-start.6 = (bf16[64,1792]{1,0:T(8,128)(2,1)S(1)}, bf16[64,1792]{1,0:T(8,128)(2,1)}, u32[]{:S(2)}) copy-start(bf16[64,1792]{1,0:T(8,128)(2,1)} %get-tuple-element.113) | copy-start | bytes 688132
  61.3 13.4 %collective-permute-start.13 = (bf16[64,1792]{1,0:T(8,128)(2,1)S(1)}, bf16[64,1792]{1,0:T(8,128)(2,1)S(1)}, u32[]{:S(2)}, u32[]{:S(2)}) collective-permute-start(bf16[64,1792]{1,0:T(8,128)(2,1)S(1)} %get-tuple-element.111), channel_id=1, source_target_pairs={{1,0},{2,3},{5,4},{6,7},{9,8},{10,11},{13,12},{14,15},{17,16},{18,... | collective-permute-start | bytes 688136 | tf_op jit(solution)/shard_map/ppermute | solution.py:262
  64.8 41.3 %collective-permute-start.21 = (bf16[256,1792]{1,0:T(8,128)(2,1)S(1)}, bf16[256,1792]{1,0:T(8,128)(2,1)}, u32[]{:S(2)}, u32[]{:S(2)}) collective-permute-start(bf16[256,1792]{1,0:T(8,128)(2,1)S(1)} %pad_maximum_fusion.2.refs_0_), channel_id=1, source_target_pairs={{0,4},{4,0},{8,12},{12,8},{16,20},{20,16},{24,28},{28,24},{1,5},{5... | collective-permute-start | bytes 2752520 | tf_op jit(solution)/shard_map/ppermute | solution.py:206
  65.2 15.2 %collective-permute-start.8 = (bf16[64,1920]{1,0:T(8,128)(2,1)S(1)}, bf16[64,1920]{1,0:T(8,128)(2,1)S(1)}, u32[]{:S(2)}, u32[]{:S(2)}) collective-permute-start(bf16[64,1920]{1,0:T(8,128)(2,1)S(1)} %concatenate.29), channel_id=1, source_target_pairs={{1,0},{2,3},{5,4},{6,7},{9,8},{10,11},{13,12},{14,15},{17,16},{18,... | collective-permute-start | bytes 737288 | tf_op jit(solution)/shard_map/ppermute | solution.py:262
  74.7 6.1 %collective-permute-start.14 = (bf16[64,1792]{1,0:T(8,128)(2,1)S(1)}, bf16[64,1792]{1,0:T(8,128)(2,1)S(1)}, u32[]{:S(2)}, u32[]{:S(2)}) collective-permute-start(bf16[64,1792]{1,0:T(8,128)(2,1)S(1)} %broadcast_select_fusion.7), channel_id=1, source_target_pairs={{0,8},{4,12},{8,0},{12,4},{16,24},{20,28},{24,16},{28,20},{1,9},{5... | collective-permute-start | bytes 688136 | tf_op jit(solution)/shard_map/ppermute | solution.py:201
  76.6 6.0 %collective-permute-start.15 = (bf16[64,1792]{1,0:T(8,128)(2,1)S(1)}, bf16[64,1792]{1,0:T(8,128)(2,1)S(1)}, u32[]{:S(2)}, u32[]{:S(2)}) collective-permute-start(bf16[64,1792]{1,0:T(8,128)(2,1)S(1)} %broadcast_select_fusion.7), channel_id=1, source_target_pairs={{0,16},{4,20},{8,24},{12,28},{16,0},{20,4},{24,8},{28,12},{1,17},{... | collective-permute-start | bytes 688136 | tf_op jit(solution)/shard_map/ppermute | solution.py:202
  80.4 7.8 %collective-permute-start.10 = (bf16[64,1920]{1,0:T(8,128)(2,1)S(1)}, bf16[64,1920]{1,0:T(8,128)(2,1)S(1)}, u32[]{:S(2)}, u32[]{:S(2)}) collective-permute-start(bf16[64,1920]{1,0:T(8,128)(2,1)S(1)} %broadcast_select_fusion.1), channel_id=1, source_target_pairs={{0,16},{4,20},{8,24},{12,28},{16,0},{20,4},{24,8},{28,12},{1,17},{... | collective-permute-start | bytes 737288 | tf_op jit(solution)/shard_map/ppermute | solution.py:202
  80.8 8.8 %collective-permute-start.9 = (bf16[64,1920]{1,0:T(8,128)(2,1)S(1)}, bf16[64,1920]{1,0:T(8,128)(2,1)S(1)}, u32[]{:S(2)}, u32[]{:S(2)}) collective-permute-start(bf16[64,1920]{1,0:T(8,128)(2,1)S(1)} %broadcast_select_fusion.1), channel_id=1, source_target_pairs={{0,8},{4,12},{8,0},{12,4},{16,24},{20,28},{24,16},{28,20},{1,9},{5... | collective-permute-start | bytes 737288 | tf_op jit(solution)/shard_map/ppermute | solution.py:201
  82.7 8.8 %collective-permute-start.16 = (bf16[64,1792]{1,0:T(8,128)(2,1)S(1)}, bf16[64,1792]{1,0:T(8,128)(2,1)S(1)}, u32[]{:S(2)}, u32[]{:S(2)}) collective-permute-start(bf16[64,1792]{1,0:T(8,128)(2,1)S(1)} %broadcast_select_fusion.4), channel_id=1, source_target_pairs={{0,16},{4,12},{8,24},{12,4},{16,0},{20,28},{24,8},{28,20},{1,17},{... | collective-permute-start | bytes 688136 | tf_op jit(solution)/shard_map/ppermute | solution.py:204
  89.7 6.3 %collective-permute-start.11 = (bf16[64,1920]{1,0:T(8,128)(2,1)S(1)}, bf16[64,1920]{1,0:T(8,128)(2,1)S(1)}, u32[]{:S(2)}, u32[]{:S(2)}) collective-permute-start(bf16[64,1920]{1,0:T(8,128)(2,1)S(1)} %broadcast_select_fusion), channel_id=1, source_target_pairs={{0,16},{4,12},{8,24},{12,4},{16,0},{20,28},{24,8},{28,20},{1,17},{... | collective-permute-start | bytes 737288 | tf_op jit(solution)/shard_map/ppermute | solution.py:204
  92.5 17.4 %collective-permute-start.17 = (bf16[256,1792]{1,0:T(8,128)(2,1)}, bf16[256,1792]{1,0:T(8,128)(2,1)}, u32[]{:S(2)}, u32[]{:S(2)}) collective-permute-start(bf16[256,1792]{1,0:T(8,128)(2,1)} %pad_maximum_fusion.1.refs_0_), channel_id=1, source_target_pairs={{0,4},{4,0},{8,12},{12,8},{16,20},{20,16},{24,28},{28,24},{1,5},{5... | collective-permute-start | bytes 2752520 | tf_op jit(solution)/shard_map/ppermute | solution.py:206
  96.0 18.0 %collective-permute-start.12 = (bf16[256,1920]{1,0:T(8,128)(2,1)S(1)}, bf16[256,1920]{1,0:T(8,128)(2,1)}, u32[]{:S(2)}, u32[]{:S(2)}) collective-permute-start(bf16[256,1920]{1,0:T(8,128)(2,1)S(1)} %pad_maximum_fusion.refs_1_), channel_id=1, source_target_pairs={{0,4},{4,0},{8,12},{12,8},{16,20},{20,16},{24,28},{28,24},{1,5},{5... | collective-permute-start | bytes 2949128 | tf_op jit(solution)/shard_map/ppermute | solution.py:206
  96.2 3.1 %copy-start = (bf16[1,7168,512]{2,1,0:T(8,128)(2,1)S(1)}, bf16[1,7168,512]{2,1,0:T(8,128)(2,1)}, u32[]{:S(2)}) copy-start(bf16[1,7168,512]{2,1,0:T(8,128)(2,1)} %refs_3_.7) | copy-start | bytes 22020100
  99.3 3.1 %copy-start.1 = (bf16[1,7168,512]{2,1,0:T(8,128)(2,1)S(1)}, bf16[1,7168,512]{2,1,0:T(8,128)(2,1)}, u32[]{:S(2)}) copy-start(bf16[1,7168,512]{2,1,0:T(8,128)(2,1)} %refs_4_.1) | copy-start | bytes 22020100
  119.7 18.6 %copy-start.10 = (f32[64,2]{0,1:T(2,128)S(1)}, f32[64,2]{0,1:T(2,128)}, u32[]{:S(2)}) copy-start(f32[64,2]{0,1:T(2,128)} %param.15) | copy-start | bytes 1540
  120.7 15.4 %all-to-all-start = ((f32[32,1,256]{2,1,0:T(1,128)}), f32[32,1,256]{2,1,0:T(1,128)S(1)}, u32[]{:S(2)}, u32[]{:S(2)}) async-start(f32[32,1,256]{2,1,0:T(1,128)} %all_to_all.6), calls=%async_computation | async-start | bytes 65536 | tf_op jit(solution)/shard_map/all_to_all | solution.py:293

commit v2 on v0

--- a/solution.py
+++ b/solution.py
@@ -1,17 +1,20 @@
 import jax
 import jax.numpy as jnp
 from jax import lax
+from jax.experimental import pallas as pl
+from jax.experimental.pallas import tpu as pltpu
 from jax.sharding import PartitionSpec as P
 
 D = 7168
 FF = 2048
 CAP = 24
+EXTRA = 128
 
 
 epsilon = 1e-06
 
 
-def per_device(residual, attn_parts, norm_gain, routes, route_weights, w_gate, w_gate_q):
+def general_device(residual, attn_parts, norm_gain, routes, route_weights, w_gate, w_gate_q):
     n_expert = lax.axis_size("expert")
     tok_count = residual.shape[0]
     local_cols = residual.shape[1]
@@ -38,8 +41,6 @@
     placing = (slot_ids[:, None] == target[None, :]).reshape(n_expert * CAP, tok_count, top_count)
     dispatch = jnp.sum(placing.astype(jnp.int32), axis=2).astype(jnp.bfloat16)
     count_send = load_counts.astype(jnp.bfloat16).reshape(n_expert, 1)
-    weight_full = w_gate[0]
-    weight_quant = w_gate_q[0]
     outgoing = jnp.dot(dispatch, normed, preferred_element_type=jnp.float32).astype(jnp.bfloat16)
     outgoing = outgoing.reshape(n_expert, CAP, local_cols)
     arrived, arrived_counts = (
@@ -48,8 +49,8 @@
     )
     own_block = arrived.reshape(n_expert * CAP, local_cols)
     column_block = lax.all_gather(own_block, "tensor", axis=1, tiled=True)
-    full_acc = jnp.dot(column_block, weight_full, preferred_element_type=jnp.float32)
-    quant_acc = jnp.dot(column_block, weight_quant, preferred_element_type=jnp.float32)
+    full_acc = jnp.dot(column_block, w_gate[0], preferred_element_type=jnp.float32)
+    quant_acc = jnp.dot(column_block, w_gate_q[0], preferred_element_type=jnp.float32)
     block_squares = jnp.einsum("rc,rc->c", own_block, own_block, preferred_element_type=jnp.float32)
     total_load = jnp.sum(arrived_counts.astype(jnp.float32))
     hess_local = 2.0 * block_squares / total_load
@@ -69,6 +70,300 @@
     return (token_error, expert_total.reshape(1), hess_local.reshape(1, local_cols))
 
 
+def in_vmem(x):
+    return pltpu.with_memory_space_constraint(x, pltpu.VMEM)
+
+
+def in_hbm(x):
+    return pltpu.with_memory_space_constraint(x, pltpu.HBM)
+
+
+VMEM_SPEC = pl.BlockSpec(memory_space=pltpu.VMEM)
+HBM_SPEC = pl.BlockSpec(memory_space=pl.ANY)
+SMEM_SPEC = pl.BlockSpec(memory_space=pltpu.SMEM)
+TILES = 2
+
+
+def load_slabs(number_ref, hbm_refs, slab_refs, sems):
+    depth, cols = slab_refs[0].shape
+    tile = cols // TILES
+    start = pl.multiple_of(number_ref[0] * depth, depth)
+    copies = []
+    for t in range(TILES):
+        columns = pl.ds(t * tile, tile)
+        for i in range(2):
+            copy = pltpu.make_async_copy(
+                hbm_refs[i].at[pl.ds(start, depth), columns],
+                slab_refs[i].at[:, columns],
+                sems.at[2 * t + i],
+            )
+            copy.start()
+            copies.append(copy)
+    return copies
+
+
+def add_kernel(first, depth, number_ref, w_ref, wq_ref, near_ref, far_ref, *refs):
+    if first:
+        outs, slabs, sems = refs[:2], refs[2:4], refs[4]
+    else:
+        ins, outs, slabs, sems = refs[:2], refs[2:4], refs[4:6], refs[6]
+    copies = load_slabs(number_ref, (w_ref, wq_ref), slabs, sems)
+    tile = slabs[0].shape[1] // TILES
+    half = near_ref.shape[0]
+    for t in range(TILES):
+        columns = slice(t * tile, (t + 1) * tile)
+        for i in range(2):
+            copies[2 * t + i].wait()
+            for part, ref in enumerate((near_ref, far_ref)):
+                rows = slice(part * half, (part + 1) * half)
+                value = jnp.dot(ref[:, :depth], slabs[i][:, columns], preferred_element_type=jnp.float32)
+                if not first:
+                    value = value + ins[i][rows, columns]
+                outs[i][rows, columns] = value
+
+
+def params():
+    return pltpu.CompilerParams(vmem_limit_bytes=24 * 1024 * 1024)
+
+
+def cost(rows, depth, cols):
+    return pl.CostEstimate(flops=4 * rows * depth * cols, bytes_accessed=4 * depth * cols, transcendentals=0)
+
+
+def add_product(number, w, wq, near, far, sums):
+    half, depth = near.shape
+    cols = w.shape[1]
+    args = [number, in_hbm(w), in_hbm(wq), in_vmem(near), in_vmem(far)]
+    args += [in_vmem(x) for x in sums or ()]
+
+    def kernel(*refs):
+        add_kernel(not sums, depth, *refs)
+
+    return pl.pallas_call(
+        kernel,
+        in_specs=[SMEM_SPEC, HBM_SPEC, HBM_SPEC] + [VMEM_SPEC] * (len(args) - 3),
+        out_specs=[VMEM_SPEC] * 2,
+        out_shape=[pltpu.VMEM((2 * half, cols), jnp.float32)] * 2,
+        input_output_aliases={5: 0, 6: 1} if sums else {},
+        scratch_shapes=[pltpu.VMEM((depth, cols), w.dtype)] * 2 + [pltpu.SemaphoreType.DMA((2 * TILES,))],
+        compiler_params=params(),
+        cost_estimate=cost(2 * half, depth, cols),
+    )(*args)
+
+
+def row_stats(depth, expert, rows_ref, slabs, ins, offset, wait):
+    half = rows_ref.shape[0]
+    tile = slabs[0].shape[1] // TILES
+    err = jnp.zeros((half, 1), jnp.float32)
+    power = jnp.zeros((half, 1), jnp.float32)
+    for t in range(TILES):
+        columns = slice(t * tile, (t + 1) * tile)
+        made = []
+        for i in range(2):
+            wait(2 * t + i)
+            value = jnp.dot(rows_ref[:, :depth], slabs[i][:, columns], preferred_element_type=jnp.float32)
+            made.append(value + ins[i][offset : offset + half, columns])
+        diff = made[0] - made[1]
+        err = err + jnp.sum(diff * diff, axis=1, keepdims=True)
+        power = power + jnp.sum(made[0] * made[0], axis=1, keepdims=True)
+    extra = rows_ref[:, depth:].astype(jnp.float32)
+    lane = lax.broadcasted_iota(jnp.int32, (half, EXTRA), 1)
+    squares = extra[:, 0:1] + extra[:, 1:2] + extra[:, 2:3]
+    scale = lax.rsqrt(squares / D + epsilon)
+    scale = scale * scale
+    named = (lane >= 3) & (extra == expert.astype(jnp.float32))
+    routed = jnp.sum(jnp.where(named, 1.0, 0.0), axis=1, keepdims=True)
+    stats = jnp.where(lane == 0, err * (scale / FF), 0.0)
+    stats = jnp.where(lane == 1, power * (scale / FF), stats)
+    stats = jnp.where(lane == 2, routed, stats)
+    stats = jnp.where(lane == 3, scale * routed, stats)
+    return stats.T[:8, :]
+
+
+def near_kernel(depth, number_ref, w_ref, wq_ref, near_ref, full_ref, quant_ref, stats_ref, slab, slab_q, sems):
+    copies = load_slabs(number_ref, (w_ref, wq_ref), (slab, slab_q), sems)
+    stats_ref[...] = row_stats(
+        depth, number_ref[1], near_ref, (slab, slab_q), (full_ref, quant_ref), 0, lambda n: copies[n].wait()
+    )
+
+
+def far_kernel(depth, tok, n_z, number_ref, far_ref, full_ref, quant_ref, slab, slab_q, near_stats_ref, stats_ref, out_ref):
+    half = far_ref.shape[0]
+    expert = number_ref[1]
+    far_stats = row_stats(depth, expert, far_ref, (slab, slab_q), (full_ref, quant_ref), half, lambda n: None)
+    near_stats = near_stats_ref[...]
+    stats_ref[...] = far_stats
+    sums = jnp.sum(near_stats * near_stats[2:3, :] + far_stats * far_stats[2:3, :], axis=1, keepdims=True)
+    lane = lax.broadcasted_iota(jnp.int32, (8, 2 * tok), 1)
+    for part, stats in enumerate((near_stats, far_stats)):
+        for pair in range(2):
+            both = stats[:, pair * 2 * tok : (pair + 1) * 2 * tok]
+            for odd in range(2):
+                owner = (4 * pair + 2 * odd + part) ^ expert
+                block = jnp.where(lane < tok, pltpu.roll(both, tok, 1) if odd else both, sums)
+                for z in range(n_z):
+                    out_ref[owner * n_z + z] = block
+
+
+def finish_kernel(n_z, number_ref, back_ref, routes_ref, weights_ref, token_ref, expert_ref):
+    top, tok = routes_ref.shape
+    n_expert = back_ref.shape[0] // n_z
+    own = jnp.zeros((8, 2 * tok), jnp.float32)
+    err = [jnp.zeros((1, tok), jnp.float32)] * top
+    power = [jnp.zeros((1, tok), jnp.float32)] * top
+    for i in range(n_expert):
+        tile = back_ref[i * n_z]
+        for z in range(1, n_z):
+            tile = tile + back_ref[i * n_z + z]
+        own = jnp.where(number_ref[1] == i, tile, own)
+        for k in range(top):
+            here = routes_ref[k : k + 1, :] == i
+            err[k] = jnp.where(here, tile[0:1, :tok], err[k])
+            power[k] = jnp.where(here, tile[1:2, :tok], power[k])
+    total = jnp.zeros((1, tok), jnp.float32)
+    for k in range(top):
+        total = total + weights_ref[k : k + 1, :] * (err[k] / (power[k] + epsilon))
+    token_ref[...] = total
+    expert_ref[...] = own[0:1, tok : tok + 1] / (own[1:2, tok : tok + 1] + epsilon)
+
+
+def last_product(number, w, wq, near, far_of, sums, n_z):
+    half, full_depth = near.shape
+    depth = full_depth - EXTRA
+    cols = w.shape[1]
+    tok = half // 4
+    sums = [in_vmem(x) for x in sums]
+    slabs = [pltpu.VMEM((depth, cols), w.dtype)] * 2
+
+    def first(*refs):
+        near_kernel(depth, *refs)
+
+    near_stats, slab, slab_q = pl.pallas_call(
+        first,
+        in_specs=[SMEM_SPEC, HBM_SPEC, HBM_SPEC] + [VMEM_SPEC] * 3,
+        out_specs=[VMEM_SPEC] * 3,
+        out_shape=[pltpu.VMEM((8, half), jnp.float32)] + slabs,
+        scratch_shapes=[pltpu.SemaphoreType.DMA((2 * TILES,))],
+        compiler_params=params(),
+        cost_estimate=cost(half, depth, cols),
+    )(number, in_hbm(w), in_hbm(wq), in_vmem(near), *sums)
+    far = far_of(near)
+
+    def second(*refs):
+        far_kernel(depth, tok, n_z, *refs)
+
+    far_stats, payload = pl.pallas_call(
+        second,
+        in_specs=[SMEM_SPEC] + [VMEM_SPEC] * 6,
+        out_specs=[VMEM_SPEC] * 2,
+        out_shape=[
+            jax.ShapeDtypeStruct((8, half), jnp.float32),
+            jax.ShapeDtypeStruct((8 * n_z, 8, 2 * tok), jnp.float32),
+        ],
+        compiler_params=params(),
+        cost_estimate=cost(half, depth, cols),
+    )(number, in_vmem(far), *sums, in_vmem(slab), in_vmem(slab_q), in_vmem(near_stats))
+    return near_stats, far_stats, payload
+
+
+def in_pieces(squares):
+    high = lax.reduce_precision(squares, 8, 7)
+    mid = lax.reduce_precision(squares - high, 8, 7)
+    return [high, mid, squares - high - mid]
+
+
+def line_device(residual, attn_parts, norm_gain, routes, route_weights, w_gate, w_gate_q):
+    z = lax.axis_index("tensor")
+    e = lax.axis_index("expert")
+    n_z = 4
+    tok = residual.shape[0]
+    width = residual.shape[1]
+
+    def over_z(x, k):
+        return lax.ppermute(x, "tensor", [(i, i ^ k) for i in range(n_z)])
+
+    swap_x = [(i, i ^ 2) for i in range(8)]
+    swap_y = [(i, i ^ 4) for i in range(8)]
+    swap_core = [(i, i ^ 1) for i in range(8)]
+    forward = [(i, i ^ 2 if i & 1 else i ^ 4) for i in range(8)]
+
+    def quarter(k):
+        return lax.dynamic_slice(attn_parts[0], (0, (z ^ k) * width), (tok, width))
+
+    arrived = [over_z(quarter(k), k) for k in (3, 2, 1)]
+    hidden = residual.astype(jnp.float32) + quarter(0).astype(jnp.float32)
+    for part in arrived:
+        hidden = hidden + part.astype(jnp.float32)
+    squares = jnp.sum(hidden * hidden, axis=1, keepdims=True)
+    own = (hidden * norm_gain.astype(jnp.float32)[None, :]).astype(jnp.bfloat16)
+
+    def extra(total):
+        return jnp.concatenate(
+            in_pieces(total)
+            + [routes.astype(jnp.float32)]
+            + [jnp.full((tok, EXTRA - 3 - routes.shape[1]), -1.0, jnp.float32)],
+            axis=1,
+        ).astype(jnp.bfloat16)
+
+    outgoing = jnp.concatenate([own, extra(squares)], axis=1)
+    others = [over_z(outgoing, k) for k in (1, 2, 3)]
+
+    def with_total(last):
+        total = squares
+        for part in (others[0], others[1], last):
+            wide = part[:, width : width + 3].astype(jnp.float32)
+            total = total + (wide[:, 0:1] + wide[:, 1:2] + wide[:, 2:3])
+        return jnp.concatenate([last[:, :width], extra(total)], axis=1)
+
+    blocks = []
+    sums = None
+    held = None
+    for k in range(n_z):
+        rows = own if k == 0 else others[k - 1]
+        if k:
+            rows, _ = lax.optimization_barrier((rows, held))
+        if k:
+            rows = with_total(rows) if k == n_z - 1 else rows[:, :width]
+        if k:
+            diagonal = lax.ppermute(held, "expert", forward)
+            near = jnp.concatenate(pieces + [diagonal], axis=0)
+            if sums:
+                near, sums = lax.optimization_barrier((near, sums))
+            far = lax.ppermute(near, "expert", swap_core)
+            number = jnp.stack([z ^ (k - 1), e]).astype(jnp.int32)
+            sums = add_product(number, w_gate[0], w_gate_q[0], near, far, sums)
+            blocks.append((near, far))
+        from_x = lax.ppermute(rows, "expert", swap_x)
+        from_y = lax.ppermute(rows, "expert", swap_y)
+        pieces = [rows, from_x, from_y]
+        held = jnp.where(e % 2 == 1, from_y, from_x)
+    diagonal = lax.ppermute(held, "expert", forward)
+    near = jnp.concatenate(pieces + [diagonal], axis=0)
+    near, sums = lax.optimization_barrier((near, sums))
+    number = jnp.stack([z ^ (n_z - 1), e]).astype(jnp.int32)
+    near_stats, far_stats, payload = last_product(
+        number, w_gate[0], w_gate_q[0], near, lambda x: lax.ppermute(x, "expert", swap_core), sums, n_z
+    )
+    back = lax.all_to_all(payload, ("expert", "tensor"), split_axis=0, concat_axis=0, tiled=True)
+
+    hess = 0.0
+    for part, stats in zip(blocks[0], (near_stats, far_stats)):
+        wide = part.astype(jnp.float32)
+        hess = hess + jnp.sum(wide * wide * stats[3][:, None], axis=0)
+    hess = 2.0 * hess / (jnp.sum(near_stats[2]) + jnp.sum(far_stats[2]))
+
+    def finish(*refs):
+        finish_kernel(n_z, *refs)
+
+    token_error, expert_total = pl.pallas_call(
+        finish,
+        in_specs=[SMEM_SPEC] + [VMEM_SPEC] * 3,
+        out_specs=[VMEM_SPEC] * 2,
+        out_shape=[jax.ShapeDtypeStruct((1, tok), jnp.float32), jax.ShapeDtypeStruct((1, 1), jnp.float32)],
+    )(number, back, routes.T, route_weights.T)
+    return (token_error.reshape(tok), expert_total.reshape(1), hess.reshape(1, width))
+
+
 def solution(mesh):
     placed = (
         P("expert", "tensor"),
@@ -79,8 +374,9 @@
         P("expert", None, "tensor"),
         P("expert", None, "tensor"),
     )
+    on_line = mesh.shape["expert"] == 8 and mesh.shape["tensor"] == 4
     return jax.shard_map(
-        per_device,
+        line_device if on_line else general_device,
         mesh=mesh,
         in_specs=placed,
         out_specs=(P("expert"), P("expert"), P("expert", "tensor")),

time: 171 us -> 113 us (0.66)
  waiting for transfers between devices: 81.1 us -> 45.5 us
  blocking collectives: 34.7 us -> 0 us
  Pallas kernels: 0 us -> 22.7 us
  starting transfers between devices: 10.6 us -> 26.7 us
  between operations: 16.7 us -> 2.21 us
  matrix products: 12 us -> 0 us
    all_gather x1 -> x0, waiting for transfers between devices: 44.4 us -> none  [per_device(): column_block = lax.all_gather(own_block, 'tensor', axis=1, tiled=True)]
    ppermute x0 -> x22, waiting for transfers between devices: none -> 40.6 us  [the longest x6 24.2 us: over_z(): return lax.ppermute(x, 'tensor', [(i, i ^ k) for i in range(n_z)])]
    reduce_scatter x1 -> x0, waiting for transfers between devices: 27.1 us -> none  [per_device(): lax.psum_scatter(attn_parts[0].astype(jnp.float32).astype(jnp.bfloat16),...]
    ppermute x0 -> x22, starting transfers between devices: none -> 22.9 us  [the longest x6 10.4 us: over_z(): return lax.ppermute(x, 'tensor', [(i, i ^ k) for i in range(n_z)])]
    pallas_call x0 -> x6, Pallas kernels: none -> 22.7 us  [the longest x3 14 us: add_product(): pl.pallas_call(kernel, in_specs=[SMEM_SPEC, HBM_SPEC, HBM_SPEC] + [VMEM_S...]
    psum x2 -> x0, blocking collectives: 19.6 us -> none  [the longest x1 9.92 us: per_device(): err_slots, pow_slots = lax.psum((err_part, pow_part), 'tensor')]
    all_to_all x1 -> x0, blocking collectives: 15.1 us -> none  [per_device(): lax.all_to_all(outgoing, 'expert', split_axis=0, concat_axis=0, tiled=True)]
    dot_general x3 -> x0, matrix products: 12 us -> none  [the longest x1 5.75 us: per_device(): jnp.dot(column_block, weight_full, preferred_element_type=jnp.float32)]
  transfers between devices with their start and end apart: 5 -> 23, of which waited for: 4 -> 11; matrix products, arithmetic and copies ran while one was open for 6% -> 10% of each run, Pallas kernels for 0% -> 13%
where the time goes in v2:
time: 113 us
  waiting for transfers between devices  45.5 us (40%)
  starting transfers between devices  26.7 us (24%)
  Pallas kernels  22.7 us (20%)
  other arithmetic  9.37 us (8%)
  local copies, waits for them, and re-layouts  6.17 us (5%)
  between operations  2.21 us (2%)
    ppermute x6, waiting for transfers between devices, over_z(): return lax.ppermute(x, 'tensor', [(i, i ^ k) for i in range(n_z)])  24.2 us
    pallas_call x3, Pallas kernels, add_product(): pl.pallas_call(kernel, in_specs=[SMEM_SPEC, HBM_SPEC, HBM_SPEC] + [VMEM_S...  14 us
    ppermute x6, starting transfers between devices, over_z(): return lax.ppermute(x, 'tensor', [(i, i ^ k) for i in range(n_z)])  10.4 us
    ppermute x4, waiting for transfers between devices, line_device(): from_x = lax.ppermute(rows, 'expert', swap_x)  6.89 us
    ppermute x4, starting transfers between devices, line_device(): from_y = lax.ppermute(rows, 'expert', swap_y)  5.07 us
    ppermute x4, waiting for transfers between devices, line_device(): from_y = lax.ppermute(rows, 'expert', swap_y)  4.93 us
    all_to_all x1, waiting for transfers between devices, line_device(): lax.all_to_all(payload, ('expert', 'tensor'), split_axis=0, concat_axis=0...  4.84 us
    ppermute x4, waiting for transfers between devices, line_device(): diagonal = lax.ppermute(held, 'expert', forward)  4.55 us
  transfers between devices with their start and end apart: 23, of which 11 were waited for; matrix products, arithmetic and copies ran while one was open for 10% of the time, Pallas kernels for 13%

profile of v2, /device:TPU:0, one launch (start us, length us, event | category | flops | bytes accessed | tf_op | source)
XLA Modules:
  0.0 112.6 jit_solution(106113826999654986)
XLA Ops:
  0.7 1.2 %dynamic-slice_bitcast_fusion.2 = (bf16[64,1792]{1,0:T(8,128)(2,1)S(1)}, bf16[64,1792]{1,0:T(8,128)(2,1)S(1)}, bf16[64,1792]{1,0:T(8,128)(2,1)S(1)}) fusion(bf16[1,64,7168]{2,1,0:T(8,128)(2,1)} %param.8, s32[]{:T(128)S(6)} %select_n.50, s32[]{:T(128)S(6)} %select_n.52, s32[]{:T(128)S(6)} %select_n.51), kind=kLoop, calls=%fused_computation.15 | loop fusion | bytes 1376268 | tf_op jit(solution)/shard_map/dynamic_slice | solution.py:291
  1.9 5.1 %collective-permute-start = (bf16[64,1792]{1,0:T(8,128)(2,1)S(1)}, bf16[64,1792]{1,0:T(8,128)(2,1)S(1)}, u32[]{:S(2)}, u32[]{:S(2)}) collective-permute-start(bf16[64,1792]{1,0:T(8,128)(2,1)S(1)} %get-tuple-element.57), channel_id=1, source_target_pairs={{0,3},{1,2},{2,1},{3,0},{4,7},{5,6},{6,5},{7,4},{8,11},{9,10},{10,... | collective-permute-start | bytes 688136 | tf_op jit(solution)/shard_map/ppermute | solution.py:283
  7.0 0.6 collective-permute-start.2
  7.6 0.7 convert_element_type.51
  8.3 0.7 convert_element_type.53
  9.0 0.1 copy.20
  9.1 0.1 pad_add_fusion.3.refs_0_
  9.2 4.4 %collective-permute-done = bf16[64,1792]{1,0:T(8,128)(2,1)S(1)} collective-permute-done((bf16[64,1792]{1,0:T(8,128)(2,1)S(1)}, bf16[64,1792]{1,0:T(8,128)(2,1)S(1)}, u32[]{:S(2)}, u32[]{:S(2)}) %collective-permute-start) | collective-permute-done | bytes 229408 | tf_op jit(solution)/shard_map/ppermute | solution.py:283
  13.6 12.9 %collective-permute-done.1 = bf16[64,1792]{1,0:T(8,128)(2,1)S(1)} collective-permute-done((bf16[64,1792]{1,0:T(8,128)(2,1)S(1)}, bf16[64,1792]{1,0:T(8,128)(2,1)S(1)}, u32[]{:S(2)}, u32[]{:S(2)}) %collective-permute-start.1) | collective-permute-done | bytes 229408 | tf_op jit(solution)/shard_map/ppermute | solution.py:283
  26.5 1.3 %multiply_reduce_fusion.2 = (f32[64]{0:T(128)S(1)}, bf16[64,1792]{1,0:T(8,128)(2,1)S(1)}) fusion(bf16[64,1792]{1,0:T(8,128)(2,1)S(1)} %collective-permute-done.2, bf16[64,1792]{1,0:T(8,128)(2,1)S(1)} %collective-permute-done.1, bf16[64,1792]{1,0:T(8,128)(2,1)S(1)} %collective-permute-done, bf16[1,64,7168]{2,1,0:T(8,128)(2,1)} %param.8, s32[]{:T(128)S(6)} %select_n.49, ...), kind=kLoop, calls=%fused_computation.10 | loop fusion | flops 1490880 | bytes 1383684 | tf_op jit(solution)/shard_map/reduce_sum | solution.py:297
  27.8 1.6 %collective-permute-start.6 = (bf16[64,1792]{1,0:T(8,128)(2,1)S(1)}, bf16[64,1792]{1,0:T(8,128)(2,1)S(1)}, u32[]{:S(2)}, u32[]{:S(2)}) collective-permute-start(bf16[64,1792]{1,0:T(8,128)(2,1)S(1)} %get-tuple-element.56), channel_id=1, source_target_pairs={{0,16},{4,20},{8,24},{12,28},{16,0},{20,4},{24,8},{28,12},{1,17},{... | collective-permute-start | bytes 688136 | tf_op jit(solution)/shard_map/ppermute | solution.py:337
  29.4 1.5 %collective-permute-start.7 = (bf16[64,1792]{1,0:T(8,128)(2,1)S(1)}, bf16[64,1792]{1,0:T(8,128)(2,1)S(1)}, u32[]{:S(2)}, u32[]{:S(2)}) collective-permute-start(bf16[64,1792]{1,0:T(8,128)(2,1)S(1)} %get-tuple-element.56), channel_id=1, source_target_pairs={{0,8},{4,12},{8,0},{12,4},{16,24},{20,28},{24,16},{28,20},{1,9},{5... | collective-permute-start | bytes 688136 | tf_op jit(solution)/shard_map/ppermute | solution.py:336
  30.9 0.1 copy.19
  31.0 0.1 copy.18
  31.1 0.1 copy.21
  31.2 0.1 concatenate.24
  31.4 0.1 collective-permute-start.5
  31.4 3.0 %collective-permute-start.4 = (bf16[64,1920]{1,0:T(8,128)(2,1)S(1)}, bf16[64,1920]{1,0:T(8,128)(2,1)S(1)}, u32[]{:S(2)}, u32[]{:S(2)}) collective-permute-start(bf16[64,1920]{1,0:T(8,128)(2,1)S(1)} %concatenate.24), channel_id=1, source_target_pairs={{0,2},{1,3},{2,0},{3,1},{4,6},{5,7},{6,4},{7,5},{8,10},{9,11},{10,... | collective-permute-start | bytes 737288 | tf_op jit(solution)/shard_map/ppermute | solution.py:283
  34.5 0.1 collective-permute-done.6
  34.6 1.2 %collective-permute-done.7 = bf16[64,1792]{1,0:T(8,128)(2,1)S(1)} collective-permute-done((bf16[64,1792]{1,0:T(8,128)(2,1)S(1)}, bf16[64,1792]{1,0:T(8,128)(2,1)S(1)}, u32[]{:S(2)}, u32[]{:S(2)}) %collective-permute-start.7) | collective-permute-done | bytes 229408 | tf_op jit(solution)/shard_map/ppermute | solution.py:336
  35.8 6.9 %collective-permute-done.5 = bf16[64,1920]{1,0:T(8,128)(2,1)S(1)} collective-permute-done((bf16[64,1920]{1,0:T(8,128)(2,1)S(1)}, bf16[64,1920]{1,0:T(8,128)(2,1)S(1)}, u32[]{:S(2)}, u32[]{:S(2)}) %collective-permute-start.5) | collective-permute-done | bytes 245792 | tf_op jit(solution)/shard_map/ppermute | solution.py:283
  42.8 0.6 collective-permute-start.8
  43.4 0.5 collective-permute-start.9
  43.9 0.1 pad_add_fusion.2.refs_0_
  44.0 1.5 %collective-permute-start.3 = (bf16[64,1920]{1,0:T(8,128)(2,1)S(1)}, bf16[64,1920]{1,0:T(8,128)(2,1)S(1)}, u32[]{:S(2)}, u32[]{:S(2)}) collective-permute-start(bf16[64,1920]{1,0:T(8,128)(2,1)S(1)} %concatenate.24), channel_id=1, source_target_pairs={{0,3},{1,2},{2,1},{3,0},{4,7},{5,6},{6,5},{7,4},{8,11},{9,10},{10,... | collective-permute-start | bytes 737288 | tf_op jit(solution)/shard_map/ppermute | solution.py:283
  45.5 1.5 %collective-permute-start.17 = (bf16[64,1792]{1,0:T(8,128)(2,1)S(1)}, bf16[64,1792]{1,0:T(8,128)(2,1)S(1)}, u32[]{:S(2)}, u32[]{:S(2)}) collective-permute-start(bf16[64,1792]{1,0:T(8,128)(2,1)S(1)} %broadcast_select_fusion.3), channel_id=1, source_target_pairs={{0,16},{4,12},{8,24},{12,4},{16,0},{20,28},{24,8},{28,20},{1,17},{... | collective-permute-start | bytes 688136 | tf_op jit(solution)/shard_map/ppermute | solution.py:328
  47.0 2.3 %collective-permute-done.8 = bf16[64,1792]{1,0:T(8,128)(2,1)S(1)} collective-permute-done((bf16[64,1792]{1,0:T(8,128)(2,1)S(1)}, bf16[64,1792]{1,0:T(8,128)(2,1)S(1)}, u32[]{:S(2)}, u32[]{:S(2)}) %collective-permute-start.8) | collective-permute-done | bytes 229408 | tf_op jit(solution)/shard_map/ppermute | solution.py:337
  49.3 2.6 %collective-permute-done.9 = bf16[64,1792]{1,0:T(8,128)(2,1)S(1)} collective-permute-done((bf16[64,1792]{1,0:T(8,128)(2,1)S(1)}, bf16[64,1792]{1,0:T(8,128)(2,1)S(1)}, u32[]{:S(2)}, u32[]{:S(2)}) %collective-permute-start.9) | collective-permute-done | bytes 229408 | tf_op jit(solution)/shard_map/ppermute | solution.py:336
  52.0 1.6 %collective-permute-start.10 = (bf16[64,1792]{1,0:T(8,128)(2,1)S(1)}, bf16[64,1792]{1,0:T(8,128)(2,1)S(1)}, u32[]{:S(2)}, u32[]{:S(2)}) collective-permute-start(bf16[64,1792]{1,0:T(8,128)(2,1)S(1)} %slice.58), channel_id=1, source_target_pairs={{0,16},{4,20},{8,24},{12,28},{16,0},{20,4},{24,8},{28,12},{1,17},{... | collective-permute-start | bytes 688136 | tf_op jit(solution)/shard_map/ppermute | solution.py:337
  53.6 0.5 collective-permute-start.11
  54.1 0.7 copy-done.4
  54.9 0.1 collective-permute-start.18
  54.9 0.6 collective-permute-start.16
  55.5 2.5 %collective-permute-done.10 = bf16[64,1792]{1,0:T(8,128)(2,1)S(1)} collective-permute-done((bf16[64,1792]{1,0:T(8,128)(2,1)S(1)}, bf16[64,1792]{1,0:T(8,128)(2,1)S(1)}, u32[]{:S(2)}, u32[]{:S(2)}) %collective-permute-start.10) | collective-permute-done | bytes 229408 | tf_op jit(solution)/shard_map/ppermute | solution.py:337
  58.1 3.1 %collective-permute-done.11 = bf16[64,1792]{1,0:T(8,128)(2,1)S(1)} collective-permute-done((bf16[64,1792]{1,0:T(8,128)(2,1)S(1)}, bf16[64,1792]{1,0:T(8,128)(2,1)S(1)}, u32[]{:S(2)}, u32[]{:S(2)}) %collective-permute-start.11) | collective-permute-done | bytes 229408 | tf_op jit(solution)/shard_map/ppermute | solution.py:336
  61.1 0.8 broadcast_select_fusion.1
  61.9 1.0 pad_maximum_fusion.2.refs_3_
  63.0 4.3 %shard_map.94 = (f32[512,512]{1,0:T(8,128)S(1)}, f32[512,512]{1,0:T(8,128)S(1)}) custom-call(s32[2]{0:T(128)S(1)} %pad_add_fusion.3.refs_0_, bf16[7168,512]{1,0:T(8,128)(2,1)} %bitcast.30, bf16[7168,512]{1,0:T(8,128)(2,1)} %bitcast.34, bf16[256,1792]{1,0:T(8,128)(2,1)S(1)} %pad_maximum_fusion.3.refs_3_, bf16[256,1792]{1,0:T(8,128)(2,1)S(1)} %collective-permute-done.18.refs_4_), custom_call_target="tpu_custom_call" | custom-call | flops 1879048192 | bytes 3670016 | tf_op jit(solution)/shard_map/pallas_call | solution.py:142
  67.3 0.1 collective-permute-start.19
  67.4 0.7 fusion.4
  68.1 0.7 slice.59
  68.8 1.7 %concatenate.25 = bf16[64,1920]{1,0:T(8,128)(2,1)} concatenate(bf16[64,1792]{1,0:T(8,128)(2,1)} %slice.59, bf16[64,1]{1,0:T(8,128)(2,1)S(1)} %get-tuple-element.63, bf16[64,1]{1,0:T(8,128)(2,1)S(1)} %get-tuple-element.62, bf16[64,1]{1,0:T(8,128)(2,1)} %get-tuple-element.53, bf16[64,2]{1,0:T(8,128)(2,1)S(1)} %copy.20, bf16[64,123]{1,0:T(8,128)(2,1)S(1)} %broadcast.27), dimensions={1} | concatenate | bytes 491520 | tf_op jit(solution)/shard_map/concatenate | solution.py:316
  70.5 0.7 collective-permute-start.12
  71.2 1.3 %collective-permute-start.13 = (bf16[64,1920]{1,0:T(8,128)(2,1)}, bf16[64,1920]{1,0:T(8,128)(2,1)S(1)}, u32[]{:S(2)}, u32[]{:S(2)}) collective-permute-start(bf16[64,1920]{1,0:T(8,128)(2,1)} %concatenate.25), channel_id=1, source_target_pairs={{0,16},{4,20},{8,24},{12,28},{16,0},{20,4},{24,8},{28,12},{1,17},{... | collective-permute-start | bytes 737288 | tf_op jit(solution)/shard_map/ppermute | solution.py:337
  72.6 1.3 %pad_maximum_fusion.1.refs_3_ = bf16[256,1792]{1,0:T(8,128)(2,1)S(1)} fusion(bf16[64,1792]{1,0:T(8,128)(2,1)} %collective-permute-done.15, bf16[64,1792]{1,0:T(8,128)(2,1)} %copy-done.5, bf16[64,1792]{1,0:T(8,128)(2,1)} %copy-done.6, bf16[64,1792]{1,0:T(8,128)(2,1)} %copy-done.3), kind=kLoop, calls=%fused_computation.3 | loop fusion | flops 3670016 | bytes 1835008 | tf_op jit(solution)/shard_map/concatenate | solution.py:329
  73.9 5.3 %shard_map.95 = (f32[512,512]{1,0:T(8,128)S(1)}, f32[512,512]{1,0:T(8,128)S(1)}) custom-call(s32[2]{0:T(128)S(1)} %pad_add_fusion.2.refs_0_, bf16[7168,512]{1,0:T(8,128)(2,1)} %bitcast.31, bf16[7168,512]{1,0:T(8,128)(2,1)} %bitcast.35, bf16[256,1792]{1,0:T(8,128)(2,1)} %pad_maximum_fusion.2.refs_3_, ...), custom_call_target="tpu_custom_call", output_to_operand_aliasing={{0}: (5, {}), {1}: (6, {})} | custom-call | flops 1879048192 | bytes 3670016 | tf_op jit(solution)/shard_map/pallas_call | solution.py:142
  79.3 0.3 collective-permute-start.20
  79.6 1.6 %collective-permute-start.14 = (bf16[64,1920]{1,0:T(8,128)(2,1)S(1)}, bf16[64,1920]{1,0:T(8,128)(2,1)S(1)}, u32[]{:S(2)}, u32[]{:S(2)}) collective-permute-start(bf16[64,1920]{1,0:T(8,128)(2,1)S(1)} %broadcast_select_fusion), channel_id=1, source_target_pairs={{0,16},{4,12},{8,24},{12,4},{16,0},{20,28},{24,8},{28,20},{1,17},{... | collective-permute-start | bytes 737288 | tf_op jit(solution)/shard_map/ppermute | solution.py:340
  81.2 0.1 pad_add_fusion.1.refs_0_
  81.3 4.5 %collective-permute-done.14 = bf16[64,1920]{1,0:T(8,128)(2,1)S(1)} collective-permute-done((bf16[64,1920]{1,0:T(8,128)(2,1)S(1)}, bf16[64,1920]{1,0:T(8,128)(2,1)S(1)}, u32[]{:S(2)}, u32[]{:S(2)}) %collective-permute-start.14) | collective-permute-done | bytes 245792 | tf_op jit(solution)/shard_map/ppermute | solution.py:340
  85.8 0.1 pad_maximum_fusion.refs_3_
  85.9 4.4 %shard_map.96 = (f32[512,512]{1,0:T(8,128)S(1)}, f32[512,512]{1,0:T(8,128)S(1)}) custom-call(s32[2]{0:T(128)S(1)} %pad_add_fusion.1.refs_0_, bf16[7168,512]{1,0:T(8,128)(2,1)} %bitcast.32, bf16[7168,512]{1,0:T(8,128)(2,1)} %bitcast.36, bf16[256,1792]{1,0:T(8,128)(2,1)S(1)} %pad_maximum_fusion.1.refs_3_, ...), custom_call_target="tpu_custom_call", output_to_operand_aliasing={{0}: (5, {}), {1}: (6, {})} | custom-call | flops 1879048192 | bytes 3670016 | tf_op jit(solution)/shard_map/pallas_call | solution.py:142
  90.3 0.1 collective-permute-start.21
  90.4 0.1 pad_add_fusion.refs_0_
  90.5 4.5 %shard_map.97 = (f32[8,256]{1,0:T(8,128)S(1)}, bf16[1792,512]{1,0:T(8,128)(2,1)S(1)}, bf16[1792,512]{1,0:T(8,128)(2,1)S(1)}) custom-call(s32[2]{0:T(128)S(1)} %pad_add_fusion.refs_0_, bf16[7168,512]{1,0:T(8,128)(2,1)} %bitcast.33, bf16[7168,512]{1,0:T(8,128)(2,1)} %bitcast.37, bf16[256,1920]{1,0:T(8,128)(2,1)S(1)} %pad_maximum_fusion.refs_3_, ...), custom_call_target="tpu_custom_call" | custom-call | flops 939524096 | bytes 3670016 | tf_op jit(solution)/shard_map/pallas_call | solution.py:241
  95.0 2.6 %shard_map.98 = (f32[8,256]{1,0:T(8,128)S(1)}, f32[32,8,128]{2,1,0:T(8,128)}) custom-call(s32[2]{0:T(128)S(1)} %pad_add_fusion.refs_0_, bf16[256,1920]{1,0:T(8,128)(2,1)S(1)} %collective-permute-done.21.refs_1_, f32[512,512]{1,0:T(8,128)S(1)} %get-tuple-element.44.refs_4_.refs_2_, f32[512,512]{1,0:T(8,128)S(1)} %get-tuple-element.45.refs_5_.refs_3_, ...), custom_call_target="tpu_custom_call" | custom-call | flops 939524096 | bytes 3670016 | tf_op jit(solution)/shard_map/pallas_call | solution.py:255
  97.6 0.6 slice_reduce_fusion
  98.2 3.8 %all-to-all-start = ((f32[32,8,128]{2,1,0:T(8,128)}), f32[32,8,128]{2,1,0:T(8,128)S(1)}, u32[]{:S(2)}, u32[]{:S(2)}) async-start(f32[32,8,128]{2,1,0:T(8,128)} %get-tuple-element.49), calls=%async_computation | async-start | bytes 262144 | tf_op jit(solution)/shard_map/all_to_all | solution.py:347
  102.0 1.3 %multiply_reduce_fusion.1 = f32[1792]{0:T(1024)S(1)} fusion(f32[256]{0:T(256)S(1)} %bitcast.39, bf16[64,1792]{1,0:T(8,128)(2,1)} %copy-done.4, bf16[64,1792]{1,0:T(8,128)(2,1)S(1)} %collective-permute-done.6, bf16[64,1792]{1,0:T(8,128)(2,1)} %copy-done.1, bf16[64,1792]{1,0:T(8,128)(2,1)S(1)} %get-tuple-element.56), kind=kLoop, calls=%fused_computation.1 | loop fusion | flops 5044480 | bytes 925696 | tf_op jit(solution)/shard_map/reduce_sum | solution.py:352
  103.3 0.3 multiply_reduce_fusion
  104.9 0.6 div.18
  105.5 4.8 %all-to-all-done.refs_1_ = f32[32,8,128]{2,1,0:T(8,128)S(1)} async-done(((f32[32,8,128]{2,1,0:T(8,128)}), f32[32,8,128]{2,1,0:T(8,128)S(1)}, u32[]{:S(2)}, u32[]{:S(2)}) %all-to-all-start) | async-done | bytes 131104 | tf_op jit(solution)/shard_map/all_to_all | solution.py:347
  110.4 0.6 copy-done.7
  111.0 1.5 %shard_map.99 = (f32[1,64]{1,0:T(1,128)}, f32[1,1]{1,0:T(1,128)}) custom-call(s32[2]{0:T(128)} %copy-done, f32[32,8,128]{2,1,0:T(8,128)} %copy-done.7, s32[2,64]{1,0:T(2,128)} %bitcast.41, f32[2,64]{1,0:T(2,128)} %bitcast.42), custom_call_target="tpu_custom_call" | custom-call | tf_op jit(solution)/shard_map/pallas_call | solution.py:358
  (42 shorter events, 0.3 us)
Async XLA Ops:
  1.9 11.7 %collective-permute-start = (bf16[64,1792]{1,0:T(8,128)(2,1)S(1)}, bf16[64,1792]{1,0:T(8,128)(2,1)S(1)}, u32[]{:S(2)}, u32[]{:S(2)}) collective-permute-start(bf16[64,1792]{1,0:T(8,128)(2,1)S(1)} %get-tuple-element.57), channel_id=1, source_target_pairs={{0,3},{1,2},{2,1},{3,0},{4,7},{5,6},{6,5},{7,4},{8,11},{9,10},{10,... | collective-permute-start | bytes 688136 | tf_op jit(solution)/shard_map/ppermute | solution.py:283
  7.0 19.5 %collective-permute-start.1 = (bf16[64,1792]{1,0:T(8,128)(2,1)S(1)}, bf16[64,1792]{1,0:T(8,128)(2,1)S(1)}, u32[]{:S(2)}, u32[]{:S(2)}) collective-permute-start(bf16[64,1792]{1,0:T(8,128)(2,1)S(1)} %get-tuple-element.59), channel_id=1, source_target_pairs={{0,2},{1,3},{2,0},{3,1},{4,6},{5,7},{6,4},{7,5},{8,10},{9,11},{10,... | collective-permute-start | bytes 688136 | tf_op jit(solution)/shard_map/ppermute | solution.py:283
  7.0 19.5 %collective-permute-start.2 = (bf16[64,1792]{1,0:T(8,128)(2,1)S(1)}, bf16[64,1792]{1,0:T(8,128)(2,1)S(1)}, u32[]{:S(2)}, u32[]{:S(2)}) collective-permute-start(bf16[64,1792]{1,0:T(8,128)(2,1)S(1)} %get-tuple-element.58), channel_id=1, source_target_pairs={{0,1},{1,0},{2,3},{3,2},{4,5},{5,4},{6,7},{7,6},{8,9},{9,8},{10,11... | collective-permute-start | bytes 688136 | tf_op jit(solution)/shard_map/ppermute | solution.py:283
  27.8 6.7 %collective-permute-start.6 = (bf16[64,1792]{1,0:T(8,128)(2,1)S(1)}, bf16[64,1792]{1,0:T(8,128)(2,1)S(1)}, u32[]{:S(2)}, u32[]{:S(2)}) collective-permute-start(bf16[64,1792]{1,0:T(8,128)(2,1)S(1)} %get-tuple-element.56), channel_id=1, source_target_pairs={{0,16},{4,20},{8,24},{12,28},{16,0},{20,4},{24,8},{28,12},{1,17},{... | collective-permute-start | bytes 688136 | tf_op jit(solution)/shard_map/ppermute | solution.py:337
  29.4 6.4 %collective-permute-start.7 = (bf16[64,1792]{1,0:T(8,128)(2,1)S(1)}, bf16[64,1792]{1,0:T(8,128)(2,1)S(1)}, u32[]{:S(2)}, u32[]{:S(2)}) collective-permute-start(bf16[64,1792]{1,0:T(8,128)(2,1)S(1)} %get-tuple-element.56), channel_id=1, source_target_pairs={{0,8},{4,12},{8,0},{12,4},{16,24},{20,28},{24,16},{28,20},{1,9},{5... | collective-permute-start | bytes 688136 | tf_op jit(solution)/shard_map/ppermute | solution.py:336
  31.4 11.4 %collective-permute-start.5 = (bf16[64,1920]{1,0:T(8,128)(2,1)S(1)}, bf16[64,1920]{1,0:T(8,128)(2,1)S(1)}, u32[]{:S(2)}, u32[]{:S(2)}) collective-permute-start(bf16[64,1920]{1,0:T(8,128)(2,1)S(1)} %concatenate.24), channel_id=1, source_target_pairs={{0,1},{1,0},{2,3},{3,2},{4,5},{5,4},{6,7},{7,6},{8,9},{9,8},{10,11... | collective-permute-start | bytes 737288 | tf_op jit(solution)/shard_map/ppermute | solution.py:283
  31.4 15.6 %collective-permute-start.4 = (bf16[64,1920]{1,0:T(8,128)(2,1)S(1)}, bf16[64,1920]{1,0:T(8,128)(2,1)S(1)}, u32[]{:S(2)}, u32[]{:S(2)}) collective-permute-start(bf16[64,1920]{1,0:T(8,128)(2,1)S(1)} %concatenate.24), channel_id=1, source_target_pairs={{0,2},{1,3},{2,0},{3,1},{4,6},{5,7},{6,4},{7,5},{8,10},{9,11},{10,... | collective-permute-start | bytes 737288 | tf_op jit(solution)/shard_map/ppermute | solution.py:283
  35.8 18.3 %copy-start.1 = (bf16[64,1792]{1,0:T(8,128)(2,1)}, bf16[64,1792]{1,0:T(8,128)(2,1)S(1)}, u32[]{:S(2)}) copy-start(bf16[64,1792]{1,0:T(8,128)(2,1)S(1)} %collective-permute-done.7) | copy-start | bytes 688132
  42.8 6.5 %collective-permute-start.8 = (bf16[64,1792]{1,0:T(8,128)(2,1)S(1)}, bf16[64,1792]{1,0:T(8,128)(2,1)S(1)}, u32[]{:S(2)}, u32[]{:S(2)}) collective-permute-start(bf16[64,1792]{1,0:T(8,128)(2,1)S(1)} %slice.57), channel_id=1, source_target_pairs={{0,16},{4,20},{8,24},{12,28},{16,0},{20,4},{24,8},{28,12},{1,17},{... | collective-permute-start | bytes 688136 | tf_op jit(solution)/shard_map/ppermute | solution.py:337
  43.4 8.5 %collective-permute-start.9 = (bf16[64,1792]{1,0:T(8,128)(2,1)S(1)}, bf16[64,1792]{1,0:T(8,128)(2,1)S(1)}, u32[]{:S(2)}, u32[]{:S(2)}) collective-permute-start(bf16[64,1792]{1,0:T(8,128)(2,1)S(1)} %slice.57), channel_id=1, source_target_pairs={{0,8},{4,12},{8,0},{12,4},{16,24},{20,28},{24,16},{28,20},{1,9},{5... | collective-permute-start | bytes 688136 | tf_op jit(solution)/shard_map/ppermute | solution.py:336
  44.0 17.9 %collective-permute-start.3 = (bf16[64,1920]{1,0:T(8,128)(2,1)S(1)}, bf16[64,1920]{1,0:T(8,128)(2,1)S(1)}, u32[]{:S(2)}, u32[]{:S(2)}) collective-permute-start(bf16[64,1920]{1,0:T(8,128)(2,1)S(1)} %concatenate.24), channel_id=1, source_target_pairs={{0,3},{1,2},{2,1},{3,0},{4,7},{5,6},{6,5},{7,4},{8,11},{9,10},{10,... | collective-permute-start | bytes 737288 | tf_op jit(solution)/shard_map/ppermute | solution.py:283
  45.5 8.6 %collective-permute-start.17 = (bf16[64,1792]{1,0:T(8,128)(2,1)S(1)}, bf16[64,1792]{1,0:T(8,128)(2,1)S(1)}, u32[]{:S(2)}, u32[]{:S(2)}) collective-permute-start(bf16[64,1792]{1,0:T(8,128)(2,1)S(1)} %broadcast_select_fusion.3), channel_id=1, source_target_pairs={{0,16},{4,12},{8,24},{12,4},{16,0},{20,28},{24,8},{28,20},{1,17},{... | collective-permute-start | bytes 688136 | tf_op jit(solution)/shard_map/ppermute | solution.py:328
  52.0 11.0 %copy-start.3 = (bf16[64,1792]{1,0:T(8,128)(2,1)}, bf16[64,1792]{1,0:T(8,128)(2,1)S(1)}, u32[]{:S(2)}) copy-start(bf16[64,1792]{1,0:T(8,128)(2,1)S(1)} %slice.58) | copy-start | bytes 688132
  52.0 6.1 %collective-permute-start.10 = (bf16[64,1792]{1,0:T(8,128)(2,1)S(1)}, bf16[64,1792]{1,0:T(8,128)(2,1)S(1)}, u32[]{:S(2)}, u32[]{:S(2)}) collective-permute-start(bf16[64,1792]{1,0:T(8,128)(2,1)S(1)} %slice.58), channel_id=1, source_target_pairs={{0,16},{4,20},{8,24},{12,28},{16,0},{20,4},{24,8},{28,12},{1,17},{... | collective-permute-start | bytes 688136 | tf_op jit(solution)/shard_map/ppermute | solution.py:337
  53.6 7.6 %collective-permute-start.11 = (bf16[64,1792]{1,0:T(8,128)(2,1)S(1)}, bf16[64,1792]{1,0:T(8,128)(2,1)S(1)}, u32[]{:S(2)}, u32[]{:S(2)}) collective-permute-start(bf16[64,1792]{1,0:T(8,128)(2,1)S(1)} %slice.58), channel_id=1, source_target_pairs={{0,8},{4,12},{8,0},{12,4},{16,24},{20,28},{24,16},{28,20},{1,9},{5... | collective-permute-start | bytes 688136 | tf_op jit(solution)/shard_map/ppermute | solution.py:336
  54.1 0.7 copy-start.4
  54.9 8.1 %collective-permute-start.18 = (bf16[256,1792]{1,0:T(8,128)(2,1)S(1)}, bf16[256,1792]{1,0:T(8,128)(2,1)S(1)}, u32[]{:S(2)}, u32[]{:S(2)}) collective-permute-start(bf16[256,1792]{1,0:T(8,128)(2,1)S(1)} %pad_maximum_fusion.3.refs_3_), channel_id=1, source_target_pairs={{0,4},{4,0},{8,12},{12,8},{16,20},{20,16},{24,28},{28,24},{1,5},{5... | collective-permute-start | bytes 2752520 | tf_op jit(solution)/shard_map/ppermute | solution.py:332
  54.9 7.0 %collective-permute-start.16 = (bf16[64,1792]{1,0:T(8,128)(2,1)S(1)}, bf16[64,1792]{1,0:T(8,128)(2,1)S(1)}, u32[]{:S(2)}, u32[]{:S(2)}) collective-permute-start(bf16[64,1792]{1,0:T(8,128)(2,1)S(1)} %broadcast_select_fusion.2), channel_id=1, source_target_pairs={{0,16},{4,12},{8,24},{12,4},{16,0},{20,28},{24,8},{28,20},{1,17},{... | collective-permute-start | bytes 688136 | tf_op jit(solution)/shard_map/ppermute | solution.py:328
  58.1 4.9 %copy-start.5 = (bf16[64,1792]{1,0:T(8,128)(2,1)}, bf16[64,1792]{1,0:T(8,128)(2,1)S(1)}, u32[]{:S(2)}) copy-start(bf16[64,1792]{1,0:T(8,128)(2,1)S(1)} %collective-permute-done.10) | copy-start | bytes 688132
  61.1 1.8 %copy-start.6 = (bf16[64,1792]{1,0:T(8,128)(2,1)}, bf16[64,1792]{1,0:T(8,128)(2,1)S(1)}, u32[]{:S(2)}) copy-start(bf16[64,1792]{1,0:T(8,128)(2,1)S(1)} %collective-permute-done.11) | copy-start | bytes 688132
  61.9 10.7 %collective-permute-start.15 = (bf16[64,1792]{1,0:T(8,128)(2,1)}, bf16[64,1792]{1,0:T(8,128)(2,1)}, u32[]{:S(2)}, u32[]{:S(2)}) collective-permute-start(bf16[64,1792]{1,0:T(8,128)(2,1)} %broadcast_select_fusion.1), channel_id=1, source_target_pairs={{0,16},{4,12},{8,24},{12,4},{16,0},{20,28},{24,8},{28,20},{1,17},{... | collective-permute-start | bytes 688136 | tf_op jit(solution)/shard_map/ppermute | solution.py:328
  67.3 6.6 %collective-permute-start.19 = (bf16[256,1792]{1,0:T(8,128)(2,1)}, bf16[256,1792]{1,0:T(8,128)(2,1)}, u32[]{:S(2)}, u32[]{:S(2)}) collective-permute-start(bf16[256,1792]{1,0:T(8,128)(2,1)} %pad_maximum_fusion.2.refs_3_), channel_id=1, source_target_pairs={{0,4},{4,0},{8,12},{12,8},{16,20},{20,16},{24,28},{28,24},{1,5},{5... | collective-permute-start | bytes 2752520 | tf_op jit(solution)/shard_map/ppermute | solution.py:332
  70.5 9.0 %collective-permute-start.12 = (bf16[64,1920]{1,0:T(8,128)(2,1)}, bf16[64,1920]{1,0:T(8,128)(2,1)S(1)}, u32[]{:S(2)}, u32[]{:S(2)}) collective-permute-start(bf16[64,1920]{1,0:T(8,128)(2,1)} %concatenate.25), channel_id=1, source_target_pairs={{0,8},{4,12},{8,0},{12,4},{16,24},{20,28},{24,16},{28,20},{1,9},{5... | collective-permute-start | bytes 737288 | tf_op jit(solution)/shard_map/ppermute | solution.py:336
  71.2 8.3 %collective-permute-start.13 = (bf16[64,1920]{1,0:T(8,128)(2,1)}, bf16[64,1920]{1,0:T(8,128)(2,1)S(1)}, u32[]{:S(2)}, u32[]{:S(2)}) collective-permute-start(bf16[64,1920]{1,0:T(8,128)(2,1)} %concatenate.25), channel_id=1, source_target_pairs={{0,16},{4,20},{8,24},{12,28},{16,0},{20,4},{24,8},{28,12},{1,17},{... | collective-permute-start | bytes 737288 | tf_op jit(solution)/shard_map/ppermute | solution.py:337
  73.9 11.9 %copy-start.2 = (bf16[64,1920]{1,0:T(8,128)(2,1)S(1)}, bf16[64,1920]{1,0:T(8,128)(2,1)}, u32[]{:S(2)}) copy-start(bf16[64,1920]{1,0:T(8,128)(2,1)} %concatenate.25) | copy-start | bytes 737284
  79.3 6.7 %collective-permute-start.20 = (bf16[256,1792]{1,0:T(8,128)(2,1)S(1)}, bf16[256,1792]{1,0:T(8,128)(2,1)S(1)}, u32[]{:S(2)}, u32[]{:S(2)}) collective-permute-start(bf16[256,1792]{1,0:T(8,128)(2,1)S(1)} %pad_maximum_fusion.1.refs_3_), channel_id=1, source_target_pairs={{0,4},{4,0},{8,12},{12,8},{16,20},{20,16},{24,28},{28,24},{1,5},{5... | collective-permute-start | bytes 2752520 | tf_op jit(solution)/shard_map/ppermute | solution.py:332
  79.6 6.3 %collective-permute-start.14 = (bf16[64,1920]{1,0:T(8,128)(2,1)S(1)}, bf16[64,1920]{1,0:T(8,128)(2,1)S(1)}, u32[]{:S(2)}, u32[]{:S(2)}) collective-permute-start(bf16[64,1920]{1,0:T(8,128)(2,1)S(1)} %broadcast_select_fusion), channel_id=1, source_target_pairs={{0,16},{4,12},{8,24},{12,4},{16,0},{20,28},{24,8},{28,20},{1,17},{... | collective-permute-start | bytes 737288 | tf_op jit(solution)/shard_map/ppermute | solution.py:340
  90.3 4.7 %collective-permute-start.21 = (bf16[256,1920]{1,0:T(8,128)(2,1)S(1)}, bf16[256,1920]{1,0:T(8,128)(2,1)S(1)}, u32[]{:S(2)}, u32[]{:S(2)}) collective-permute-start(bf16[256,1920]{1,0:T(8,128)(2,1)S(1)} %pad_maximum_fusion.refs_3_), channel_id=1, source_target_pairs={{0,4},{4,0},{8,12},{12,8},{16,20},{20,16},{24,28},{28,24},{1,5},{5... | collective-permute-start | bytes 2949128 | tf_op jit(solution)/shard_map/ppermute | solution.py:345
  90.4 4.5 %copy-start = (s32[2]{0:T(128)}, s32[2]{0:T(128)S(1)}, u32[]{:S(2)}) copy-start(s32[2]{0:T(128)S(1)} %pad_add_fusion.refs_0_) | copy-start | bytes 28
  98.2 12.2 %all-to-all-start = ((f32[32,8,128]{2,1,0:T(8,128)}), f32[32,8,128]{2,1,0:T(8,128)S(1)}, u32[]{:S(2)}, u32[]{:S(2)}) async-start(f32[32,8,128]{2,1,0:T(8,128)} %get-tuple-element.49), calls=%async_computation | async-start | bytes 262144 | tf_op jit(solution)/shard_map/all_to_all | solution.py:347
  110.4 0.7 copy-start.7

commit v3 on v0

--- a/solution.py
+++ b/solution.py
@@ -1,17 +1,20 @@
 import jax
 import jax.numpy as jnp
 from jax import lax
+from jax.experimental import pallas as pl
+from jax.experimental.pallas import tpu as pltpu
 from jax.sharding import PartitionSpec as P
 
 D = 7168
 FF = 2048
 CAP = 24
+EXTRA = 128
 
 
 epsilon = 1e-06
 
 
-def per_device(residual, attn_parts, norm_gain, routes, route_weights, w_gate, w_gate_q):
+def general_device(residual, attn_parts, norm_gain, routes, route_weights, w_gate, w_gate_q):
     n_expert = lax.axis_size("expert")
     tok_count = residual.shape[0]
     local_cols = residual.shape[1]
@@ -38,8 +41,6 @@
     placing = (slot_ids[:, None] == target[None, :]).reshape(n_expert * CAP, tok_count, top_count)
     dispatch = jnp.sum(placing.astype(jnp.int32), axis=2).astype(jnp.bfloat16)
     count_send = load_counts.astype(jnp.bfloat16).reshape(n_expert, 1)
-    weight_full = w_gate[0]
-    weight_quant = w_gate_q[0]
     outgoing = jnp.dot(dispatch, normed, preferred_element_type=jnp.float32).astype(jnp.bfloat16)
     outgoing = outgoing.reshape(n_expert, CAP, local_cols)
     arrived, arrived_counts = (
@@ -48,8 +49,8 @@
     )
     own_block = arrived.reshape(n_expert * CAP, local_cols)
     column_block = lax.all_gather(own_block, "tensor", axis=1, tiled=True)
-    full_acc = jnp.dot(column_block, weight_full, preferred_element_type=jnp.float32)
-    quant_acc = jnp.dot(column_block, weight_quant, preferred_element_type=jnp.float32)
+    full_acc = jnp.dot(column_block, w_gate[0], preferred_element_type=jnp.float32)
+    quant_acc = jnp.dot(column_block, w_gate_q[0], preferred_element_type=jnp.float32)
     block_squares = jnp.einsum("rc,rc->c", own_block, own_block, preferred_element_type=jnp.float32)
     total_load = jnp.sum(arrived_counts.astype(jnp.float32))
     hess_local = 2.0 * block_squares / total_load
@@ -69,6 +70,363 @@
     return (token_error, expert_total.reshape(1), hess_local.reshape(1, local_cols))
 
 
+def in_vmem(x):
+    return pltpu.with_memory_space_constraint(x, pltpu.VMEM)
+
+
+def in_hbm(x):
+    return pltpu.with_memory_space_constraint(x, pltpu.HBM)
+
+
+VMEM_SPEC = pl.BlockSpec(memory_space=pltpu.VMEM)
+HBM_SPEC = pl.BlockSpec(memory_space=pl.ANY)
+SMEM_SPEC = pl.BlockSpec(memory_space=pltpu.SMEM)
+PARAMS = pltpu.CompilerParams(vmem_limit_bytes=24 * 1024 * 1024)
+
+
+def cost(rows, depth, cols):
+    return pl.CostEstimate(flops=4 * rows * depth * cols, bytes_accessed=4 * depth * cols, transcendentals=0)
+
+
+def start_slab(number, hbm_ref, slab_ref, sem):
+    depth = slab_ref.shape[0]
+    first = pl.multiple_of(number * depth, depth)
+    copy = pltpu.make_async_copy(hbm_ref.at[pl.ds(first, depth), :], slab_ref, sem)
+    copy.start()
+    return copy
+
+
+def load_kernel(numbers_ref, w_ref, wq_ref, slab_ref, slab_q_ref, sems):
+    copies = [
+        start_slab(numbers_ref[1], w_ref, slab_ref, sems.at[0]),
+        start_slab(numbers_ref[1], wq_ref, slab_q_ref, sems.at[1]),
+    ]
+    for copy in copies:
+        copy.wait()
+
+
+def load_product(numbers, w, wq, depth):
+    return pl.pallas_call(
+        load_kernel,
+        in_specs=[SMEM_SPEC, HBM_SPEC, HBM_SPEC],
+        out_specs=[VMEM_SPEC] * 2,
+        out_shape=[pltpu.VMEM((depth, w.shape[1]), w.dtype)] * 2,
+        scratch_shapes=[pltpu.SemaphoreType.DMA((2,))],
+        compiler_params=PARAMS,
+        cost_estimate=cost(0, depth, w.shape[1]),
+    )(numbers, in_hbm(w), in_hbm(wq))
+
+
+def first_product(rows, slabs):
+    count = rows.shape[0]
+    depth, cols = slabs[0].shape
+
+    def kernel(rows_ref, slab_ref, slab_q_ref, full_ref, quant_ref, tail_ref):
+        half = count // 2
+        for part in range(2):
+            here = slice(part * half, (part + 1) * half)
+            x = rows_ref[here, :depth]
+            full_ref[here, :] = jnp.dot(x, slab_ref[...], preferred_element_type=jnp.float32)
+            quant_ref[here, :] = jnp.dot(x, slab_q_ref[...], preferred_element_type=jnp.float32)
+        tail_ref[...] = rows_ref[:, depth:].astype(jnp.float32)
+
+    return pl.pallas_call(
+        kernel,
+        in_specs=[VMEM_SPEC] * 3,
+        out_specs=[VMEM_SPEC] * 3,
+        out_shape=[pltpu.VMEM((count, cols), jnp.float32)] * 2 + [pltpu.VMEM((count, EXTRA), jnp.float32)],
+        compiler_params=PARAMS,
+        cost_estimate=cost(count, depth, cols),
+    )(*[in_vmem(x) for x in (rows, *slabs)])
+
+
+def fetching(numbers_ref, hbm_refs, slabs, sems, first):
+    copies = []
+    for n, slab in enumerate(slabs):
+        copies.append(start_slab(numbers_ref[first + n // 2], hbm_refs[n % 2], slab, sems.at[n]))
+    return copies
+
+
+def add_product(numbers, w, wq, rows, depth, sums):
+    count = rows[0].shape[0]
+    cols = w.shape[1]
+    quarters = len(rows)
+
+    def kernel(numbers_ref, w_ref, wq_ref, *refs):
+        row_refs, ins, outs = refs[:quarters], refs[quarters : quarters + 3], refs[quarters + 3 : quarters + 6]
+        slabs, sems = refs[quarters + 6 : -1], refs[-1]
+        copies = fetching(numbers_ref, (w_ref, wq_ref), slabs, sems, 2)
+        half = count // 2
+        for q in range(quarters):
+            for i in range(2):
+                copies[2 * q + i].wait()
+                before = outs[i] if q else ins[i]
+                for part in range(2):
+                    here = slice(part * half, (part + 1) * half)
+                    outs[i][here, :] = before[here, :] + jnp.dot(
+                        row_refs[q][here, :depth], slabs[2 * q + i][...], preferred_element_type=jnp.float32
+                    )
+        tail = ins[2][:count, :]
+        for ref in row_refs:
+            tail = tail + ref[:, depth:].astype(jnp.float32)
+        outs[2][...] = tail
+
+    return pl.pallas_call(
+        kernel,
+        in_specs=[SMEM_SPEC, HBM_SPEC, HBM_SPEC] + [VMEM_SPEC] * (quarters + 3),
+        out_specs=[VMEM_SPEC] * 3,
+        out_shape=[pltpu.VMEM((count, cols), jnp.float32)] * 2 + [pltpu.VMEM((count, EXTRA), jnp.float32)],
+        scratch_shapes=[pltpu.VMEM((depth, cols), w.dtype)] * (2 * quarters)
+        + [pltpu.SemaphoreType.DMA((2 * quarters,))],
+        compiler_params=PARAMS,
+        cost_estimate=cost(count * quarters, depth, cols),
+    )(numbers, in_hbm(w), in_hbm(wq), *[in_vmem(x) for x in (*rows, *sums)])
+
+
+def row_stats(expert, full, quant, total, extra):
+    count = full.shape[0]
+    diff = full - quant
+    err = jnp.sum(diff * diff, axis=1, keepdims=True)
+    power = jnp.sum(full * full, axis=1, keepdims=True)
+    lane = lax.broadcasted_iota(jnp.int32, (count, EXTRA), 1)
+    squares = total[:, 0:1] + total[:, 1:2] + total[:, 2:3]
+    scale = lax.rsqrt(squares / D + epsilon)
+    scale = scale * scale
+    named = (lane >= 3) & (extra == expert.astype(jnp.float32))
+    routed = jnp.sum(jnp.where(named, 1.0, 0.0), axis=1, keepdims=True)
+    stats = jnp.where(lane == 0, err * (scale / FF), 0.0)
+    stats = jnp.where(lane == 1, power * (scale / FF), stats)
+    stats = jnp.where(lane == 2, routed, stats)
+    stats = jnp.where(lane == 3, scale * routed, stats)
+    return stats.T[:8, :]
+
+
+def early_stats(numbers, w, wq, rows, depth, sums, n_z):
+    count = rows.shape[0]
+    cols = w.shape[1]
+    kept = 2 * (n_z - 1)
+
+    def kernel(numbers_ref, w_ref, wq_ref, rows_ref, full_ref, quant_ref, tail_ref, stats_ref, *refs):
+        slabs, sems = refs[:kept], refs[kept]
+        last = fetching(numbers_ref, (w_ref, wq_ref), slabs[kept - 2 :], sems.at[pl.ds(kept - 2, 2)], n_z)
+        others = fetching(numbers_ref, (w_ref, wq_ref), slabs[: kept - 2], sems, 2)
+        x = rows_ref[:, :depth]
+        made = []
+        for i, before in enumerate((full_ref, quant_ref)):
+            last[i].wait()
+            made.append(before[...] + jnp.dot(x, slabs[kept - 2 + i][...], preferred_element_type=jnp.float32))
+        extra = rows_ref[:, depth:].astype(jnp.float32)
+        stats_ref[...] = row_stats(numbers_ref[0], *made, tail_ref[...] + extra, extra)
+        for copy in others:
+            copy.wait()
+
+    out = pl.pallas_call(
+        kernel,
+        in_specs=[SMEM_SPEC, HBM_SPEC, HBM_SPEC] + [VMEM_SPEC] * 4,
+        out_specs=[VMEM_SPEC] * (1 + kept),
+        out_shape=[pltpu.VMEM((8, count), jnp.float32)] + [pltpu.VMEM((depth, cols), w.dtype)] * kept,
+        scratch_shapes=[pltpu.SemaphoreType.DMA((kept,))],
+        compiler_params=PARAMS,
+        cost_estimate=cost(count, depth, cols),
+    )(numbers, in_hbm(w), in_hbm(wq), *[in_vmem(x) for x in (rows, *sums)])
+    return out[0], out[1:]
+
+
+def late_stats(numbers, rows, slabs, sums, early, tok, n_z):
+    quarters = len(rows)
+    count = rows[0].shape[0]
+    depth, cols = slabs[0].shape
+
+    def kernel(numbers_ref, *refs):
+        row_refs, slab_refs = refs[:quarters], refs[quarters : 3 * quarters]
+        full_ref, quant_ref, tail_ref, early_ref, stats_ref, out_ref = refs[3 * quarters :]
+        expert = numbers_ref[0]
+        core = expert % 2
+        before = early_ref[...]
+        here = slice(before.shape[1], before.shape[1] + count)
+        total = tail_ref[here, :]
+        made = [full_ref[here, :], quant_ref[here, :]]
+        for q, ref in enumerate(row_refs):
+            extra = ref[:, depth:].astype(jnp.float32)
+            total = total + extra
+            for i in range(2):
+                made[i] = made[i] + jnp.dot(
+                    ref[:, :depth], slab_refs[2 * q + i][...], preferred_element_type=jnp.float32
+                )
+        stats = row_stats(expert, *made, total, extra)
+        stats_ref[...] = stats
+        sums_early = jnp.sum(before * before[2:3, :], axis=1, keepdims=True)
+        sums_here = sums_early + jnp.sum(stats * stats[2:3, :], axis=1, keepdims=True)
+        lane = lax.broadcasted_iota(jnp.int32, (8, 2 * tok), 1)
+        order = ((0, 0), (1, 1), (2, 4), (3, 5), (5, 3), (4, 2), (6, 6), (7, 7))
+        for pair in range(4):
+            both = stats if pair == 3 else before[:, pair * 2 * tok : (pair + 1) * 2 * tok]
+            for odd in range(2):
+                zero, one = order[2 * pair + odd]
+                owner = expert ^ (zero + core * (one - zero))
+                block = jnp.where(lane < tok, pltpu.roll(both, tok, 1) if odd else both, sums_here)
+                for z in range(n_z):
+                    out_ref[owner * n_z + z] = block
+
+    return pl.pallas_call(
+        kernel,
+        in_specs=[SMEM_SPEC] + [VMEM_SPEC] * (3 * quarters + 4),
+        out_specs=[VMEM_SPEC] * 2,
+        out_shape=[
+            pltpu.VMEM((8, count), jnp.float32),
+            jax.ShapeDtypeStruct((8 * n_z, 8, 2 * tok), jnp.float32),
+        ],
+        compiler_params=PARAMS,
+        cost_estimate=cost(count, depth, cols),
+    )(numbers, *[in_vmem(x) for x in (*rows, *slabs, *sums, early)])
+
+
+def hessian(rows, early, late, width):
+    def kernel(rows_ref, early_ref, late_ref, out_ref):
+        split = early_ref.shape[1]
+        total = jnp.sum(early_ref[2:3, :], axis=1, keepdims=True) + jnp.sum(
+            late_ref[2:3, :], axis=1, keepdims=True
+        )
+        weight_early = early_ref[...].T[:, 3:4]
+        weight_late = late_ref[...].T[:, 3:4]
+        step = 256
+        for first in range(0, width, step):
+            columns = slice(first, first + step)
+            x = rows_ref[:split, columns].astype(jnp.float32)
+            y = rows_ref[split:, columns].astype(jnp.float32)
+            value = jnp.sum(x * x * weight_early, axis=0, keepdims=True)
+            value = value + jnp.sum(y * y * weight_late, axis=0, keepdims=True)
+            out_ref[:, columns] = 2.0 * value / total
+
+    return pl.pallas_call(
+        kernel,
+        in_specs=[VMEM_SPEC] * 3,
+        out_specs=VMEM_SPEC,
+        out_shape=jax.ShapeDtypeStruct((1, width), jnp.float32),
+        compiler_params=PARAMS,
+        cost_estimate=pl.CostEstimate(flops=4 * rows.size, bytes_accessed=2 * rows.size, transcendentals=0),
+    )(rows, in_vmem(early), in_vmem(late))
+
+
+def finish(numbers, back, routes, weights, n_z):
+    top, tok = routes.shape
+
+    def kernel(numbers_ref, back_ref, routes_ref, weights_ref, token_ref, expert_ref):
+        own = jnp.zeros((8, 2 * tok), jnp.float32)
+        err = [jnp.zeros((1, tok), jnp.float32)] * top
+        power = [jnp.zeros((1, tok), jnp.float32)] * top
+        for i in range(back_ref.shape[0] // n_z):
+            tile = back_ref[i * n_z]
+            for z in range(1, n_z):
+                tile = tile + back_ref[i * n_z + z]
+            own = jnp.where(numbers_ref[0] == i, tile, own)
+            for k in range(top):
+                here = routes_ref[k : k + 1, :] == i
+                err[k] = jnp.where(here, tile[0:1, :tok], err[k])
+                power[k] = jnp.where(here, tile[1:2, :tok], power[k])
+        total = jnp.zeros((1, tok), jnp.float32)
+        for k in range(top):
+            total = total + weights_ref[k : k + 1, :] * (err[k] / (power[k] + epsilon))
+        token_ref[...] = total
+        expert_ref[...] = own[0:1, tok : tok + 1] / (own[1:2, tok : tok + 1] + epsilon)
+
+    return pl.pallas_call(
+        kernel,
+        in_specs=[SMEM_SPEC] + [VMEM_SPEC] * 3,
+        out_specs=[VMEM_SPEC] * 2,
+        out_shape=[jax.ShapeDtypeStruct((1, tok), jnp.float32), jax.ShapeDtypeStruct((1, 1), jnp.float32)],
+    )(numbers, back, in_vmem(routes), in_vmem(weights))
+
+
+def in_pieces(squares):
+    high = lax.reduce_precision(squares, 8, 7)
+    mid = lax.reduce_precision(squares - high, 8, 7)
+    return [high, mid, squares - high - mid]
+
+
+def line_device(residual, attn_parts, norm_gain, routes, route_weights, w_gate, w_gate_q):
+    z = lax.axis_index("tensor")
+    e = lax.axis_index("expert")
+    n_z = 4
+    tok = residual.shape[0]
+    width = residual.shape[1]
+
+    def over_z(x, k):
+        return lax.ppermute(x, "tensor", [(i, i ^ k) for i in range(n_z)])
+
+    def in_plane(x, zero, one):
+        return lax.ppermute(x, "expert", [(i, i ^ (one if i & 1 else zero)) for i in range(8)])
+
+    def quarter(k):
+        return lax.dynamic_slice(attn_parts[0], (0, (z ^ k) * width), (tok, width))
+
+    numbers = jnp.stack([e, z, z ^ 1, z ^ 2, z ^ 3]).astype(jnp.int32)
+    w, wq = w_gate[0], w_gate_q[0]
+
+    arrived = [over_z(quarter(k), k) for k in (3, 2, 1)]
+    slabs = load_product(numbers, w, wq, width)
+    residual, *slabs = lax.optimization_barrier((residual, *slabs))
+    hidden = residual.astype(jnp.float32) + quarter(0).astype(jnp.float32)
+    for part in arrived:
+        hidden = hidden + part.astype(jnp.float32)
+    squares = jnp.sum(hidden * hidden, axis=1, keepdims=True)
+    own = (hidden * norm_gain.astype(jnp.float32)[None, :]).astype(jnp.bfloat16)
+    extra = jnp.concatenate(
+        in_pieces(squares)
+        + [routes.astype(jnp.float32)]
+        + [jnp.full((tok, EXTRA - 3 - routes.shape[1]), -1.0, jnp.float32)],
+        axis=1,
+    ).astype(jnp.bfloat16)
+    own = jnp.concatenate([own, extra], axis=1)
+    z_near, z_far = over_z(own, 1), over_z(own, 2)
+    z_both = over_z(z_far, 1)
+
+    def other_core(rows):
+        return in_plane(rows, 1, 1)
+
+    def next_chip(rows):
+        return in_plane(rows, 2, 4)
+
+    def opposite(rows):
+        return in_plane(rows, 4, 2)
+
+    def tied(x, *values):
+        return lax.optimization_barrier((x, *values))[0]
+
+    def most(near, beside):
+        return (*near, *beside, *map(other_core, beside))
+
+    near = own, other_core(own)
+    beside = next_chip(near[0]), next_chip(near[1])
+    across = opposite(beside[0])
+    rows = jnp.concatenate([*most(near, beside), across, other_core(across)], axis=0)
+    first_sums = first_product(rows, slabs)
+
+    def of_quarters(parts):
+        return [jnp.concatenate([x[q * tok : (q + 1) * tok] for x in parts], axis=0) for q in range(2)]
+
+    pair = tied(jnp.concatenate([z_near, z_far], axis=0), *beside)
+    near = pair, other_core(pair)
+    beside = next_chip(near[0]), next_chip(near[1])
+    across = opposite(tied(*beside, *first_sums))
+    gathered = most(near, beside)
+    sums = add_product(numbers, w, wq, of_quarters(gathered), width, first_sums)
+    last = of_quarters((across, other_core(across)))
+
+    single = tied(z_both, beside[1])
+    near = single, tied(other_core(single), gathered[4], gathered[5])
+    beside = next_chip(near[0]), next_chip(near[1])
+    across = opposite(tied(*beside, *sums))
+    early, slabs = early_stats(numbers, w, wq, jnp.concatenate(most(near, beside), axis=0), width, sums, n_z)
+    last.append(jnp.concatenate([across, other_core(tied(across, early))], axis=0))
+    late, payload = late_stats(numbers, last, slabs, first_sums, early, tok, n_z)
+
+    back = lax.all_to_all(payload, ("expert", "tensor"), split_axis=0, concat_axis=0, tiled=True)
+    hess = hessian(rows, early, late, width)
+    token_error, expert_total = finish(numbers, back, routes.T, route_weights.T, n_z)
+    return (token_error.reshape(tok), expert_total.reshape(1), hess.reshape(1, width))
+
+
 def solution(mesh):
     placed = (
         P("expert", "tensor"),
@@ -79,8 +437,9 @@
         P("expert", None, "tensor"),
         P("expert", None, "tensor"),
     )
+    on_line = mesh.shape["expert"] == 8 and mesh.shape["tensor"] == 4
     return jax.shard_map(
-        per_device,
+        line_device if on_line else general_device,
         mesh=mesh,
         in_specs=placed,
         out_specs=(P("expert"), P("expert"), P("expert", "tensor")),

time: 171 us -> 102 us (0.60)
  waiting for transfers between devices: 81.1 us -> 45.7 us
  blocking collectives: 34.7 us -> 0 us
  Pallas kernels: 0 us -> 20.9 us
  between operations: 16.7 us -> 0.98 us
  starting transfers between devices: 10.6 us -> 25.3 us
  matrix products: 12 us -> 0 us
  other arithmetic: 9.16 us -> 2.76 us
    all_gather x1 -> x0, waiting for transfers between devices: 44.4 us -> none  [per_device(): column_block = lax.all_gather(own_block, 'tensor', axis=1, tiled=True)]
    ppermute x0 -> x27, waiting for transfers between devices: none -> 38.5 us  [the longest x21 19.5 us: in_plane(): lax.ppermute(x, 'expert', [(i, i ^ (one if i & 1 else zero)) for i in ran...]
    reduce_scatter x1 -> x0, waiting for transfers between devices: 27.1 us -> none  [per_device(): lax.psum_scatter(attn_parts[0].astype(jnp.float32).astype(jnp.bfloat16),...]
    ppermute x0 -> x27, starting transfers between devices: none -> 21.9 us  [the longest x21 13.1 us: in_plane(): lax.ppermute(x, 'expert', [(i, i ^ (one if i & 1 else zero)) for i in ran...]
    pallas_call x0 -> x7, Pallas kernels: none -> 20.9 us  [the longest x1 5.56 us: add_product(): pl.pallas_call(kernel, in_specs=[SMEM_SPEC, HBM_SPEC, HBM_SPEC] + [VMEM_S...]
    psum x2 -> x0, blocking collectives: 19.6 us -> none  [the longest x1 9.92 us: per_device(): err_slots, pow_slots = lax.psum((err_part, pow_part), 'tensor')]
    all_to_all x1 -> x0, blocking collectives: 15.1 us -> none  [per_device(): lax.all_to_all(outgoing, 'expert', split_axis=0, concat_axis=0, tiled=True)]
    dot_general x3 -> x0, matrix products: 12 us -> none  [the longest x1 5.75 us: per_device(): jnp.dot(column_block, weight_full, preferred_element_type=jnp.float32)]
  transfers between devices with their start and end apart: 5 -> 28, of which waited for: 4 -> 13; matrix products, arithmetic and copies ran while one was open for 6% -> 2% of each run, Pallas kernels for 0% -> 16%
where the time goes in v3:
time: 102 us; the launch traced here: 101 us
  waiting for transfers between devices  45.7 us (45%)
  starting transfers between devices  25.3 us (25%)
  Pallas kernels  20.9 us (20%)
  local copies, waits for them, and re-layouts  5.69 us (6%)
  other arithmetic  2.76 us (3%)
    ppermute x21, waiting for transfers between devices, in_plane(): lax.ppermute(x, 'expert', [(i, i ^ (one if i & 1 else zero)) for i in ran...  19.5 us
    ppermute x6, waiting for transfers between devices, over_z(): return lax.ppermute(x, 'tensor', [(i, i ^ k) for i in range(n_z)])  19 us
    ppermute x21, starting transfers between devices, in_plane(): lax.ppermute(x, 'expert', [(i, i ^ (one if i & 1 else zero)) for i in ran...  13.1 us
    ppermute x6, starting transfers between devices, over_z(): return lax.ppermute(x, 'tensor', [(i, i ^ k) for i in range(n_z)])  8.8 us
    all_to_all x1, waiting for transfers between devices, line_device(): lax.all_to_all(payload, ('expert', 'tensor'), split_axis=0, concat_axis=0...  7.18 us
    pallas_call x1, Pallas kernels, add_product(): pl.pallas_call(kernel, in_specs=[SMEM_SPEC, HBM_SPEC, HBM_SPEC] + [VMEM_S...  5.56 us
    pallas_call x1, Pallas kernels, early_stats(): pl.pallas_call(kernel, in_specs=[SMEM_SPEC, HBM_SPEC, HBM_SPEC] + [VMEM_S...  4.8 us
    unnamed x35, local copies, waits for them, and re-layouts  3.69 us
  transfers between devices with their start and end apart: 28, of which 13 were waited for; matrix products, arithmetic and copies ran while one was open for 2% of the time, Pallas kernels for 16%

profile of v3, /device:TPU:0, one launch (start us, length us, event | category | flops | bytes accessed | tf_op | source)
XLA Modules:
  0.0 101.3 jit_solution(5057565819830921222)
XLA Ops:
  0.7 1.2 %dynamic-slice_bitcast_fusion.2 = (bf16[64,1792]{1,0:T(8,128)(2,1)S(1)}, bf16[64,1792]{1,0:T(8,128)(2,1)S(1)}, bf16[64,1792]{1,0:T(8,128)(2,1)S(1)}) fusion(bf16[1,64,7168]{2,1,0:T(8,128)(2,1)} %param.8, s32[]{:T(128)S(6)} %select_n.13, s32[]{:T(128)S(6)} %select_n.15, s32[]{:T(128)S(6)} %select_n.14), kind=kLoop, calls=%fused_computation.24 | loop fusion | bytes 1376268 | tf_op jit(solution)/shard_map/dynamic_slice | solution.py:361
  1.9 5.1 %collective-permute-start = (bf16[64,1792]{1,0:T(8,128)(2,1)S(1)}, bf16[64,1792]{1,0:T(8,128)(2,1)S(1)}, u32[]{:S(2)}, u32[]{:S(2)}) collective-permute-start(bf16[64,1792]{1,0:T(8,128)(2,1)S(1)} %get-tuple-element.61), channel_id=1, source_target_pairs={{0,3},{1,2},{2,1},{3,0},{4,7},{5,6},{6,5},{7,4},{8,11},{9,10},{10,... | collective-permute-start | bytes 688136 | tf_op jit(solution)/shard_map/ppermute | solution.py:355
  7.0 0.0 collective-permute-start.2
  7.0 0.6 collective-permute-start.1
  7.6 0.7 convert_element_type.34
  8.3 0.7 convert_convert_fusion
  9.0 0.1 copy.16
  9.1 0.1 stack.23.numbers_ref
  9.2 2.6 %shard_map.94 = (bf16[1792,512]{1,0:T(8,128)(2,1)S(1)}, bf16[1792,512]{1,0:T(8,128)(2,1)S(1)}) custom-call(s32[5]{0:T(128)S(1)} %stack.23.numbers_ref, bf16[7168,512]{1,0:T(8,128)(2,1)} %bitcast.30, bf16[7168,512]{1,0:T(8,128)(2,1)} %bitcast.33), custom_call_target="tpu_custom_call" | custom-call | bytes 3670016 | tf_op jit(solution)/shard_map/pallas_call | solution.py:109
  11.8 1.3 %copy-done.3 = bf16[1792,512]{1,0:T(8,128)(2,1)} copy-done((bf16[1792,512]{1,0:T(8,128)(2,1)}, bf16[1792,512]{1,0:T(8,128)(2,1)S(1)}, u32[]{:S(2)}) %copy-start.3) | copy-done | bytes 1835032
  13.1 1.2 %copy-done.5 = bf16[1792,512]{1,0:T(8,128)(2,1)} copy-done((bf16[1792,512]{1,0:T(8,128)(2,1)}, bf16[1792,512]{1,0:T(8,128)(2,1)S(1)}, u32[]{:S(2)}) %copy-start.5) | copy-done | bytes 1835032
  14.3 0.0 collective-permute-done
  14.3 4.3 %collective-permute-done.2 = bf16[64,1792]{1,0:T(8,128)(2,1)S(1)} collective-permute-done((bf16[64,1792]{1,0:T(8,128)(2,1)S(1)}, bf16[64,1792]{1,0:T(8,128)(2,1)S(1)}, u32[]{:S(2)}, u32[]{:S(2)}) %collective-permute-start.2) | collective-permute-done | bytes 229408 | tf_op jit(solution)/shard_map/ppermute | solution.py:355
  18.6 7.9 %collective-permute-done.1 = bf16[64,1792]{1,0:T(8,128)(2,1)S(1)} collective-permute-done((bf16[64,1792]{1,0:T(8,128)(2,1)S(1)}, bf16[64,1792]{1,0:T(8,128)(2,1)S(1)}, u32[]{:S(2)}, u32[]{:S(2)}) %collective-permute-start.1) | collective-permute-done | bytes 229408 | tf_op jit(solution)/shard_map/ppermute | solution.py:355
  26.5 1.2 %multiply_reduce_fusion = (f32[64]{0:T(128)S(1)}, bf16[64,1792]{1,0:T(8,128)(2,1)S(1)}) fusion(bf16[64,1792]{1,0:T(8,128)(2,1)S(1)} %collective-permute-done.2, bf16[64,1792]{1,0:T(8,128)(2,1)S(1)} %collective-permute-done.1, bf16[64,1792]{1,0:T(8,128)(2,1)S(1)} %collective-permute-done, bf16[1,64,7168]{2,1,0:T(8,128)(2,1)} %param.8, s32[]{:T(128)S(6)} %select_n.12, ...), kind=kLoop, calls=%fused_computation.8 | loop fusion | flops 1490880 | bytes 1383684 | tf_op jit(solution)/shard_map/reduce_sum | solution.py:372
  27.7 0.1 copy.15
  27.8 0.1 copy.14
  27.9 0.1 copy.13
  28.1 0.1 concatenate.30
  28.2 1.6 %collective-permute-start.5 = (bf16[64,1920]{1,0:T(8,128)(2,1)S(1)}, bf16[64,1920]{1,0:T(8,128)(2,1)S(1)}, u32[]{:S(2)}, u32[]{:S(2)}) collective-permute-start(bf16[64,1920]{1,0:T(8,128)(2,1)S(1)} %concatenate.30), channel_id=1, source_target_pairs={{0,8},{4,20},{8,0},{12,28},{16,24},{20,4},{24,16},{28,12},{1,9},{5... | collective-permute-start | bytes 737288 | tf_op jit(solution)/shard_map/ppermute | solution.py:358
  29.8 3.0 %collective-permute-start.3 = (bf16[64,1920]{1,0:T(8,128)(2,1)S(1)}, bf16[64,1920]{1,0:T(8,128)(2,1)S(1)}, u32[]{:S(2)}, u32[]{:S(2)}) collective-permute-start(bf16[64,1920]{1,0:T(8,128)(2,1)S(1)} %concatenate.30), channel_id=1, source_target_pairs={{0,1},{1,0},{2,3},{3,2},{4,5},{5,4},{6,7},{7,6},{8,9},{9,8},{10,11... | collective-permute-start | bytes 737288 | tf_op jit(solution)/shard_map/ppermute | solution.py:355
  32.8 1.6 %collective-permute-done.5 = bf16[64,1920]{1,0:T(8,128)(2,1)S(1)} collective-permute-done((bf16[64,1920]{1,0:T(8,128)(2,1)S(1)}, bf16[64,1920]{1,0:T(8,128)(2,1)S(1)}, u32[]{:S(2)}, u32[]{:S(2)}) %collective-permute-start.5) | collective-permute-done | bytes 245792 | tf_op jit(solution)/shard_map/ppermute | solution.py:358
  34.5 1.5 %collective-permute-start.13 = (bf16[64,1920]{1,0:T(8,128)(2,1)S(1)}, bf16[64,1920]{1,0:T(8,128)(2,1)S(1)}, u32[]{:S(2)}, u32[]{:S(2)}) collective-permute-start(bf16[64,1920]{1,0:T(8,128)(2,1)S(1)} %collective-permute-done.5), channel_id=1, source_target_pairs={{0,16},{4,12},{8,24},{12,4},{16,0},{20,28},{24,8},{28,20},{1,17},{... | collective-permute-start | bytes 737288 | tf_op jit(solution)/shard_map/ppermute | solution.py:358
  36.0 0.0 collective-permute-start.11
  36.0 0.0 collective-permute-done.6
  36.0 1.5 %collective-permute-start.7 = (bf16[64,1920]{1,0:T(8,128)(2,1)S(1)}, bf16[64,1920]{1,0:T(8,128)(2,1)S(1)}, u32[]{:S(2)}, u32[]{:S(2)}) collective-permute-start(bf16[64,1920]{1,0:T(8,128)(2,1)S(1)} %collective-permute-done.6), channel_id=1, source_target_pairs={{0,8},{4,20},{8,0},{12,28},{16,24},{20,4},{24,16},{28,12},{1,9},{5... | collective-permute-start | bytes 737288 | tf_op jit(solution)/shard_map/ppermute | solution.py:358
  37.5 6.7 %collective-permute-done.4 = bf16[64,1920]{1,0:T(8,128)(2,1)S(1)} collective-permute-done((bf16[64,1920]{1,0:T(8,128)(2,1)S(1)}, bf16[64,1920]{1,0:T(8,128)(2,1)S(1)}, u32[]{:S(2)}, u32[]{:S(2)}) %collective-permute-start.4) | collective-permute-done | bytes 245792 | tf_op jit(solution)/shard_map/ppermute | solution.py:355
  44.2 0.0 collective-permute-start.17
  44.3 0.1 collective-permute-done.3
  44.4 0.0 collective-permute-done.7
  44.4 0.1 collective-permute-start.9
  44.6 0.6 collective-permute-start.12
  45.2 0.6 collective-permute-start.8
  45.8 0.0 collective-permute-done.11
  45.8 0.7 collective-permute-start.14
  46.5 0.2 collective-permute-done.12
  46.8 0.9 collective-permute-done.14
  47.7 2.1 %shard_map.95 = (f32[512,512]{1,0:T(8,128)S(1)}, f32[512,512]{1,0:T(8,128)S(1)}, f32[512,128]{1,0:T(8,128)S(1)}) custom-call(bf16[512,1920]{1,0:T(8,128)(2,1)S(1)} %constant_dynamic-update-slice_fusion.rows_ref, bf16[1792,512]{1,0:T(8,128)(2,1)S(1)} %copy-done.4, bf16[1792,512]{1,0:T(8,128)(2,1)S(1)} %copy-done.6), custom_call_target="tpu_custom_call" | custom-call | flops 1879048192 | bytes 3670016 | tf_op jit(solution)/shard_map/pallas_call | solution.py:133
  49.7 1.2 %collective-permute-start.10 = (bf16[128,1920]{1,0:T(8,128)(2,1)S(1)}, bf16[128,1920]{1,0:T(8,128)(2,1)S(1)}, u32[]{:S(2)}, u32[]{:S(2)}) collective-permute-start(bf16[128,1920]{1,0:T(8,128)(2,1)S(1)} %collective-permute-done.9), channel_id=1, source_target_pairs={{0,8},{4,20},{8,0},{12,28},{16,24},{20,4},{24,16},{28,12},{1,9},{5... | collective-permute-start | bytes 1474568 | tf_op jit(solution)/shard_map/ppermute | solution.py:358
  51.0 3.1 %collective-permute-done.8 = bf16[128,1920]{1,0:T(8,128)(2,1)S(1)} collective-permute-done((bf16[128,1920]{1,0:T(8,128)(2,1)S(1)}, bf16[128,1920]{1,0:T(8,128)(2,1)S(1)}, u32[]{:S(2)}, u32[]{:S(2)}) %collective-permute-start.8) | collective-permute-done | bytes 491552 | tf_op jit(solution)/shard_map/ppermute | solution.py:358
  54.1 0.0 collective-permute-start.20
  54.2 0.0 collective-permute-done.17
  54.2 5.1 %collective-permute-done.10 = bf16[128,1920]{1,0:T(8,128)(2,1)S(1)} collective-permute-done((bf16[128,1920]{1,0:T(8,128)(2,1)S(1)}, bf16[128,1920]{1,0:T(8,128)(2,1)S(1)}, u32[]{:S(2)}, u32[]{:S(2)}) %collective-permute-start.10) | collective-permute-done | bytes 491552 | tf_op jit(solution)/shard_map/ppermute | solution.py:358
  59.3 0.5 collective-permute-start.18
  59.9 1.5 %collective-permute-start.15 = (bf16[128,1920]{1,0:T(8,128)(2,1)S(1)}, bf16[128,1920]{1,0:T(8,128)(2,1)S(1)}, u32[]{:S(2)}, u32[]{:S(2)}) collective-permute-start(bf16[128,1920]{1,0:T(8,128)(2,1)S(1)} %collective-permute-done.8), channel_id=1, source_target_pairs={{0,16},{4,12},{8,24},{12,4},{16,0},{20,28},{24,8},{28,20},{1,17},{... | collective-permute-start | bytes 1474568 | tf_op jit(solution)/shard_map/ppermute | solution.py:358
  61.4 0.0 collective-permute-start.21
  61.4 0.0 collective-permute-done.20
  61.5 5.9 %collective-permute-done.18 = bf16[64,1920]{1,0:T(8,128)(2,1)S(1)} collective-permute-done((bf16[64,1920]{1,0:T(8,128)(2,1)S(1)}, bf16[64,1920]{1,0:T(8,128)(2,1)S(1)}, u32[]{:S(2)}, u32[]{:S(2)}) %collective-permute-start.18) | collective-permute-done | bytes 245792 | tf_op jit(solution)/shard_map/ppermute | solution.py:358
  67.4 0.0 collective-permute-start.24
  67.4 0.6 collective-permute-start.22
  68.1 5.6 %shard_map.96 = (f32[384,512]{1,0:T(8,128)S(1)}, f32[384,512]{1,0:T(8,128)S(1)}, f32[384,128]{1,0:T(8,128)S(1)}) custom-call(s32[5]{0:T(128)S(1)} %stack.23.numbers_ref, bf16[7168,512]{1,0:T(8,128)(2,1)} %bitcast.31, bf16[7168,512]{1,0:T(8,128)(2,1)} %bitcast.34, bf16[384,1920]{1,0:T(8,128)(2,1)S(1)} %get-tuple-element.65.refs_0_, ...), custom_call_target="tpu_custom_call" | custom-call | flops 2818572288 | bytes 3670016 | tf_op jit(solution)/shard_map/pallas_call | solution.py:174
  73.7 2.0 %collective-permute-start.16 = (bf16[128,1920]{1,0:T(8,128)(2,1)S(1)}, bf16[128,1920]{1,0:T(8,128)(2,1)S(1)}, u32[]{:S(2)}, u32[]{:S(2)}) collective-permute-start(bf16[128,1920]{1,0:T(8,128)(2,1)S(1)} %collective-permute-done.15), channel_id=1, source_target_pairs={{0,4},{4,0},{8,12},{12,8},{16,20},{20,16},{24,28},{28,24},{1,5},{5... | collective-permute-start | bytes 1474568 | tf_op jit(solution)/shard_map/ppermute | solution.py:358
  75.7 0.5 collective-permute-start.23
  76.2 1.4 %collective-permute-done.25 = bf16[64,1920]{1,0:T(8,128)(2,1)S(1)} collective-permute-done((bf16[64,1920]{1,0:T(8,128)(2,1)S(1)}, bf16[64,1920]{1,0:T(8,128)(2,1)S(1)}, u32[]{:S(2)}, u32[]{:S(2)}) %collective-permute-start.25) | collective-permute-done | bytes 245792 | tf_op jit(solution)/shard_map/ppermute | solution.py:358
  77.7 4.8 %shard_map.97 = (f32[8,384]{1,0:T(8,128)S(1)}, bf16[1792,512]{1,0:T(8,128)(2,1)S(1)}, bf16[1792,512]{1,0:T(8,128)(2,1)S(1)}, bf16[1792,512]{1,0:T(8,128)(2,1)S(1...) custom-call(s32[5]{0:T(128)S(1)} %stack.23.numbers_ref, ...), custom_call_target="tpu_custom_call" | custom-call | flops 1409286144 | bytes 3670016 | tf_op jit(solution)/shard_map/pallas_call | solution.py:223
  82.5 0.3 collective-permute-start.26
  82.9 0.1 pad_maximum_fusion.1
  82.9 1.2 %collective-permute-done.26 = bf16[64,1920]{1,0:T(8,128)(2,1)S(1)} collective-permute-done((bf16[64,1920]{1,0:T(8,128)(2,1)S(1)}, bf16[64,1920]{1,0:T(8,128)(2,1)S(1)}, u32[]{:S(2)}, u32[]{:S(2)}) %collective-permute-start.26) | collective-permute-done | bytes 245792 | tf_op jit(solution)/shard_map/ppermute | solution.py:358
  84.2 3.1 %shard_map.98 = (f32[8,128]{1,0:T(8,128)S(1)}, f32[32,8,128]{2,1,0:T(8,128)}) custom-call(s32[5]{0:T(128)S(1)} %stack.23.numbers_ref, bf16[128,1920]{1,0:T(8,128)(2,1)S(1)} %get-tuple-element.84.refs_0_, bf16[128,1920]{1,0:T(8,128)(2,1)S(1)} %get-tuple-element.85.refs_1_, bf16[128,1920]{1,0:T(8,128)(2,1)S(1)} %pad_maximum_fusion.3.refs_2_, ...), custom_call_target="tpu_custom_call" | custom-call | flops 469762048 | bytes 3670016 | tf_op jit(solution)/shard_map/pallas_call | solution.py:271
  87.3 3.4 %all-to-all-start = ((f32[32,8,128]{2,1,0:T(8,128)}), f32[32,8,128]{2,1,0:T(8,128)S(1)}, u32[]{:S(2)}, u32[]{:S(2)}) async-start(f32[32,8,128]{2,1,0:T(8,128)} %get-tuple-element.55), calls=%async_computation | async-start | bytes 262144 | tf_op jit(solution)/shard_map/all_to_all | solution.py:424
  90.7 1.2 %shard_map.100 = f32[1,1792]{1,0:T(1,128)} custom-call(bf16[512,1920]{1,0:T(8,128)(2,1)S(1)} %constant_dynamic-update-slice_fusion.rows_ref, f32[8,384]{1,0:T(8,128)S(1)} %get-tuple-element.47.refs_12_.early_ref, f32[8,128]{1,0:T(8,128)S(1)} %get-tuple-element.58.late_ref), custom_call_target="tpu_custom_call" | custom-call | flops 3932160 | bytes 1966080 | tf_op jit(solution)/shard_map/pallas_call | solution.py:301
  91.9 7.2 %all-to-all-done.back_ref = f32[32,8,128]{2,1,0:T(8,128)S(1)} async-done(((f32[32,8,128]{2,1,0:T(8,128)}), f32[32,8,128]{2,1,0:T(8,128)S(1)}, u32[]{:S(2)}, u32[]{:S(2)}) %all-to-all-start) | async-done | bytes 131104 | tf_op jit(solution)/shard_map/all_to_all | solution.py:424
  99.1 0.7 copy-done.7
  99.7 1.5 %shard_map.99 = (f32[1,64]{1,0:T(1,128)}, f32[1,1]{1,0:T(1,128)}) custom-call(s32[5]{0:T(128)} %copy-done, f32[32,8,128]{2,1,0:T(8,128)} %copy-done.7, s32[2,64]{1,0:T(2,128)S(1)} %bitcast.28, f32[2,64]{1,0:T(2,128)S(1)} %bitcast.29), custom_call_target="tpu_custom_call" | custom-call | tf_op jit(solution)/shard_map/pallas_call | solution.py:333
  (55 shorter events, 0.8 us)
Async XLA Ops:
  1.9 12.5 %collective-permute-start = (bf16[64,1792]{1,0:T(8,128)(2,1)S(1)}, bf16[64,1792]{1,0:T(8,128)(2,1)S(1)}, u32[]{:S(2)}, u32[]{:S(2)}) collective-permute-start(bf16[64,1792]{1,0:T(8,128)(2,1)S(1)} %get-tuple-element.61), channel_id=1, source_target_pairs={{0,3},{1,2},{2,1},{3,0},{4,7},{5,6},{6,5},{7,4},{8,11},{9,10},{10,... | collective-permute-start | bytes 688136 | tf_op jit(solution)/shard_map/ppermute | solution.py:355
  7.0 11.6 %collective-permute-start.2 = (bf16[64,1792]{1,0:T(8,128)(2,1)S(1)}, bf16[64,1792]{1,0:T(8,128)(2,1)S(1)}, u32[]{:S(2)}, u32[]{:S(2)}) collective-permute-start(bf16[64,1792]{1,0:T(8,128)(2,1)S(1)} %get-tuple-element.62), channel_id=1, source_target_pairs={{0,1},{1,0},{2,3},{3,2},{4,5},{5,4},{6,7},{7,6},{8,9},{9,8},{10,11... | collective-permute-start | bytes 688136 | tf_op jit(solution)/shard_map/ppermute | solution.py:355
  7.0 19.5 %collective-permute-start.1 = (bf16[64,1792]{1,0:T(8,128)(2,1)S(1)}, bf16[64,1792]{1,0:T(8,128)(2,1)S(1)}, u32[]{:S(2)}, u32[]{:S(2)}) collective-permute-start(bf16[64,1792]{1,0:T(8,128)(2,1)S(1)} %get-tuple-element.63), channel_id=1, source_target_pairs={{0,2},{1,3},{2,0},{3,1},{4,6},{5,7},{6,4},{7,5},{8,10},{9,11},{10,... | collective-permute-start | bytes 688136 | tf_op jit(solution)/shard_map/ppermute | solution.py:355
  9.2 75.0 %copy-start = (s32[5]{0:T(128)}, s32[5]{0:T(128)S(1)}, u32[]{:S(2)}) copy-start(s32[5]{0:T(128)S(1)} %stack.23.numbers_ref) | copy-start | bytes 64
  9.2 17.3 %copy-start.8 = (bf16[64,1792]{1,0:T(8,128)(2,1)S(1)}, bf16[64,1792]{1,0:T(8,128)(2,1)}, u32[]{:S(2)}) copy-start(bf16[64,1792]{1,0:T(8,128)(2,1)} %param.7) | copy-start | bytes 688132
  11.8 1.3 %copy-start.3 = (bf16[1792,512]{1,0:T(8,128)(2,1)}, bf16[1792,512]{1,0:T(8,128)(2,1)S(1)}, u32[]{:S(2)}) copy-start(bf16[1792,512]{1,0:T(8,128)(2,1)S(1)} %get-tuple-element.35.slab_ref) | copy-start | bytes 5505028
  13.1 1.2 %copy-start.5 = (bf16[1792,512]{1,0:T(8,128)(2,1)}, bf16[1792,512]{1,0:T(8,128)(2,1)S(1)}, u32[]{:S(2)}) copy-start(bf16[1792,512]{1,0:T(8,128)(2,1)S(1)} %get-tuple-element.36.slab_q_ref) | copy-start | bytes 5505028
  28.2 6.3 %collective-permute-start.5 = (bf16[64,1920]{1,0:T(8,128)(2,1)S(1)}, bf16[64,1920]{1,0:T(8,128)(2,1)S(1)}, u32[]{:S(2)}, u32[]{:S(2)}) collective-permute-start(bf16[64,1920]{1,0:T(8,128)(2,1)S(1)} %concatenate.30), channel_id=1, source_target_pairs={{0,8},{4,20},{8,0},{12,28},{16,24},{20,4},{24,16},{28,12},{1,9},{5... | collective-permute-start | bytes 737288 | tf_op jit(solution)/shard_map/ppermute | solution.py:358
  29.7 6.2 %collective-permute-start.6 = (bf16[64,1920]{1,0:T(8,128)(2,1)S(1)}, bf16[64,1920]{1,0:T(8,128)(2,1)S(1)}, u32[]{:S(2)}, u32[]{:S(2)}) collective-permute-start(bf16[64,1920]{1,0:T(8,128)(2,1)S(1)} %concatenate.30), channel_id=1, source_target_pairs={{0,4},{4,0},{8,12},{12,8},{16,20},{20,16},{24,28},{28,24},{1,5},{5... | collective-permute-start | bytes 737288 | tf_op jit(solution)/shard_map/ppermute | solution.py:358
  29.7 14.5 %collective-permute-start.4 = (bf16[64,1920]{1,0:T(8,128)(2,1)S(1)}, bf16[64,1920]{1,0:T(8,128)(2,1)S(1)}, u32[]{:S(2)}, u32[]{:S(2)}) collective-permute-start(bf16[64,1920]{1,0:T(8,128)(2,1)S(1)} %concatenate.30), channel_id=1, source_target_pairs={{0,2},{1,3},{2,0},{3,1},{4,6},{5,7},{6,4},{7,5},{8,10},{9,11},{10,... | collective-permute-start | bytes 737288 | tf_op jit(solution)/shard_map/ppermute | solution.py:355
  29.8 14.6 %collective-permute-start.3 = (bf16[64,1920]{1,0:T(8,128)(2,1)S(1)}, bf16[64,1920]{1,0:T(8,128)(2,1)S(1)}, u32[]{:S(2)}, u32[]{:S(2)}) collective-permute-start(bf16[64,1920]{1,0:T(8,128)(2,1)S(1)} %concatenate.30), channel_id=1, source_target_pairs={{0,1},{1,0},{2,3},{3,2},{4,5},{5,4},{6,7},{7,6},{8,9},{9,8},{10,11... | collective-permute-start | bytes 737288 | tf_op jit(solution)/shard_map/ppermute | solution.py:355
  34.5 10.7 %collective-permute-start.13 = (bf16[64,1920]{1,0:T(8,128)(2,1)S(1)}, bf16[64,1920]{1,0:T(8,128)(2,1)S(1)}, u32[]{:S(2)}, u32[]{:S(2)}) collective-permute-start(bf16[64,1920]{1,0:T(8,128)(2,1)S(1)} %collective-permute-done.5), channel_id=1, source_target_pairs={{0,16},{4,12},{8,24},{12,4},{16,0},{20,28},{24,8},{28,20},{1,17},{... | collective-permute-start | bytes 737288 | tf_op jit(solution)/shard_map/ppermute | solution.py:358
  36.0 9.8 %collective-permute-start.11 = (bf16[64,1920]{1,0:T(8,128)(2,1)S(1)}, bf16[64,1920]{1,0:T(8,128)(2,1)S(1)}, u32[]{:S(2)}, u32[]{:S(2)}) collective-permute-start(bf16[64,1920]{1,0:T(8,128)(2,1)S(1)} %collective-permute-done.5), channel_id=1, source_target_pairs={{0,4},{4,0},{8,12},{12,8},{16,20},{20,16},{24,28},{28,24},{1,5},{5... | collective-permute-start | bytes 737288 | tf_op jit(solution)/shard_map/ppermute | solution.py:358
  36.0 8.5 %collective-permute-start.7 = (bf16[64,1920]{1,0:T(8,128)(2,1)S(1)}, bf16[64,1920]{1,0:T(8,128)(2,1)S(1)}, u32[]{:S(2)}, u32[]{:S(2)}) collective-permute-start(bf16[64,1920]{1,0:T(8,128)(2,1)S(1)} %collective-permute-done.6), channel_id=1, source_target_pairs={{0,8},{4,20},{8,0},{12,28},{16,24},{20,4},{24,16},{28,12},{1,9},{5... | collective-permute-start | bytes 737288 | tf_op jit(solution)/shard_map/ppermute | solution.py:358
  44.2 10.0 %collective-permute-start.17 = (bf16[64,1920]{1,0:T(8,128)(2,1)S(1)}, bf16[64,1920]{1,0:T(8,128)(2,1)S(1)}, u32[]{:S(2)}, u32[]{:S(2)}) collective-permute-start(bf16[64,1920]{1,0:T(8,128)(2,1)S(1)} %collective-permute-done.4), channel_id=1, source_target_pairs={{0,1},{1,0},{2,3},{3,2},{4,5},{5,4},{6,7},{7,6},{8,9},{9,8},{10,11... | collective-permute-start | bytes 737288 | tf_op jit(solution)/shard_map/ppermute | solution.py:355
  44.4 3.3 %copy-start.6 = (bf16[1792,512]{1,0:T(8,128)(2,1)S(1)}, bf16[1792,512]{1,0:T(8,128)(2,1)}, u32[]{:S(2)}) copy-start(bf16[1792,512]{1,0:T(8,128)(2,1)} %copy-done.5) | copy-start | bytes 5505028
  44.4 5.3 %collective-permute-start.9 = (bf16[128,1920]{1,0:T(8,128)(2,1)S(1)}, bf16[128,1920]{1,0:T(8,128)(2,1)S(1)}, u32[]{:S(2)}, u32[]{:S(2)}) collective-permute-start(bf16[128,1920]{1,0:T(8,128)(2,1)S(1)} %pad_maximum_fusion), channel_id=1, source_target_pairs={{0,4},{4,0},{8,12},{12,8},{16,20},{20,16},{24,28},{28,24},{1,5},{5... | collective-permute-start | bytes 1474568 | tf_op jit(solution)/shard_map/ppermute | solution.py:358
  44.6 3.1 %copy-start.4 = (bf16[1792,512]{1,0:T(8,128)(2,1)S(1)}, bf16[1792,512]{1,0:T(8,128)(2,1)}, u32[]{:S(2)}) copy-start(bf16[1792,512]{1,0:T(8,128)(2,1)} %copy-done.3) | copy-start | bytes 5505028
  44.6 2.1 %collective-permute-start.12 = (bf16[64,1920]{1,0:T(8,128)(2,1)S(1)}, bf16[64,1920]{1,0:T(8,128)(2,1)S(1)}, u32[]{:S(2)}, u32[]{:S(2)}) collective-permute-start(bf16[64,1920]{1,0:T(8,128)(2,1)S(1)} %collective-permute-done.7), channel_id=1, source_target_pairs={{0,4},{4,0},{8,12},{12,8},{16,20},{20,16},{24,28},{28,24},{1,5},{5... | collective-permute-start | bytes 737288 | tf_op jit(solution)/shard_map/ppermute | solution.py:358
  45.2 8.9 %collective-permute-start.8 = (bf16[128,1920]{1,0:T(8,128)(2,1)S(1)}, bf16[128,1920]{1,0:T(8,128)(2,1)S(1)}, u32[]{:S(2)}, u32[]{:S(2)}) collective-permute-start(bf16[128,1920]{1,0:T(8,128)(2,1)S(1)} %pad_maximum_fusion), channel_id=1, source_target_pairs={{0,8},{4,20},{8,0},{12,28},{16,24},{20,4},{24,16},{28,12},{1,9},{5... | collective-permute-start | bytes 1474568 | tf_op jit(solution)/shard_map/ppermute | solution.py:358
  45.8 1.9 %collective-permute-start.14 = (bf16[64,1920]{1,0:T(8,128)(2,1)S(1)}, bf16[64,1920]{1,0:T(8,128)(2,1)S(1)}, u32[]{:S(2)}, u32[]{:S(2)}) collective-permute-start(bf16[64,1920]{1,0:T(8,128)(2,1)S(1)} %collective-permute-done.13), channel_id=1, source_target_pairs={{0,4},{4,0},{8,12},{12,8},{16,20},{20,16},{24,28},{28,24},{1,5},{5... | collective-permute-start | bytes 737288 | tf_op jit(solution)/shard_map/ppermute | solution.py:358
  49.7 9.6 %collective-permute-start.10 = (bf16[128,1920]{1,0:T(8,128)(2,1)S(1)}, bf16[128,1920]{1,0:T(8,128)(2,1)S(1)}, u32[]{:S(2)}, u32[]{:S(2)}) collective-permute-start(bf16[128,1920]{1,0:T(8,128)(2,1)S(1)} %collective-permute-done.9), channel_id=1, source_target_pairs={{0,8},{4,20},{8,0},{12,28},{16,24},{20,4},{24,16},{28,12},{1,9},{5... | collective-permute-start | bytes 1474568 | tf_op jit(solution)/shard_map/ppermute | solution.py:358
  54.1 7.4 %collective-permute-start.20 = (bf16[128,1920]{1,0:T(8,128)(2,1)S(1)}, bf16[128,1920]{1,0:T(8,128)(2,1)S(1)}, u32[]{:S(2)}, u32[]{:S(2)}) collective-permute-start(bf16[128,1920]{1,0:T(8,128)(2,1)S(1)} %collective-permute-done.8), channel_id=1, source_target_pairs={{0,4},{4,0},{8,12},{12,8},{16,20},{20,16},{24,28},{28,24},{1,5},{5... | collective-permute-start | bytes 1474568 | tf_op jit(solution)/shard_map/ppermute | solution.py:358
  59.3 8.1 %collective-permute-start.19 = (bf16[64,1920]{1,0:T(8,128)(2,1)S(1)}, bf16[64,1920]{1,0:T(8,128)(2,1)S(1)}, u32[]{:S(2)}, u32[]{:S(2)}) collective-permute-start(bf16[64,1920]{1,0:T(8,128)(2,1)S(1)} %collective-permute-done.17), channel_id=1, source_target_pairs={{0,4},{4,0},{8,12},{12,8},{16,20},{20,16},{24,28},{28,24},{1,5},{5... | collective-permute-start | bytes 737288 | tf_op jit(solution)/shard_map/ppermute | solution.py:358
  59.3 8.1 %collective-permute-start.18 = (bf16[64,1920]{1,0:T(8,128)(2,1)S(1)}, bf16[64,1920]{1,0:T(8,128)(2,1)S(1)}, u32[]{:S(2)}, u32[]{:S(2)}) collective-permute-start(bf16[64,1920]{1,0:T(8,128)(2,1)S(1)} %collective-permute-done.17), channel_id=1, source_target_pairs={{0,8},{4,20},{8,0},{12,28},{16,24},{20,4},{24,16},{28,12},{1,9},{5... | collective-permute-start | bytes 737288 | tf_op jit(solution)/shard_map/ppermute | solution.py:358
  59.9 13.8 %collective-permute-start.15 = (bf16[128,1920]{1,0:T(8,128)(2,1)S(1)}, bf16[128,1920]{1,0:T(8,128)(2,1)S(1)}, u32[]{:S(2)}, u32[]{:S(2)}) collective-permute-start(bf16[128,1920]{1,0:T(8,128)(2,1)S(1)} %collective-permute-done.8), channel_id=1, source_target_pairs={{0,16},{4,12},{8,24},{12,4},{16,0},{20,28},{24,8},{28,20},{1,17},{... | collective-permute-start | bytes 1474568 | tf_op jit(solution)/shard_map/ppermute | solution.py:358
  61.4 6.0 %collective-permute-start.21 = (bf16[128,1920]{1,0:T(8,128)(2,1)S(1)}, bf16[128,1920]{1,0:T(8,128)(2,1)S(1)}, u32[]{:S(2)}, u32[]{:S(2)}) collective-permute-start(bf16[128,1920]{1,0:T(8,128)(2,1)S(1)} %collective-permute-done.10), channel_id=1, source_target_pairs={{0,4},{4,0},{8,12},{12,8},{16,20},{20,16},{24,28},{28,24},{1,5},{5... | collective-permute-start | bytes 1474568 | tf_op jit(solution)/shard_map/ppermute | solution.py:358
  67.4 8.8 %collective-permute-start.24 = (bf16[64,1920]{1,0:T(8,128)(2,1)S(1)}, bf16[64,1920]{1,0:T(8,128)(2,1)S(1)}, u32[]{:S(2)}, u32[]{:S(2)}) collective-permute-start(bf16[64,1920]{1,0:T(8,128)(2,1)S(1)} %collective-permute-done.18), channel_id=1, source_target_pairs={{0,4},{4,0},{8,12},{12,8},{16,20},{20,16},{24,28},{28,24},{1,5},{5... | collective-permute-start | bytes 737288 | tf_op jit(solution)/shard_map/ppermute | solution.py:358
  67.4 8.3 %collective-permute-start.22 = (bf16[64,1920]{1,0:T(8,128)(2,1)S(1)}, bf16[64,1920]{1,0:T(8,128)(2,1)S(1)}, u32[]{:S(2)}, u32[]{:S(2)}) collective-permute-start(bf16[64,1920]{1,0:T(8,128)(2,1)S(1)} %collective-permute-done.19), channel_id=1, source_target_pairs={{0,8},{4,20},{8,0},{12,28},{16,24},{20,4},{24,16},{28,12},{1,9},{5... | collective-permute-start | bytes 737288 | tf_op jit(solution)/shard_map/ppermute | solution.py:358
  73.7 9.1 %collective-permute-start.16 = (bf16[128,1920]{1,0:T(8,128)(2,1)S(1)}, bf16[128,1920]{1,0:T(8,128)(2,1)S(1)}, u32[]{:S(2)}, u32[]{:S(2)}) collective-permute-start(bf16[128,1920]{1,0:T(8,128)(2,1)S(1)} %collective-permute-done.15), channel_id=1, source_target_pairs={{0,4},{4,0},{8,12},{12,8},{16,20},{20,16},{24,28},{28,24},{1,5},{5... | collective-permute-start | bytes 1474568 | tf_op jit(solution)/shard_map/ppermute | solution.py:358
  75.7 6.8 %collective-permute-start.23 = (bf16[64,1920]{1,0:T(8,128)(2,1)S(1)}, bf16[64,1920]{1,0:T(8,128)(2,1)S(1)}, u32[]{:S(2)}, u32[]{:S(2)}) collective-permute-start(bf16[64,1920]{1,0:T(8,128)(2,1)S(1)} %collective-permute-done.18), channel_id=1, source_target_pairs={{0,16},{4,12},{8,24},{12,4},{16,0},{20,28},{24,8},{28,20},{1,17},{... | collective-permute-start | bytes 737288 | tf_op jit(solution)/shard_map/ppermute | solution.py:358
  76.2 1.5 %collective-permute-start.25 = (bf16[64,1920]{1,0:T(8,128)(2,1)S(1)}, bf16[64,1920]{1,0:T(8,128)(2,1)S(1)}, u32[]{:S(2)}, u32[]{:S(2)}) collective-permute-start(bf16[64,1920]{1,0:T(8,128)(2,1)S(1)} %collective-permute-done.22), channel_id=1, source_target_pairs={{0,4},{4,0},{8,12},{12,8},{16,20},{20,16},{24,28},{28,24},{1,5},{5... | collective-permute-start | bytes 737288 | tf_op jit(solution)/shard_map/ppermute | solution.py:358
  82.5 1.6 %collective-permute-start.26 = (bf16[64,1920]{1,0:T(8,128)(2,1)S(1)}, bf16[64,1920]{1,0:T(8,128)(2,1)S(1)}, u32[]{:S(2)}, u32[]{:S(2)}) collective-permute-start(bf16[64,1920]{1,0:T(8,128)(2,1)S(1)} %collective-permute-done.23), channel_id=1, source_target_pairs={{0,4},{4,0},{8,12},{12,8},{16,20},{20,16},{24,28},{28,24},{1,5},{5... | collective-permute-start | bytes 737288 | tf_op jit(solution)/shard_map/ppermute | solution.py:358
  87.3 12.5 %copy-start.1 = (s32[64,2]{0,1:T(2,128)S(1)}, s32[64,2]{0,1:T(2,128)}, u32[]{:S(2)}) copy-start(s32[64,2]{0,1:T(2,128)} %param.10) | copy-start | bytes 1540
  87.3 12.5 %copy-start.2 = (f32[64,2]{0,1:T(2,128)S(1)}, f32[64,2]{0,1:T(2,128)}, u32[]{:S(2)}) copy-start(f32[64,2]{0,1:T(2,128)} %param.11) | copy-start | bytes 1540
  87.3 11.8 %all-to-all-start = ((f32[32,8,128]{2,1,0:T(8,128)}), f32[32,8,128]{2,1,0:T(8,128)S(1)}, u32[]{:S(2)}, u32[]{:S(2)}) async-start(f32[32,8,128]{2,1,0:T(8,128)} %get-tuple-element.55), calls=%async_computation | async-start | bytes 262144 | tf_op jit(solution)/shard_map/all_to_all | solution.py:424
  99.1 0.7 copy-start.7

commit v4 on v3

--- a/solution.py
+++ b/solution.py
@@ -151,36 +151,38 @@
     count = rows[0].shape[0]
     cols = w.shape[1]
     quarters = len(rows)
+    kept = 2 * quarters + 2
 
     def kernel(numbers_ref, w_ref, wq_ref, *refs):
         row_refs, ins, outs = refs[:quarters], refs[quarters : quarters + 3], refs[quarters + 3 : quarters + 6]
         slabs, sems = refs[quarters + 6 : -1], refs[-1]
         copies = fetching(numbers_ref, (w_ref, wq_ref), slabs, sems, 2)
-        half = count // 2
         for q in range(quarters):
             for i in range(2):
                 copies[2 * q + i].wait()
-                before = outs[i] if q else ins[i]
-                for part in range(2):
-                    here = slice(part * half, (part + 1) * half)
-                    outs[i][here, :] = before[here, :] + jnp.dot(
-                        row_refs[q][here, :depth], slabs[2 * q + i][...], preferred_element_type=jnp.float32
-                    )
+                before = outs[i][...] if q else ins[i][:count, :]
+                outs[i][...] = before + jnp.dot(
+                    row_refs[q][:, :depth], slabs[2 * q + i][...], preferred_element_type=jnp.float32
+                )
         tail = ins[2][:count, :]
         for ref in row_refs:
             tail = tail + ref[:, depth:].astype(jnp.float32)
         outs[2][...] = tail
-
-    return pl.pallas_call(
+        for copy in copies[2 * quarters :]:
+            copy.wait()
+
+    out = pl.pallas_call(
         kernel,
         in_specs=[SMEM_SPEC, HBM_SPEC, HBM_SPEC] + [VMEM_SPEC] * (quarters + 3),
-        out_specs=[VMEM_SPEC] * 3,
-        out_shape=[pltpu.VMEM((count, cols), jnp.float32)] * 2 + [pltpu.VMEM((count, EXTRA), jnp.float32)],
-        scratch_shapes=[pltpu.VMEM((depth, cols), w.dtype)] * (2 * quarters)
-        + [pltpu.SemaphoreType.DMA((2 * quarters,))],
+        out_specs=[VMEM_SPEC] * (3 + kept),
+        out_shape=[pltpu.VMEM((count, cols), jnp.float32)] * 2
+        + [pltpu.VMEM((count, EXTRA), jnp.float32)]
+        + [pltpu.VMEM((depth, cols), w.dtype)] * kept,
+        scratch_shapes=[pltpu.SemaphoreType.DMA((kept,))],
         compiler_params=PARAMS,
         cost_estimate=cost(count * quarters, depth, cols),
     )(numbers, in_hbm(w), in_hbm(wq), *[in_vmem(x) for x in (*rows, *sums)])
+    return out[3:], out[:3]
 
 
 def row_stats(expert, full, quant, total, extra):
@@ -201,35 +203,47 @@
     return stats.T[:8, :]
 
 
-def early_stats(numbers, w, wq, rows, depth, sums, n_z):
+def early_stats(numbers, rows, rest, slabs, sums, first_sums):
     count = rows.shape[0]
-    cols = w.shape[1]
-    kept = 2 * (n_z - 1)
-
-    def kernel(numbers_ref, w_ref, wq_ref, rows_ref, full_ref, quant_ref, tail_ref, stats_ref, *refs):
-        slabs, sems = refs[:kept], refs[kept]
-        last = fetching(numbers_ref, (w_ref, wq_ref), slabs[kept - 2 :], sems.at[pl.ds(kept - 2, 2)], n_z)
-        others = fetching(numbers_ref, (w_ref, wq_ref), slabs[: kept - 2], sems, 2)
-        x = rows_ref[:, :depth]
-        made = []
-        for i, before in enumerate((full_ref, quant_ref)):
-            last[i].wait()
-            made.append(before[...] + jnp.dot(x, slabs[kept - 2 + i][...], preferred_element_type=jnp.float32))
-        extra = rows_ref[:, depth:].astype(jnp.float32)
-        stats_ref[...] = row_stats(numbers_ref[0], *made, tail_ref[...] + extra, extra)
-        for copy in others:
-            copy.wait()
-
-    out = pl.pallas_call(
-        kernel,
-        in_specs=[SMEM_SPEC, HBM_SPEC, HBM_SPEC] + [VMEM_SPEC] * 4,
-        out_specs=[VMEM_SPEC] * (1 + kept),
-        out_shape=[pltpu.VMEM((8, count), jnp.float32)] + [pltpu.VMEM((depth, cols), w.dtype)] * kept,
-        scratch_shapes=[pltpu.SemaphoreType.DMA((kept,))],
+    done = sums[0].shape[0]
+    depth, cols = slabs[0].shape
+    quarters = len(rest)
+
+    def kernel(numbers_ref, rows_ref, *refs):
+        rest_refs, refs = refs[:quarters], refs[quarters:]
+        slab_refs, ins, firsts, stats_ref = refs[: len(slabs)], refs[-7:-4], refs[-4:-1], refs[-1]
+        expert = numbers_ref[0]
+        here = slice(0, done)
+        made = [
+            before[...] + jnp.dot(rows_ref[here, :depth], slab[...], preferred_element_type=jnp.float32)
+            for before, slab in zip(ins[:2], slab_refs[-2:])
+        ]
+        extra = rows_ref[here, depth:].astype(jnp.float32)
+        stats_ref[:, here] = row_stats(expert, *made, ins[2][...] + extra, extra)
+        here = slice(done, count)
+        made = [
+            before[here, :] + jnp.dot(rows_ref[here, :depth], slab[...], preferred_element_type=jnp.float32)
+            for before, slab in zip(firsts[:2], slab_refs[-2:])
+        ]
+        extra = rows_ref[here, depth:].astype(jnp.float32)
+        total = firsts[2][here, :] + extra
+        for q, ref in enumerate(rest_refs):
+            total = total + ref[:, depth:].astype(jnp.float32)
+            for i in range(2):
+                made[i] = made[i] + jnp.dot(
+                    ref[:, :depth], slab_refs[2 * q + i][...], preferred_element_type=jnp.float32
+                )
+        stats_ref[:, here] = row_stats(expert, *made, total, extra)
+
+    args = [rows, *rest, *slabs, *sums, *first_sums]
+    return pl.pallas_call(
+        kernel,
+        in_specs=[SMEM_SPEC] + [VMEM_SPEC] * len(args),
+        out_specs=VMEM_SPEC,
+        out_shape=pltpu.VMEM((8, count), jnp.float32),
         compiler_params=PARAMS,
         cost_estimate=cost(count, depth, cols),
-    )(numbers, in_hbm(w), in_hbm(wq), *[in_vmem(x) for x in (rows, *sums)])
-    return out[0], out[1:]
+    )(numbers, *[in_vmem(x) for x in args])
 
 
 def late_stats(numbers, rows, slabs, sums, early, tok, n_z):
@@ -266,7 +280,7 @@
                 owner = expert ^ (zero + core * (one - zero))
                 block = jnp.where(lane < tok, pltpu.roll(both, tok, 1) if odd else both, sums_here)
                 for z in range(n_z):
-                    out_ref[owner * n_z + z] = block
+                    out_ref[owner * n_z + z] = block[:2, :]
 
     return pl.pallas_call(
         kernel,
@@ -274,7 +288,7 @@
         out_specs=[VMEM_SPEC] * 2,
         out_shape=[
             pltpu.VMEM((8, count), jnp.float32),
-            jax.ShapeDtypeStruct((8 * n_z, 8, 2 * tok), jnp.float32),
+            jax.ShapeDtypeStruct((8 * n_z, 2, 2 * tok), jnp.float32),
         ],
         compiler_params=PARAMS,
         cost_estimate=cost(count, depth, cols),
@@ -312,7 +326,7 @@
     top, tok = routes.shape
 
     def kernel(numbers_ref, back_ref, routes_ref, weights_ref, token_ref, expert_ref):
-        own = jnp.zeros((8, 2 * tok), jnp.float32)
+        own = jnp.zeros((2, 2 * tok), jnp.float32)
         err = [jnp.zeros((1, tok), jnp.float32)] * top
         power = [jnp.zeros((1, tok), jnp.float32)] * top
         for i in range(back_ref.shape[0] // n_z):
@@ -335,7 +349,7 @@
         in_specs=[SMEM_SPEC] + [VMEM_SPEC] * 3,
         out_specs=[VMEM_SPEC] * 2,
         out_shape=[jax.ShapeDtypeStruct((1, tok), jnp.float32), jax.ShapeDtypeStruct((1, 1), jnp.float32)],
-    )(numbers, back, in_vmem(routes), in_vmem(weights))
+    )(numbers, in_hbm(back), in_vmem(routes), in_vmem(weights))
 
 
 def in_pieces(squares):
@@ -409,15 +423,16 @@
     near = pair, other_core(pair)
     beside = next_chip(near[0]), next_chip(near[1])
     across = opposite(tied(*beside, *first_sums))
-    gathered = most(near, beside)
-    sums = add_product(numbers, w, wq, of_quarters(gathered), width, first_sums)
+    slabs, sums = add_product(numbers, w, wq, of_quarters((*near, *beside)), width, first_sums)
+    rest = of_quarters(list(map(other_core, beside)))
     last = of_quarters((across, other_core(across)))
 
     single = tied(z_both, beside[1])
-    near = single, tied(other_core(single), gathered[4], gathered[5])
+    near = single, other_core(single)
     beside = next_chip(near[0]), next_chip(near[1])
     across = opposite(tied(*beside, *sums))
-    early, slabs = early_stats(numbers, w, wq, jnp.concatenate(most(near, beside), axis=0), width, sums, n_z)
+    most3 = jnp.concatenate(most(near, beside), axis=0)
+    early = early_stats(numbers, most3, rest, slabs, sums, first_sums)
     last.append(jnp.concatenate([across, other_core(tied(across, early))], axis=0))
     late, payload = late_stats(numbers, last, slabs, first_sums, early, tok, n_z)
 

time: 102 us -> 97.1 us (0.952)
  Pallas kernels: 20.9 us -> 18.6 us
  other arithmetic: 2.76 us -> 1.62 us
    pallas_call x1, Pallas kernels: 4.8 us -> 3.44 us  [early_stats(): pl.pallas_call(kernel, in_specs=[SMEM_SPEC] + [VMEM_SPEC] * len(args), ou...]
    ppermute x6, waiting for transfers between devices: 19 us -> 20.4 us  [over_z(): return lax.ppermute(x, 'tensor', [(i, i ^ k) for i in range(n_z)])]
    ppermute x21, waiting for transfers between devices: 19.5 us -> 18.3 us  [in_plane(): lax.ppermute(x, 'expert', [(i, i ^ (one if i & 1 else zero)) for i in ran...]
    all_to_all x1, waiting for transfers between devices: 7.18 us -> 6.07 us  [line_device(): lax.all_to_all(payload, ('expert', 'tensor'), split_axis=0, concat_axis=0...]
    unnamed x35 -> x32, local copies, waits for them, and re-layouts: 3.69 us -> 3.43 us
  transfers between devices with their start and end apart: 28 -> 28, of which waited for: 13 -> 13; matrix products, arithmetic and copies ran while one was open for 2% -> 1% of each run, Pallas kernels for 16% -> 15%
where the time goes in v4:
time: 97.1 us; the launch traced here: 96.8 us
  waiting for transfers between devices  44.7 us (46%)
  starting transfers between devices  25.2 us (26%)
  Pallas kernels  18.6 us (19%)
  local copies, waits for them, and re-layouts  5.61 us (6%)
  other arithmetic  1.62 us (2%)
  between operations  1.02 us (1%)
    ppermute x6, waiting for transfers between devices, over_z(): return lax.ppermute(x, 'tensor', [(i, i ^ k) for i in range(n_z)])  20.4 us
    ppermute x21, waiting for transfers between devices, in_plane(): lax.ppermute(x, 'expert', [(i, i ^ (one if i & 1 else zero)) for i in ran...  18.3 us
    ppermute x21, starting transfers between devices, in_plane(): lax.ppermute(x, 'expert', [(i, i ^ (one if i & 1 else zero)) for i in ran...  13.5 us
    ppermute x6, starting transfers between devices, over_z(): return lax.ppermute(x, 'tensor', [(i, i ^ k) for i in range(n_z)])  8.8 us
    all_to_all x1, waiting for transfers between devices, line_device(): lax.all_to_all(payload, ('expert', 'tensor'), split_axis=0, concat_axis=0...  6.07 us
    pallas_call x1, Pallas kernels, add_product(): pl.pallas_call(kernel, in_specs=[SMEM_SPEC, HBM_SPEC, HBM_SPEC] + [VMEM_S...  4.81 us
    pallas_call x1, Pallas kernels, early_stats(): pl.pallas_call(kernel, in_specs=[SMEM_SPEC] + [VMEM_SPEC] * len(args), ou...  3.44 us
    unnamed x32, local copies, waits for them, and re-layouts  3.43 us
  transfers between devices with their start and end apart: 28, of which 13 were waited for; matrix products, arithmetic and copies ran while one was open for 1% of the time, Pallas kernels for 15%

profile of v4, /device:TPU:0, one launch (start us, length us, event | category | flops | bytes accessed | tf_op | source)
XLA Modules:
  0.0 96.8 jit_solution(5381554447514013992)
XLA Ops:
  0.7 1.2 %dynamic-slice_bitcast_fusion.2 = (bf16[64,1792]{1,0:T(8,128)(2,1)S(1)}, bf16[64,1792]{1,0:T(8,128)(2,1)S(1)}, bf16[64,1792]{1,0:T(8,128)(2,1)S(1)}) fusion(bf16[1,64,7168]{2,1,0:T(8,128)(2,1)} %param.8, s32[]{:T(128)S(6)} %select_n.13, s32[]{:T(128)S(6)} %select_n.15, s32[]{:T(128)S(6)} %select_n.14), kind=kLoop, calls=%fused_computation.16 | loop fusion | bytes 1376268 | tf_op jit(solution)/shard_map/dynamic_slice | solution.py:375
  1.9 5.1 %collective-permute-start = (bf16[64,1792]{1,0:T(8,128)(2,1)S(1)}, bf16[64,1792]{1,0:T(8,128)(2,1)S(1)}, u32[]{:S(2)}, u32[]{:S(2)}) collective-permute-start(bf16[64,1792]{1,0:T(8,128)(2,1)S(1)} %get-tuple-element.57), channel_id=1, source_target_pairs={{0,3},{1,2},{2,1},{3,0},{4,7},{5,6},{6,5},{7,4},{8,11},{9,10},{10,... | collective-permute-start | bytes 688136 | tf_op jit(solution)/shard_map/ppermute | solution.py:369
  7.0 0.0 collective-permute-start.1
  7.0 0.6 collective-permute-start.2
  7.6 0.1 stack.23.numbers_ref
  7.7 2.6 %shard_map.94 = (bf16[1792,512]{1,0:T(8,128)(2,1)S(1)}, bf16[1792,512]{1,0:T(8,128)(2,1)S(1)}) custom-call(s32[5]{0:T(128)S(1)} %stack.23.numbers_ref, bf16[7168,512]{1,0:T(8,128)(2,1)} %bitcast.30, bf16[7168,512]{1,0:T(8,128)(2,1)} %bitcast.32), custom_call_target="tpu_custom_call" | custom-call | bytes 3670016 | tf_op jit(solution)/shard_map/pallas_call | solution.py:109
  10.4 1.3 %copy-done.3 = bf16[1792,512]{1,0:T(8,128)(2,1)} copy-done((bf16[1792,512]{1,0:T(8,128)(2,1)}, bf16[1792,512]{1,0:T(8,128)(2,1)S(1)}, u32[]{:S(2)}) %copy-start.3) | copy-done | bytes 1835032
  11.6 1.2 %copy-done.5 = bf16[1792,512]{1,0:T(8,128)(2,1)} copy-done((bf16[1792,512]{1,0:T(8,128)(2,1)}, bf16[1792,512]{1,0:T(8,128)(2,1)S(1)}, u32[]{:S(2)}) %copy-start.5) | copy-done | bytes 1835032
  12.9 0.1 copy.16
  13.0 0.6 collective-permute-done
  13.6 12.9 %collective-permute-done.1 = bf16[64,1792]{1,0:T(8,128)(2,1)S(1)} collective-permute-done((bf16[64,1792]{1,0:T(8,128)(2,1)S(1)}, bf16[64,1792]{1,0:T(8,128)(2,1)S(1)}, u32[]{:S(2)}, u32[]{:S(2)}) %collective-permute-start.1) | collective-permute-done | bytes 229408 | tf_op jit(solution)/shard_map/ppermute | solution.py:369
  26.5 0.0 collective-permute-done.2
  26.5 1.2 %multiply_reduce_fusion = (f32[64]{0:T(128)S(1)}, bf16[64,1792]{1,0:T(8,128)(2,1)S(1)}) fusion(bf16[64,1792]{1,0:T(8,128)(2,1)S(1)} %collective-permute-done.2, bf16[64,1792]{1,0:T(8,128)(2,1)S(1)} %collective-permute-done.1, bf16[64,1792]{1,0:T(8,128)(2,1)S(1)} %collective-permute-done, bf16[1,64,7168]{2,1,0:T(8,128)(2,1)} %param.8, s32[]{:T(128)S(6)} %select_n.12, ...), kind=kLoop, calls=%fused_computation.12 | loop fusion | flops 1490880 | bytes 1383684 | tf_op jit(solution)/shard_map/reduce_sum | solution.py:386
  27.7 0.1 copy.14
  27.8 0.1 copy.13
  27.9 0.1 copy.15
  28.1 0.1 concatenate.36
  28.2 1.6 %collective-permute-start.5 = (bf16[64,1920]{1,0:T(8,128)(2,1)S(1)}, bf16[64,1920]{1,0:T(8,128)(2,1)S(1)}, u32[]{:S(2)}, u32[]{:S(2)}) collective-permute-start(bf16[64,1920]{1,0:T(8,128)(2,1)S(1)} %concatenate.36), channel_id=1, source_target_pairs={{0,8},{4,20},{8,0},{12,28},{16,24},{20,4},{24,16},{28,12},{1,9},{5... | collective-permute-start | bytes 737288 | tf_op jit(solution)/shard_map/ppermute | solution.py:372
  29.8 3.0 %collective-permute-start.3 = (bf16[64,1920]{1,0:T(8,128)(2,1)S(1)}, bf16[64,1920]{1,0:T(8,128)(2,1)S(1)}, u32[]{:S(2)}, u32[]{:S(2)}) collective-permute-start(bf16[64,1920]{1,0:T(8,128)(2,1)S(1)} %concatenate.36), channel_id=1, source_target_pairs={{0,1},{1,0},{2,3},{3,2},{4,5},{5,4},{6,7},{7,6},{8,9},{9,8},{10,11... | collective-permute-start | bytes 737288 | tf_op jit(solution)/shard_map/ppermute | solution.py:369
  32.8 1.6 %collective-permute-done.5 = bf16[64,1920]{1,0:T(8,128)(2,1)S(1)} collective-permute-done((bf16[64,1920]{1,0:T(8,128)(2,1)S(1)}, bf16[64,1920]{1,0:T(8,128)(2,1)S(1)}, u32[]{:S(2)}, u32[]{:S(2)}) %collective-permute-start.5) | collective-permute-done | bytes 245792 | tf_op jit(solution)/shard_map/ppermute | solution.py:372
  34.5 0.0 collective-permute-start.11
  34.5 1.5 %collective-permute-start.13 = (bf16[64,1920]{1,0:T(8,128)(2,1)S(1)}, bf16[64,1920]{1,0:T(8,128)(2,1)S(1)}, u32[]{:S(2)}, u32[]{:S(2)}) collective-permute-start(bf16[64,1920]{1,0:T(8,128)(2,1)S(1)} %collective-permute-done.5), channel_id=1, source_target_pairs={{0,16},{4,12},{8,24},{12,4},{16,0},{20,28},{24,8},{28,20},{1,17},{... | collective-permute-start | bytes 737288 | tf_op jit(solution)/shard_map/ppermute | solution.py:372
  36.0 0.0 collective-permute-done.6
  36.0 1.5 %collective-permute-start.7 = (bf16[64,1920]{1,0:T(8,128)(2,1)S(1)}, bf16[64,1920]{1,0:T(8,128)(2,1)S(1)}, u32[]{:S(2)}, u32[]{:S(2)}) collective-permute-start(bf16[64,1920]{1,0:T(8,128)(2,1)S(1)} %collective-permute-done.6), channel_id=1, source_target_pairs={{0,8},{4,20},{8,0},{12,28},{16,24},{20,4},{24,16},{28,12},{1,9},{5... | collective-permute-start | bytes 737288 | tf_op jit(solution)/shard_map/ppermute | solution.py:372
  37.5 6.7 %collective-permute-done.4 = bf16[64,1920]{1,0:T(8,128)(2,1)S(1)} collective-permute-done((bf16[64,1920]{1,0:T(8,128)(2,1)S(1)}, bf16[64,1920]{1,0:T(8,128)(2,1)S(1)}, u32[]{:S(2)}, u32[]{:S(2)}) %collective-permute-start.4) | collective-permute-done | bytes 245792 | tf_op jit(solution)/shard_map/ppermute | solution.py:369
  44.2 0.0 collective-permute-start.17
  44.3 0.1 collective-permute-done.3
  44.4 0.0 collective-permute-done.7
  44.5 0.1 collective-permute-start.9
  44.6 0.6 collective-permute-start.12
  45.2 0.0 collective-permute-done.11
  45.2 0.6 collective-permute-start.8
  45.8 0.0 collective-permute-done.13
  45.8 0.7 collective-permute-start.14
  46.5 0.2 collective-permute-done.12
  46.8 0.8 collective-permute-done.14
  47.7 2.1 %shard_map.95 = (f32[512,512]{1,0:T(8,128)S(1)}, f32[512,512]{1,0:T(8,128)S(1)}, f32[512,128]{1,0:T(8,128)S(1)}) custom-call(bf16[512,1920]{1,0:T(8,128)(2,1)S(1)} %constant_dynamic-update-slice_fusion.rows_ref, bf16[1792,512]{1,0:T(8,128)(2,1)S(1)} %copy-done.4, bf16[1792,512]{1,0:T(8,128)(2,1)S(1)} %copy-done.6), custom_call_target="tpu_custom_call" | custom-call | flops 1879048192 | bytes 3670016 | tf_op jit(solution)/shard_map/pallas_call | solution.py:133
  49.8 0.0 collective-permute-done.9
  49.8 1.2 %collective-permute-start.10 = (bf16[128,1920]{1,0:T(8,128)(2,1)S(1)}, bf16[128,1920]{1,0:T(8,128)(2,1)S(1)}, u32[]{:S(2)}, u32[]{:S(2)}) collective-permute-start(bf16[128,1920]{1,0:T(8,128)(2,1)S(1)} %collective-permute-done.9), channel_id=1, source_target_pairs={{0,8},{4,20},{8,0},{12,28},{16,24},{20,4},{24,16},{28,12},{1,9},{5... | collective-permute-start | bytes 1474568 | tf_op jit(solution)/shard_map/ppermute | solution.py:372
  51.0 3.0 %collective-permute-done.8 = bf16[128,1920]{1,0:T(8,128)(2,1)S(1)} collective-permute-done((bf16[128,1920]{1,0:T(8,128)(2,1)S(1)}, bf16[128,1920]{1,0:T(8,128)(2,1)S(1)}, u32[]{:S(2)}, u32[]{:S(2)}) %collective-permute-start.8) | collective-permute-done | bytes 491552 | tf_op jit(solution)/shard_map/ppermute | solution.py:372
  54.1 5.2 %collective-permute-done.10 = bf16[128,1920]{1,0:T(8,128)(2,1)S(1)} collective-permute-done((bf16[128,1920]{1,0:T(8,128)(2,1)S(1)}, bf16[128,1920]{1,0:T(8,128)(2,1)S(1)}, u32[]{:S(2)}, u32[]{:S(2)}) %collective-permute-start.10) | collective-permute-done | bytes 491552 | tf_op jit(solution)/shard_map/ppermute | solution.py:372
  59.4 0.1 collective-permute-start.19
  59.4 0.6 collective-permute-start.18
  60.0 1.5 %collective-permute-start.15 = (bf16[128,1920]{1,0:T(8,128)(2,1)S(1)}, bf16[128,1920]{1,0:T(8,128)(2,1)S(1)}, u32[]{:S(2)}, u32[]{:S(2)}) collective-permute-start(bf16[128,1920]{1,0:T(8,128)(2,1)S(1)} %collective-permute-done.8), channel_id=1, source_target_pairs={{0,16},{4,12},{8,24},{12,4},{16,0},{20,28},{24,8},{28,20},{1,17},{... | collective-permute-start | bytes 1474568 | tf_op jit(solution)/shard_map/ppermute | solution.py:372
  61.7 0.1 pad_maximum_fusion
  61.8 4.8 %shard_map.96 = (f32[256,512]{1,0:T(8,128)S(1)}, f32[256,512]{1,0:T(8,128)S(1)}, f32[256,128]{1,0:T(8,128)S(1)}, bf16[1792,512]{1,0:T(8,128)(2,1)S(1)}, bf16[179...) custom-call(s32[5]{0:T(128)S(1)} %stack.23.numbers_ref, ...), custom_call_target="tpu_custom_call" | custom-call | flops 1879048192 | bytes 3670016 | tf_op jit(solution)/shard_map/pallas_call | solution.py:174
  66.6 1.6 %collective-permute-start.20 = (bf16[64,1920]{1,0:T(8,128)(2,1)S(1)}, bf16[64,1920]{1,0:T(8,128)(2,1)S(1)}, u32[]{:S(2)}, u32[]{:S(2)}) collective-permute-start(bf16[64,1920]{1,0:T(8,128)(2,1)S(1)} %collective-permute-done.19), channel_id=1, source_target_pairs={{0,8},{4,20},{8,0},{12,28},{16,24},{20,4},{24,16},{28,12},{1,9},{5... | collective-permute-start | bytes 737288 | tf_op jit(solution)/shard_map/ppermute | solution.py:372
  68.2 0.1 collective-permute-start.22
  68.3 5.3 %collective-permute-done.20 = bf16[64,1920]{1,0:T(8,128)(2,1)S(1)} collective-permute-done((bf16[64,1920]{1,0:T(8,128)(2,1)S(1)}, bf16[64,1920]{1,0:T(8,128)(2,1)S(1)}, u32[]{:S(2)}, u32[]{:S(2)}) %collective-permute-start.20) | collective-permute-done | bytes 245792 | tf_op jit(solution)/shard_map/ppermute | solution.py:372
  73.6 1.2 %collective-permute-start.21 = (bf16[64,1920]{1,0:T(8,128)(2,1)S(1)}, bf16[64,1920]{1,0:T(8,128)(2,1)S(1)}, u32[]{:S(2)}, u32[]{:S(2)}) collective-permute-start(bf16[64,1920]{1,0:T(8,128)(2,1)S(1)} %collective-permute-done.18), channel_id=1, source_target_pairs={{0,16},{4,12},{8,24},{12,4},{16,0},{20,28},{24,8},{28,20},{1,17},{... | collective-permute-start | bytes 737288 | tf_op jit(solution)/shard_map/ppermute | solution.py:372
  74.9 0.6 collective-permute-start.16
  75.5 0.1 pad_maximum_fusion.5
  75.6 0.7 collective-permute-done.23
  76.3 3.4 %shard_map.97.refs_12_.early_ref = f32[8,384]{1,0:T(8,128)S(1)} custom-call(s32[5]{0:T(128)S(1)} %stack.23.numbers_ref, bf16[384,1920]{1,0:T(8,128)(2,1)S(1)} %constant_dynamic-update-slice_fusion.8.rows_ref, bf16[128,1920]{1,0:T(8,128)(2,1)S(1)} %get-tuple-element.84.refs_0_, bf16[128,1920]{1,0:T(8,128)(2,1)S(1)} %get-tuple-element.85.refs_1_, ...), custom_call_target="tpu_custom_call" | custom-call | flops 1409286144 | bytes 3670016 | tf_op jit(solution)/shard_map/pallas_call | solution.py:239
  79.8 0.0 collective-permute-done.21
  79.8 0.1 collective-permute-start.26
  80.0 1.3 %collective-permute-done.26 = bf16[64,1920]{1,0:T(8,128)(2,1)S(1)} collective-permute-done((bf16[64,1920]{1,0:T(8,128)(2,1)S(1)}, bf16[64,1920]{1,0:T(8,128)(2,1)S(1)}, u32[]{:S(2)}, u32[]{:S(2)}) %collective-permute-start.26) | collective-permute-done | bytes 245792 | tf_op jit(solution)/shard_map/ppermute | solution.py:372
  81.4 0.1 pad_maximum_fusion.3
  81.5 3.1 %shard_map.98 = (f32[8,128]{1,0:T(8,128)S(1)}, f32[32,2,128]{2,1,0:T(2,128)}) custom-call(s32[5]{0:T(128)S(1)} %stack.23.numbers_ref, bf16[128,1920]{1,0:T(8,128)(2,1)S(1)} %get-tuple-element.80.refs_0_, bf16[128,1920]{1,0:T(8,128)(2,1)S(1)} %get-tuple-element.81.refs_1_, bf16[128,1920]{1,0:T(8,128)(2,1)S(1)} %pad_maximum_fusion.7.refs_2_, ...), custom_call_target="tpu_custom_call" | custom-call | flops 469762048 | bytes 3670016 | tf_op jit(solution)/shard_map/pallas_call | solution.py:285
  84.6 2.9 %all-to-all-start = ((f32[32,2,128]{2,1,0:T(2,128)}), f32[32,2,128]{2,1,0:T(2,128)S(1)}, u32[]{:S(2)}, u32[]{:S(2)}) async-start(f32[32,2,128]{2,1,0:T(2,128)} %get-tuple-element.51), calls=%async_computation | async-start | bytes 65536 | tf_op jit(solution)/shard_map/all_to_all | solution.py:439
  87.6 1.2 %shard_map.100 = f32[1,1792]{1,0:T(1,128)} custom-call(bf16[512,1920]{1,0:T(8,128)(2,1)S(1)} %constant_dynamic-update-slice_fusion.rows_ref, f32[8,384]{1,0:T(8,128)S(1)} %shard_map.97.refs_12_.early_ref, f32[8,128]{1,0:T(8,128)S(1)} %get-tuple-element.54.late_ref), custom_call_target="tpu_custom_call" | custom-call | flops 3932160 | bytes 1966080 | tf_op jit(solution)/shard_map/pallas_call | solution.py:315
  88.8 6.1 %all-to-all-done.back_ref = f32[32,2,128]{2,1,0:T(2,128)S(1)} async-done(((f32[32,2,128]{2,1,0:T(2,128)}), f32[32,2,128]{2,1,0:T(2,128)S(1)}, u32[]{:S(2)}, u32[]{:S(2)}) %all-to-all-start) | async-done | bytes 32800 | tf_op jit(solution)/shard_map/all_to_all | solution.py:439
  94.9 0.6 copy-done.8
  95.5 1.4 %shard_map.99 = (f32[1,64]{1,0:T(1,128)}, f32[1,1]{1,0:T(1,128)}) custom-call(s32[5]{0:T(128)} %copy-done, f32[32,2,128]{2,1,0:T(2,128)} %copy-done.8, s32[2,64]{1,0:T(2,128)S(1)} %bitcast.28, f32[2,64]{1,0:T(2,128)S(1)} %bitcast.29), custom_call_target="tpu_custom_call" | custom-call | tf_op jit(solution)/shard_map/pallas_call | solution.py:347
  (59 shorter events, 0.8 us)
Async XLA Ops:
  1.9 11.7 %collective-permute-start = (bf16[64,1792]{1,0:T(8,128)(2,1)S(1)}, bf16[64,1792]{1,0:T(8,128)(2,1)S(1)}, u32[]{:S(2)}, u32[]{:S(2)}) collective-permute-start(bf16[64,1792]{1,0:T(8,128)(2,1)S(1)} %get-tuple-element.57), channel_id=1, source_target_pairs={{0,3},{1,2},{2,1},{3,0},{4,7},{5,6},{6,5},{7,4},{8,11},{9,10},{10,... | collective-permute-start | bytes 688136 | tf_op jit(solution)/shard_map/ppermute | solution.py:369
  7.0 19.5 %collective-permute-start.1 = (bf16[64,1792]{1,0:T(8,128)(2,1)S(1)}, bf16[64,1792]{1,0:T(8,128)(2,1)S(1)}, u32[]{:S(2)}, u32[]{:S(2)}) collective-permute-start(bf16[64,1792]{1,0:T(8,128)(2,1)S(1)} %get-tuple-element.59), channel_id=1, source_target_pairs={{0,2},{1,3},{2,0},{3,1},{4,6},{5,7},{6,4},{7,5},{8,10},{9,11},{10,... | collective-permute-start | bytes 688136 | tf_op jit(solution)/shard_map/ppermute | solution.py:369
  7.0 19.5 %collective-permute-start.2 = (bf16[64,1792]{1,0:T(8,128)(2,1)S(1)}, bf16[64,1792]{1,0:T(8,128)(2,1)S(1)}, u32[]{:S(2)}, u32[]{:S(2)}) collective-permute-start(bf16[64,1792]{1,0:T(8,128)(2,1)S(1)} %get-tuple-element.58), channel_id=1, source_target_pairs={{0,1},{1,0},{2,3},{3,2},{4,5},{5,4},{6,7},{7,6},{8,9},{9,8},{10,11... | collective-permute-start | bytes 688136 | tf_op jit(solution)/shard_map/ppermute | solution.py:369
  7.7 73.8 %copy-start = (s32[5]{0:T(128)}, s32[5]{0:T(128)S(1)}, u32[]{:S(2)}) copy-start(s32[5]{0:T(128)S(1)} %stack.23.numbers_ref) | copy-start | bytes 64
  7.7 5.2 %copy-start.9 = (bf16[1792]{0:T(1024)(128)(2,1)S(1)}, bf16[1792]{0:T(1024)(128)(2,1)}, u32[]{:S(2)}) copy-start(bf16[1792]{0:T(1024)(128)(2,1)} %param.9) | copy-start | bytes 10756
  7.7 5.2 %copy-start.1 = (s32[64,2]{0,1:T(2,128)S(1)}, s32[64,2]{0,1:T(2,128)}, u32[]{:S(2)}) copy-start(s32[64,2]{0,1:T(2,128)} %param.10) | copy-start | bytes 1540
  7.7 18.8 %copy-start.7 = (bf16[64,1792]{1,0:T(8,128)(2,1)S(1)}, bf16[64,1792]{1,0:T(8,128)(2,1)}, u32[]{:S(2)}) copy-start(bf16[64,1792]{1,0:T(8,128)(2,1)} %param.7) | copy-start | bytes 688132
  10.3 1.3 %copy-start.3 = (bf16[1792,512]{1,0:T(8,128)(2,1)}, bf16[1792,512]{1,0:T(8,128)(2,1)S(1)}, u32[]{:S(2)}) copy-start(bf16[1792,512]{1,0:T(8,128)(2,1)S(1)} %get-tuple-element.33.slab_ref) | copy-start | bytes 5505028
  11.6 1.2 %copy-start.5 = (bf16[1792,512]{1,0:T(8,128)(2,1)}, bf16[1792,512]{1,0:T(8,128)(2,1)S(1)}, u32[]{:S(2)}) copy-start(bf16[1792,512]{1,0:T(8,128)(2,1)S(1)} %get-tuple-element.34.slab_q_ref) | copy-start | bytes 5505028
  28.2 6.3 %collective-permute-start.5 = (bf16[64,1920]{1,0:T(8,128)(2,1)S(1)}, bf16[64,1920]{1,0:T(8,128)(2,1)S(1)}, u32[]{:S(2)}, u32[]{:S(2)}) collective-permute-start(bf16[64,1920]{1,0:T(8,128)(2,1)S(1)} %concatenate.36), channel_id=1, source_target_pairs={{0,8},{4,20},{8,0},{12,28},{16,24},{20,4},{24,16},{28,12},{1,9},{5... | collective-permute-start | bytes 737288 | tf_op jit(solution)/shard_map/ppermute | solution.py:372
  29.7 6.2 %collective-permute-start.6 = (bf16[64,1920]{1,0:T(8,128)(2,1)S(1)}, bf16[64,1920]{1,0:T(8,128)(2,1)S(1)}, u32[]{:S(2)}, u32[]{:S(2)}) collective-permute-start(bf16[64,1920]{1,0:T(8,128)(2,1)S(1)} %concatenate.36), channel_id=1, source_target_pairs={{0,4},{4,0},{8,12},{12,8},{16,20},{20,16},{24,28},{28,24},{1,5},{5... | collective-permute-start | bytes 737288 | tf_op jit(solution)/shard_map/ppermute | solution.py:372
  29.8 14.5 %collective-permute-start.4 = (bf16[64,1920]{1,0:T(8,128)(2,1)S(1)}, bf16[64,1920]{1,0:T(8,128)(2,1)S(1)}, u32[]{:S(2)}, u32[]{:S(2)}) collective-permute-start(bf16[64,1920]{1,0:T(8,128)(2,1)S(1)} %concatenate.36), channel_id=1, source_target_pairs={{0,2},{1,3},{2,0},{3,1},{4,6},{5,7},{6,4},{7,5},{8,10},{9,11},{10,... | collective-permute-start | bytes 737288 | tf_op jit(solution)/shard_map/ppermute | solution.py:369
  29.8 14.6 %collective-permute-start.3 = (bf16[64,1920]{1,0:T(8,128)(2,1)S(1)}, bf16[64,1920]{1,0:T(8,128)(2,1)S(1)}, u32[]{:S(2)}, u32[]{:S(2)}) collective-permute-start(bf16[64,1920]{1,0:T(8,128)(2,1)S(1)} %concatenate.36), channel_id=1, source_target_pairs={{0,1},{1,0},{2,3},{3,2},{4,5},{5,4},{6,7},{7,6},{8,9},{9,8},{10,11... | collective-permute-start | bytes 737288 | tf_op jit(solution)/shard_map/ppermute | solution.py:369
  34.5 10.7 %collective-permute-start.11 = (bf16[64,1920]{1,0:T(8,128)(2,1)S(1)}, bf16[64,1920]{1,0:T(8,128)(2,1)S(1)}, u32[]{:S(2)}, u32[]{:S(2)}) collective-permute-start(bf16[64,1920]{1,0:T(8,128)(2,1)S(1)} %collective-permute-done.5), channel_id=1, source_target_pairs={{0,4},{4,0},{8,12},{12,8},{16,20},{20,16},{24,28},{28,24},{1,5},{5... | collective-permute-start | bytes 737288 | tf_op jit(solution)/shard_map/ppermute | solution.py:372
  34.5 11.3 %collective-permute-start.13 = (bf16[64,1920]{1,0:T(8,128)(2,1)S(1)}, bf16[64,1920]{1,0:T(8,128)(2,1)S(1)}, u32[]{:S(2)}, u32[]{:S(2)}) collective-permute-start(bf16[64,1920]{1,0:T(8,128)(2,1)S(1)} %collective-permute-done.5), channel_id=1, source_target_pairs={{0,16},{4,12},{8,24},{12,4},{16,0},{20,28},{24,8},{28,20},{1,17},{... | collective-permute-start | bytes 737288 | tf_op jit(solution)/shard_map/ppermute | solution.py:372
  36.0 8.5 %collective-permute-start.7 = (bf16[64,1920]{1,0:T(8,128)(2,1)S(1)}, bf16[64,1920]{1,0:T(8,128)(2,1)S(1)}, u32[]{:S(2)}, u32[]{:S(2)}) collective-permute-start(bf16[64,1920]{1,0:T(8,128)(2,1)S(1)} %collective-permute-done.6), channel_id=1, source_target_pairs={{0,8},{4,20},{8,0},{12,28},{16,24},{20,4},{24,16},{28,12},{1,9},{5... | collective-permute-start | bytes 737288 | tf_op jit(solution)/shard_map/ppermute | solution.py:372
  44.2 9.9 %collective-permute-start.17 = (bf16[64,1920]{1,0:T(8,128)(2,1)S(1)}, bf16[64,1920]{1,0:T(8,128)(2,1)S(1)}, u32[]{:S(2)}, u32[]{:S(2)}) collective-permute-start(bf16[64,1920]{1,0:T(8,128)(2,1)S(1)} %collective-permute-done.4), channel_id=1, source_target_pairs={{0,1},{1,0},{2,3},{3,2},{4,5},{5,4},{6,7},{7,6},{8,9},{9,8},{10,11... | collective-permute-start | bytes 737288 | tf_op jit(solution)/shard_map/ppermute | solution.py:369
  44.4 3.3 %copy-start.6 = (bf16[1792,512]{1,0:T(8,128)(2,1)S(1)}, bf16[1792,512]{1,0:T(8,128)(2,1)}, u32[]{:S(2)}) copy-start(bf16[1792,512]{1,0:T(8,128)(2,1)} %copy-done.5) | copy-start | bytes 5505028
  44.4 3.2 %copy-start.4 = (bf16[1792,512]{1,0:T(8,128)(2,1)S(1)}, bf16[1792,512]{1,0:T(8,128)(2,1)}, u32[]{:S(2)}) copy-start(bf16[1792,512]{1,0:T(8,128)(2,1)} %copy-done.3) | copy-start | bytes 5505028
  44.5 5.3 %collective-permute-start.9 = (bf16[128,1920]{1,0:T(8,128)(2,1)S(1)}, bf16[128,1920]{1,0:T(8,128)(2,1)S(1)}, u32[]{:S(2)}, u32[]{:S(2)}) collective-permute-start(bf16[128,1920]{1,0:T(8,128)(2,1)S(1)} %pad_maximum_fusion.2), channel_id=1, source_target_pairs={{0,4},{4,0},{8,12},{12,8},{16,20},{20,16},{24,28},{28,24},{1,5},{5... | collective-permute-start | bytes 1474568 | tf_op jit(solution)/shard_map/ppermute | solution.py:372
  44.6 2.2 %collective-permute-start.12 = (bf16[64,1920]{1,0:T(8,128)(2,1)S(1)}, bf16[64,1920]{1,0:T(8,128)(2,1)S(1)}, u32[]{:S(2)}, u32[]{:S(2)}) collective-permute-start(bf16[64,1920]{1,0:T(8,128)(2,1)S(1)} %collective-permute-done.7), channel_id=1, source_target_pairs={{0,4},{4,0},{8,12},{12,8},{16,20},{20,16},{24,28},{28,24},{1,5},{5... | collective-permute-start | bytes 737288 | tf_op jit(solution)/shard_map/ppermute | solution.py:372
  45.2 8.9 %collective-permute-start.8 = (bf16[128,1920]{1,0:T(8,128)(2,1)S(1)}, bf16[128,1920]{1,0:T(8,128)(2,1)S(1)}, u32[]{:S(2)}, u32[]{:S(2)}) collective-permute-start(bf16[128,1920]{1,0:T(8,128)(2,1)S(1)} %pad_maximum_fusion.2), channel_id=1, source_target_pairs={{0,8},{4,20},{8,0},{12,28},{16,24},{20,4},{24,16},{28,12},{1,9},{5... | collective-permute-start | bytes 1474568 | tf_op jit(solution)/shard_map/ppermute | solution.py:372
  45.8 1.9 %collective-permute-start.14 = (bf16[64,1920]{1,0:T(8,128)(2,1)S(1)}, bf16[64,1920]{1,0:T(8,128)(2,1)S(1)}, u32[]{:S(2)}, u32[]{:S(2)}) collective-permute-start(bf16[64,1920]{1,0:T(8,128)(2,1)S(1)} %collective-permute-done.13), channel_id=1, source_target_pairs={{0,4},{4,0},{8,12},{12,8},{16,20},{20,16},{24,28},{28,24},{1,5},{5... | collective-permute-start | bytes 737288 | tf_op jit(solution)/shard_map/ppermute | solution.py:372
  49.8 9.5 %collective-permute-start.10 = (bf16[128,1920]{1,0:T(8,128)(2,1)S(1)}, bf16[128,1920]{1,0:T(8,128)(2,1)S(1)}, u32[]{:S(2)}, u32[]{:S(2)}) collective-permute-start(bf16[128,1920]{1,0:T(8,128)(2,1)S(1)} %collective-permute-done.9), channel_id=1, source_target_pairs={{0,8},{4,20},{8,0},{12,28},{16,24},{20,4},{24,16},{28,12},{1,9},{5... | collective-permute-start | bytes 1474568 | tf_op jit(solution)/shard_map/ppermute | solution.py:372
  54.1 7.5 %collective-permute-start.24 = (bf16[128,1920]{1,0:T(8,128)(2,1)S(1)}, bf16[128,1920]{1,0:T(8,128)(2,1)S(1)}, u32[]{:S(2)}, u32[]{:S(2)}) collective-permute-start(bf16[128,1920]{1,0:T(8,128)(2,1)S(1)} %collective-permute-done.8), channel_id=1, source_target_pairs={{0,4},{4,0},{8,12},{12,8},{16,20},{20,16},{24,28},{28,24},{1,5},{5... | collective-permute-start | bytes 1474568 | tf_op jit(solution)/shard_map/ppermute | solution.py:372
  59.4 7.3 %collective-permute-start.19 = (bf16[64,1920]{1,0:T(8,128)(2,1)S(1)}, bf16[64,1920]{1,0:T(8,128)(2,1)S(1)}, u32[]{:S(2)}, u32[]{:S(2)}) collective-permute-start(bf16[64,1920]{1,0:T(8,128)(2,1)S(1)} %collective-permute-done.17), channel_id=1, source_target_pairs={{0,4},{4,0},{8,12},{12,8},{16,20},{20,16},{24,28},{28,24},{1,5},{5... | collective-permute-start | bytes 737288 | tf_op jit(solution)/shard_map/ppermute | solution.py:372
  59.4 8.8 %collective-permute-start.18 = (bf16[64,1920]{1,0:T(8,128)(2,1)S(1)}, bf16[64,1920]{1,0:T(8,128)(2,1)S(1)}, u32[]{:S(2)}, u32[]{:S(2)}) collective-permute-start(bf16[64,1920]{1,0:T(8,128)(2,1)S(1)} %collective-permute-done.17), channel_id=1, source_target_pairs={{0,8},{4,20},{8,0},{12,28},{16,24},{20,4},{24,16},{28,12},{1,9},{5... | collective-permute-start | bytes 737288 | tf_op jit(solution)/shard_map/ppermute | solution.py:372
  60.0 14.9 %collective-permute-start.15 = (bf16[128,1920]{1,0:T(8,128)(2,1)S(1)}, bf16[128,1920]{1,0:T(8,128)(2,1)S(1)}, u32[]{:S(2)}, u32[]{:S(2)}) collective-permute-start(bf16[128,1920]{1,0:T(8,128)(2,1)S(1)} %collective-permute-done.8), channel_id=1, source_target_pairs={{0,16},{4,12},{8,24},{12,4},{16,0},{20,28},{24,8},{28,20},{1,17},{... | collective-permute-start | bytes 1474568 | tf_op jit(solution)/shard_map/ppermute | solution.py:372
  61.6 13.3 %collective-permute-start.25 = (bf16[128,1920]{1,0:T(8,128)(2,1)S(1)}, bf16[128,1920]{1,0:T(8,128)(2,1)S(1)}, u32[]{:S(2)}, u32[]{:S(2)}) collective-permute-start(bf16[128,1920]{1,0:T(8,128)(2,1)S(1)} %collective-permute-done.10), channel_id=1, source_target_pairs={{0,4},{4,0},{8,12},{12,8},{16,20},{20,16},{24,28},{28,24},{1,5},{5... | collective-permute-start | bytes 1474568 | tf_op jit(solution)/shard_map/ppermute | solution.py:372
  66.6 7.0 %collective-permute-start.20 = (bf16[64,1920]{1,0:T(8,128)(2,1)S(1)}, bf16[64,1920]{1,0:T(8,128)(2,1)S(1)}, u32[]{:S(2)}, u32[]{:S(2)}) collective-permute-start(bf16[64,1920]{1,0:T(8,128)(2,1)S(1)} %collective-permute-done.19), channel_id=1, source_target_pairs={{0,8},{4,20},{8,0},{12,28},{16,24},{20,4},{24,16},{28,12},{1,9},{5... | collective-permute-start | bytes 737288 | tf_op jit(solution)/shard_map/ppermute | solution.py:372
  68.2 6.6 %collective-permute-start.22 = (bf16[64,1920]{1,0:T(8,128)(2,1)S(1)}, bf16[64,1920]{1,0:T(8,128)(2,1)S(1)}, u32[]{:S(2)}, u32[]{:S(2)}) collective-permute-start(bf16[64,1920]{1,0:T(8,128)(2,1)S(1)} %collective-permute-done.18), channel_id=1, source_target_pairs={{0,4},{4,0},{8,12},{12,8},{16,20},{20,16},{24,28},{28,24},{1,5},{5... | collective-permute-start | bytes 737288 | tf_op jit(solution)/shard_map/ppermute | solution.py:372
  73.6 6.2 %collective-permute-start.21 = (bf16[64,1920]{1,0:T(8,128)(2,1)S(1)}, bf16[64,1920]{1,0:T(8,128)(2,1)S(1)}, u32[]{:S(2)}, u32[]{:S(2)}) collective-permute-start(bf16[64,1920]{1,0:T(8,128)(2,1)S(1)} %collective-permute-done.18), channel_id=1, source_target_pairs={{0,16},{4,12},{8,24},{12,4},{16,0},{20,28},{24,8},{28,20},{1,17},{... | collective-permute-start | bytes 737288 | tf_op jit(solution)/shard_map/ppermute | solution.py:372
  74.8 1.5 %collective-permute-start.23 = (bf16[64,1920]{1,0:T(8,128)(2,1)S(1)}, bf16[64,1920]{1,0:T(8,128)(2,1)S(1)}, u32[]{:S(2)}, u32[]{:S(2)}) collective-permute-start(bf16[64,1920]{1,0:T(8,128)(2,1)S(1)} %collective-permute-done.20), channel_id=1, source_target_pairs={{0,4},{4,0},{8,12},{12,8},{16,20},{20,16},{24,28},{28,24},{1,5},{5... | collective-permute-start | bytes 737288 | tf_op jit(solution)/shard_map/ppermute | solution.py:372
  74.9 6.4 %collective-permute-start.16 = (bf16[128,1920]{1,0:T(8,128)(2,1)S(1)}, bf16[128,1920]{1,0:T(8,128)(2,1)S(1)}, u32[]{:S(2)}, u32[]{:S(2)}) collective-permute-start(bf16[128,1920]{1,0:T(8,128)(2,1)S(1)} %collective-permute-done.15), channel_id=1, source_target_pairs={{0,4},{4,0},{8,12},{12,8},{16,20},{20,16},{24,28},{28,24},{1,5},{5... | collective-permute-start | bytes 1474568 | tf_op jit(solution)/shard_map/ppermute | solution.py:372
  79.8 1.5 %collective-permute-start.26 = (bf16[64,1920]{1,0:T(8,128)(2,1)S(1)}, bf16[64,1920]{1,0:T(8,128)(2,1)S(1)}, u32[]{:S(2)}, u32[]{:S(2)}) collective-permute-start(bf16[64,1920]{1,0:T(8,128)(2,1)S(1)} %collective-permute-done.21), channel_id=1, source_target_pairs={{0,4},{4,0},{8,12},{12,8},{16,20},{20,16},{24,28},{28,24},{1,5},{5... | collective-permute-start | bytes 737288 | tf_op jit(solution)/shard_map/ppermute | solution.py:372
  84.6 10.9 %copy-start.2 = (f32[64,2]{0,1:T(2,128)S(1)}, f32[64,2]{0,1:T(2,128)}, u32[]{:S(2)}) copy-start(f32[64,2]{0,1:T(2,128)} %param.11) | copy-start | bytes 1540
  84.6 10.2 %all-to-all-start = ((f32[32,2,128]{2,1,0:T(2,128)}), f32[32,2,128]{2,1,0:T(2,128)S(1)}, u32[]{:S(2)}, u32[]{:S(2)}) async-start(f32[32,2,128]{2,1,0:T(2,128)} %get-tuple-element.51), calls=%async_computation | async-start | bytes 65536 | tf_op jit(solution)/shard_map/all_to_all | solution.py:439
  94.9 0.6 copy-start.8

commit v5 on v4

--- a/solution.py
+++ b/solution.py
@@ -407,14 +407,13 @@
     def tied(x, *values):
         return lax.optimization_barrier((x, *values))[0]
 
-    def most(near, beside):
-        return (*near, *beside, *map(other_core, beside))
-
     near = own, other_core(own)
-    beside = next_chip(near[0]), next_chip(near[1])
+    beside_x = next_chip(near[0])
+    beside = beside_x, next_chip(tied(near[1], beside_x))
     across = opposite(beside[0])
-    rows = jnp.concatenate([*most(near, beside), across, other_core(across)], axis=0)
+    rows = jnp.concatenate([*near, *beside, *map(other_core, beside), across, other_core(across)], axis=0)
     first_sums = first_product(rows, slabs)
+    across_far = over_z(across, 2)
 
     def of_quarters(parts):
         return [jnp.concatenate([x[q * tok : (q + 1) * tok] for x in parts], axis=0) for q in range(2)]
@@ -422,18 +421,21 @@
     pair = tied(jnp.concatenate([z_near, z_far], axis=0), *beside)
     near = pair, other_core(pair)
     beside = next_chip(near[0]), next_chip(near[1])
-    across = opposite(tied(*beside, *first_sums))
-    slabs, sums = add_product(numbers, w, wq, of_quarters((*near, *beside)), width, first_sums)
-    rest = of_quarters(list(map(other_core, beside)))
+    across = opposite(tied(beside[0], beside[1], *first_sums))
+    ready = of_quarters((*near, *beside))
+    ready[0] = tied(ready[0], z_both)
+    slabs, sums = add_product(numbers, w, wq, ready, width, first_sums)
+    rest = of_quarters([other_core(x) for x in beside])
     last = of_quarters((across, other_core(across)))
 
     single = tied(z_both, beside[1])
+    across_far = tied(across_far, beside[1])
     near = single, other_core(single)
     beside = next_chip(near[0]), next_chip(near[1])
-    across = opposite(tied(*beside, *sums))
-    most3 = jnp.concatenate(most(near, beside), axis=0)
-    early = early_stats(numbers, most3, rest, slabs, sums, first_sums)
-    last.append(jnp.concatenate([across, other_core(tied(across, early))], axis=0))
+    across = over_z(across_far, 1)
+    most = jnp.concatenate([*near, *beside, *map(other_core, beside)], axis=0)
+    early = early_stats(numbers, most, rest, slabs, sums, first_sums)
+    last.append(jnp.concatenate([across, other_core(across)], axis=0))
     late, payload = late_stats(numbers, last, slabs, first_sums, early, tok, n_z)
 
     back = lax.all_to_all(payload, ("expert", "tensor"), split_axis=0, concat_axis=0, tiled=True)

time: 97.1 us -> 95.3 us (0.981)
  waiting for transfers between devices: 44.7 us -> 41.7 us
  starting transfers between devices: 25.2 us -> 26.4 us
    ppermute x21 -> x20, waiting for transfers between devices: 18.3 us -> 14.7 us  [in_plane(): lax.ppermute(x, 'expert', [(i, i ^ (one if i & 1 else zero)) for i in ran...]
    ppermute x6 -> x8, starting transfers between devices: 8.8 us -> 11.5 us  [over_z(): return lax.ppermute(x, 'tensor', [(i, i ^ k) for i in range(n_z)])]
    ppermute x21 -> x20, starting transfers between devices: 13.5 us -> 12.1 us  [in_plane(): lax.ppermute(x, 'expert', [(i, i ^ (one if i & 1 else zero)) for i in ran...]
    ppermute x6 -> x8, waiting for transfers between devices: 20.4 us -> 21 us  [over_z(): return lax.ppermute(x, 'tensor', [(i, i ^ k) for i in range(n_z)])]
  transfers between devices with their start and end apart: 28 -> 29, of which waited for: 13 -> 12; matrix products, arithmetic and copies ran while one was open for 1% -> 1% of each run, Pallas kernels for 15% -> 15%
where the time goes in v5:
time: 95.3 us; the launch traced here: 95 us
  waiting for transfers between devices  41.7 us (44%)
  starting transfers between devices  26.4 us (28%)
  Pallas kernels  18.6 us (20%)
  local copies, waits for them, and re-layouts  5.61 us (6%)
  other arithmetic  1.64 us (2%)
  between operations  1.04 us (1%)
    ppermute x8, waiting for transfers between devices, over_z(): return lax.ppermute(x, 'tensor', [(i, i ^ k) for i in range(n_z)])  21 us
    ppermute x20, waiting for transfers between devices, in_plane(): lax.ppermute(x, 'expert', [(i, i ^ (one if i & 1 else zero)) for i in ran...  14.7 us
    ppermute x20, starting transfers between devices, in_plane(): lax.ppermute(x, 'expert', [(i, i ^ (one if i & 1 else zero)) for i in ran...  12.1 us
    ppermute x8, starting transfers between devices, over_z(): return lax.ppermute(x, 'tensor', [(i, i ^ k) for i in range(n_z)])  11.5 us
    all_to_all x1, waiting for transfers between devices, line_device(): lax.all_to_all(payload, ('expert', 'tensor'), split_axis=0, concat_axis=0...  6.07 us
    pallas_call x1, Pallas kernels, add_product(): pl.pallas_call(kernel, in_specs=[SMEM_SPEC, HBM_SPEC, HBM_SPEC] + [VMEM_S...  4.81 us
    pallas_call x1, Pallas kernels, early_stats(): pl.pallas_call(kernel, in_specs=[SMEM_SPEC] + [VMEM_SPEC] * len(args), ou...  3.44 us
    unnamed x32, local copies, waits for them, and re-layouts  3.43 us
  transfers between devices with their start and end apart: 29, of which 12 were waited for; matrix products, arithmetic and copies ran while one was open for 1% of the time, Pallas kernels for 15%

profile of v5, /device:TPU:0, one launch (start us, length us, event | category | flops | bytes accessed | tf_op | source)
XLA Modules:
  0.0 95.0 jit_solution(9025309675950092751)
XLA Ops:
  0.7 1.2 %dynamic-slice_bitcast_fusion.2 = (bf16[64,1792]{1,0:T(8,128)(2,1)S(1)}, bf16[64,1792]{1,0:T(8,128)(2,1)S(1)}, bf16[64,1792]{1,0:T(8,128)(2,1)S(1)}) fusion(bf16[1,64,7168]{2,1,0:T(8,128)(2,1)} %param.8, s32[]{:T(128)S(6)} %select_n.13, s32[]{:T(128)S(6)} %select_n.15, s32[]{:T(128)S(6)} %select_n.14), kind=kLoop, calls=%fused_computation.16 | loop fusion | bytes 1376268 | tf_op jit(solution)/shard_map/dynamic_slice | solution.py:375
  1.9 5.1 %collective-permute-start = (bf16[64,1792]{1,0:T(8,128)(2,1)S(1)}, bf16[64,1792]{1,0:T(8,128)(2,1)S(1)}, u32[]{:S(2)}, u32[]{:S(2)}) collective-permute-start(bf16[64,1792]{1,0:T(8,128)(2,1)S(1)} %get-tuple-element.59), channel_id=1, source_target_pairs={{0,3},{1,2},{2,1},{3,0},{4,7},{5,6},{6,5},{7,4},{8,11},{9,10},{10,... | collective-permute-start | bytes 688136 | tf_op jit(solution)/shard_map/ppermute | solution.py:369
  7.0 0.0 collective-permute-start.1
  7.0 0.6 collective-permute-start.2
  7.6 0.1 stack.23.numbers_ref
  7.7 2.6 %shard_map.94 = (bf16[1792,512]{1,0:T(8,128)(2,1)S(1)}, bf16[1792,512]{1,0:T(8,128)(2,1)S(1)}) custom-call(s32[5]{0:T(128)S(1)} %stack.23.numbers_ref, bf16[7168,512]{1,0:T(8,128)(2,1)} %bitcast.30, bf16[7168,512]{1,0:T(8,128)(2,1)} %bitcast.32), custom_call_target="tpu_custom_call" | custom-call | bytes 3670016 | tf_op jit(solution)/shard_map/pallas_call | solution.py:109
  10.4 1.3 %copy-done.3 = bf16[1792,512]{1,0:T(8,128)(2,1)} copy-done((bf16[1792,512]{1,0:T(8,128)(2,1)}, bf16[1792,512]{1,0:T(8,128)(2,1)S(1)}, u32[]{:S(2)}) %copy-start.3) | copy-done | bytes 1835032
  11.6 1.2 %copy-done.5 = bf16[1792,512]{1,0:T(8,128)(2,1)} copy-done((bf16[1792,512]{1,0:T(8,128)(2,1)}, bf16[1792,512]{1,0:T(8,128)(2,1)S(1)}, u32[]{:S(2)}) %copy-start.5) | copy-done | bytes 1835032
  12.9 0.1 copy.16
  13.0 0.6 collective-permute-done
  13.6 12.9 %collective-permute-done.1 = bf16[64,1792]{1,0:T(8,128)(2,1)S(1)} collective-permute-done((bf16[64,1792]{1,0:T(8,128)(2,1)S(1)}, bf16[64,1792]{1,0:T(8,128)(2,1)S(1)}, u32[]{:S(2)}, u32[]{:S(2)}) %collective-permute-start.1) | collective-permute-done | bytes 229408 | tf_op jit(solution)/shard_map/ppermute | solution.py:369
  26.5 0.0 collective-permute-done.2
  26.5 1.2 %multiply_reduce_fusion = (f32[64]{0:T(128)S(1)}, bf16[64,1792]{1,0:T(8,128)(2,1)S(1)}) fusion(bf16[64,1792]{1,0:T(8,128)(2,1)S(1)} %collective-permute-done.2, bf16[64,1792]{1,0:T(8,128)(2,1)S(1)} %collective-permute-done.1, bf16[64,1792]{1,0:T(8,128)(2,1)S(1)} %collective-permute-done, bf16[1,64,7168]{2,1,0:T(8,128)(2,1)} %param.8, s32[]{:T(128)S(6)} %select_n.12, ...), kind=kLoop, calls=%fused_computation.12 | loop fusion | flops 1490880 | bytes 1383684 | tf_op jit(solution)/shard_map/reduce_sum | solution.py:386
  27.7 0.1 copy.14
  27.8 0.1 copy.13
  27.9 0.1 copy.15
  28.1 0.1 concatenate.36
  28.2 1.6 %collective-permute-start.5 = (bf16[64,1920]{1,0:T(8,128)(2,1)S(1)}, bf16[64,1920]{1,0:T(8,128)(2,1)S(1)}, u32[]{:S(2)}, u32[]{:S(2)}) collective-permute-start(bf16[64,1920]{1,0:T(8,128)(2,1)S(1)} %concatenate.36), channel_id=1, source_target_pairs={{0,8},{4,20},{8,0},{12,28},{16,24},{20,4},{24,16},{28,12},{1,9},{5... | collective-permute-start | bytes 737288 | tf_op jit(solution)/shard_map/ppermute | solution.py:372
  29.8 3.0 %collective-permute-start.3 = (bf16[64,1920]{1,0:T(8,128)(2,1)S(1)}, bf16[64,1920]{1,0:T(8,128)(2,1)S(1)}, u32[]{:S(2)}, u32[]{:S(2)}) collective-permute-start(bf16[64,1920]{1,0:T(8,128)(2,1)S(1)} %concatenate.36), channel_id=1, source_target_pairs={{0,1},{1,0},{2,3},{3,2},{4,5},{5,4},{6,7},{7,6},{8,9},{9,8},{10,11... | collective-permute-start | bytes 737288 | tf_op jit(solution)/shard_map/ppermute | solution.py:369
  32.8 1.6 %collective-permute-done.5 = bf16[64,1920]{1,0:T(8,128)(2,1)S(1)} collective-permute-done((bf16[64,1920]{1,0:T(8,128)(2,1)S(1)}, bf16[64,1920]{1,0:T(8,128)(2,1)S(1)}, u32[]{:S(2)}, u32[]{:S(2)}) %collective-permute-start.5) | collective-permute-done | bytes 245792 | tf_op jit(solution)/shard_map/ppermute | solution.py:372
  34.5 0.0 collective-permute-done.6
  34.5 1.5 %collective-permute-start.7 = (bf16[64,1920]{1,0:T(8,128)(2,1)S(1)}, bf16[64,1920]{1,0:T(8,128)(2,1)S(1)}, u32[]{:S(2)}, u32[]{:S(2)}) collective-permute-start(bf16[64,1920]{1,0:T(8,128)(2,1)S(1)} %collective-permute-done.6), channel_id=1, source_target_pairs={{0,8},{4,20},{8,0},{12,28},{16,24},{20,4},{24,16},{28,12},{1,9},{5... | collective-permute-start | bytes 737288 | tf_op jit(solution)/shard_map/ppermute | solution.py:372
  36.0 1.5 %collective-permute-start.13 = (bf16[64,1920]{1,0:T(8,128)(2,1)S(1)}, bf16[64,1920]{1,0:T(8,128)(2,1)S(1)}, u32[]{:S(2)}, u32[]{:S(2)}) collective-permute-start(bf16[64,1920]{1,0:T(8,128)(2,1)S(1)} %collective-permute-done.5), channel_id=1, source_target_pairs={{0,16},{4,12},{8,24},{12,4},{16,0},{20,28},{24,8},{28,20},{1,17},{... | collective-permute-start | bytes 737288 | tf_op jit(solution)/shard_map/ppermute | solution.py:372
  37.5 6.7 %collective-permute-done.4 = bf16[64,1920]{1,0:T(8,128)(2,1)S(1)} collective-permute-done((bf16[64,1920]{1,0:T(8,128)(2,1)S(1)}, bf16[64,1920]{1,0:T(8,128)(2,1)S(1)}, u32[]{:S(2)}, u32[]{:S(2)}) %collective-permute-start.4) | collective-permute-done | bytes 245792 | tf_op jit(solution)/shard_map/ppermute | solution.py:369
  44.2 0.0 collective-permute-start.20
  44.3 0.1 collective-permute-done.3
  44.4 0.0 collective-permute-done.7
  44.5 0.1 collective-permute-start.9
  44.6 0.6 collective-permute-start.12
  45.2 0.0 collective-permute-done.11
  45.2 0.6 collective-permute-start.8
  45.8 0.0 collective-permute-done.13
  45.8 0.7 collective-permute-start.14
  46.5 0.2 collective-permute-done.12
  46.7 1.8 %collective-permute-start.17 = (bf16[64,1920]{1,0:T(8,128)(2,1)S(1)}, bf16[64,1920]{1,0:T(8,128)(2,1)S(1)}, u32[]{:S(2)}, u32[]{:S(2)}) collective-permute-start(bf16[64,1920]{1,0:T(8,128)(2,1)S(1)} %collective-permute-done.13), channel_id=1, source_target_pairs={{0,2},{1,3},{2,0},{3,1},{4,6},{5,7},{6,4},{7,5},{8,10},{9,11},{10,... | collective-permute-start | bytes 737288 | tf_op jit(solution)/shard_map/ppermute | solution.py:369
  48.6 0.0 collective-permute-done.14
  48.7 2.1 %shard_map.95 = (f32[512,512]{1,0:T(8,128)S(1)}, f32[512,512]{1,0:T(8,128)S(1)}, f32[512,128]{1,0:T(8,128)S(1)}) custom-call(bf16[512,1920]{1,0:T(8,128)(2,1)S(1)} %constant_dynamic-update-slice_fusion.rows_ref, bf16[1792,512]{1,0:T(8,128)(2,1)S(1)} %copy-done.4, bf16[1792,512]{1,0:T(8,128)(2,1)S(1)} %copy-done.6), custom_call_target="tpu_custom_call" | custom-call | flops 1879048192 | bytes 3670016 | tf_op jit(solution)/shard_map/pallas_call | solution.py:133
  50.8 0.0 collective-permute-done.9
  50.8 0.7 collective-permute-start.10
  51.5 2.6 %collective-permute-done.8 = bf16[128,1920]{1,0:T(8,128)(2,1)S(1)} collective-permute-done((bf16[128,1920]{1,0:T(8,128)(2,1)S(1)}, bf16[128,1920]{1,0:T(8,128)(2,1)S(1)}, u32[]{:S(2)}, u32[]{:S(2)}) %collective-permute-start.8) | collective-permute-done | bytes 491552 | tf_op jit(solution)/shard_map/ppermute | solution.py:372
  54.1 5.6 %collective-permute-done.10 = bf16[128,1920]{1,0:T(8,128)(2,1)S(1)} collective-permute-done((bf16[128,1920]{1,0:T(8,128)(2,1)S(1)}, bf16[128,1920]{1,0:T(8,128)(2,1)S(1)}, u32[]{:S(2)}, u32[]{:S(2)}) %collective-permute-start.10) | collective-permute-done | bytes 491552 | tf_op jit(solution)/shard_map/ppermute | solution.py:372
  59.7 0.6 collective-permute-start.22
  60.3 0.6 collective-permute-done.17
  60.9 0.9 collective-permute-start.18
  61.8 1.5 %collective-permute-start.15 = (bf16[128,1920]{1,0:T(8,128)(2,1)S(1)}, bf16[128,1920]{1,0:T(8,128)(2,1)S(1)}, u32[]{:S(2)}, u32[]{:S(2)}) collective-permute-start(bf16[128,1920]{1,0:T(8,128)(2,1)S(1)} %collective-permute-done.8), channel_id=1, source_target_pairs={{0,16},{4,12},{8,24},{12,4},{16,0},{20,28},{24,8},{28,20},{1,17},{... | collective-permute-start | bytes 1474568 | tf_op jit(solution)/shard_map/ppermute | solution.py:372
  63.4 0.1 pad_maximum_fusion.refs_0_
  63.5 0.1 collective-permute-start.27
  63.6 0.1 pad_maximum_fusion.1.refs_1_
  63.7 4.8 %shard_map.96 = (f32[256,512]{1,0:T(8,128)S(1)}, f32[256,512]{1,0:T(8,128)S(1)}, f32[256,128]{1,0:T(8,128)S(1)}, bf16[1792,512]{1,0:T(8,128)(2,1)S(1)}, bf16[179...) custom-call(s32[5]{0:T(128)S(1)} %stack.23.numbers_ref, ...), custom_call_target="tpu_custom_call" | custom-call | flops 1879048192 | bytes 3670016 | tf_op jit(solution)/shard_map/pallas_call | solution.py:174
  68.5 1.6 %collective-permute-start.23 = (bf16[64,1920]{1,0:T(8,128)(2,1)S(1)}, bf16[64,1920]{1,0:T(8,128)(2,1)S(1)}, u32[]{:S(2)}, u32[]{:S(2)}) collective-permute-start(bf16[64,1920]{1,0:T(8,128)(2,1)S(1)} %collective-permute-done.21), channel_id=1, source_target_pairs={{0,8},{4,20},{8,0},{12,28},{16,24},{20,4},{24,16},{28,12},{1,9},{5... | collective-permute-start | bytes 737288 | tf_op jit(solution)/shard_map/ppermute | solution.py:372
  70.1 0.1 collective-permute-start.24
  70.2 0.5 collective-permute-start.19
  70.7 4.1 %collective-permute-done.23 = bf16[64,1920]{1,0:T(8,128)(2,1)S(1)} collective-permute-done((bf16[64,1920]{1,0:T(8,128)(2,1)S(1)}, bf16[64,1920]{1,0:T(8,128)(2,1)S(1)}, u32[]{:S(2)}, u32[]{:S(2)}) %collective-permute-start.23) | collective-permute-done | bytes 245792 | tf_op jit(solution)/shard_map/ppermute | solution.py:372
  74.9 0.6 collective-permute-start.16
  75.6 0.1 pad_maximum_fusion.6
  75.7 0.6 collective-permute-done.25
  76.3 3.4 %shard_map.97.refs_12_.early_ref = f32[8,384]{1,0:T(8,128)S(1)} custom-call(s32[5]{0:T(128)S(1)} %stack.23.numbers_ref, bf16[384,1920]{1,0:T(8,128)(2,1)S(1)} %constant_dynamic-update-slice_fusion.8.rows_ref, bf16[128,1920]{1,0:T(8,128)(2,1)S(1)} %get-tuple-element.84.refs_0_, bf16[128,1920]{1,0:T(8,128)(2,1)S(1)} %get-tuple-element.85.refs_1_, ...), custom_call_target="tpu_custom_call" | custom-call | flops 1409286144 | bytes 3670016 | tf_op jit(solution)/shard_map/pallas_call | solution.py:239
  79.8 0.1 pad_maximum_fusion.3
  79.9 3.1 %shard_map.98 = (f32[8,128]{1,0:T(8,128)S(1)}, f32[32,2,128]{2,1,0:T(2,128)}) custom-call(s32[5]{0:T(128)S(1)} %stack.23.numbers_ref, bf16[128,1920]{1,0:T(8,128)(2,1)S(1)} %get-tuple-element.82.refs_0_, bf16[128,1920]{1,0:T(8,128)(2,1)S(1)} %get-tuple-element.83.refs_1_, bf16[128,1920]{1,0:T(8,128)(2,1)S(1)} %pad_maximum_fusion.5.refs_2_, ...), custom_call_target="tpu_custom_call" | custom-call | flops 469762048 | bytes 3670016 | tf_op jit(solution)/shard_map/pallas_call | solution.py:285
  83.0 2.8 %all-to-all-start = ((f32[32,2,128]{2,1,0:T(2,128)}), f32[32,2,128]{2,1,0:T(2,128)S(1)}, u32[]{:S(2)}, u32[]{:S(2)}) async-start(f32[32,2,128]{2,1,0:T(2,128)} %get-tuple-element.53), calls=%async_computation | async-start | bytes 65536 | tf_op jit(solution)/shard_map/all_to_all | solution.py:441
  85.8 1.2 %shard_map.100 = f32[1,1792]{1,0:T(1,128)} custom-call(bf16[512,1920]{1,0:T(8,128)(2,1)S(1)} %constant_dynamic-update-slice_fusion.rows_ref, f32[8,384]{1,0:T(8,128)S(1)} %shard_map.97.refs_12_.early_ref, f32[8,128]{1,0:T(8,128)S(1)} %get-tuple-element.56.late_ref), custom_call_target="tpu_custom_call" | custom-call | flops 3932160 | bytes 1966080 | tf_op jit(solution)/shard_map/pallas_call | solution.py:315
  87.0 6.1 %all-to-all-done.back_ref = f32[32,2,128]{2,1,0:T(2,128)S(1)} async-done(((f32[32,2,128]{2,1,0:T(2,128)}), f32[32,2,128]{2,1,0:T(2,128)S(1)}, u32[]{:S(2)}, u32[]{:S(2)}) %all-to-all-start) | async-done | bytes 32800 | tf_op jit(solution)/shard_map/all_to_all | solution.py:441
  93.1 0.6 copy-done.8
  93.7 1.4 %shard_map.99 = (f32[1,64]{1,0:T(1,128)}, f32[1,1]{1,0:T(1,128)}) custom-call(s32[5]{0:T(128)} %copy-done, f32[32,2,128]{2,1,0:T(2,128)} %copy-done.8, s32[2,64]{1,0:T(2,128)S(1)} %bitcast.28, f32[2,64]{1,0:T(2,128)S(1)} %bitcast.29), custom_call_target="tpu_custom_call" | custom-call | tf_op jit(solution)/shard_map/pallas_call | solution.py:347
  (62 shorter events, 0.8 us)
Async XLA Ops:
  1.9 11.7 %collective-permute-start = (bf16[64,1792]{1,0:T(8,128)(2,1)S(1)}, bf16[64,1792]{1,0:T(8,128)(2,1)S(1)}, u32[]{:S(2)}, u32[]{:S(2)}) collective-permute-start(bf16[64,1792]{1,0:T(8,128)(2,1)S(1)} %get-tuple-element.59), channel_id=1, source_target_pairs={{0,3},{1,2},{2,1},{3,0},{4,7},{5,6},{6,5},{7,4},{8,11},{9,10},{10,... | collective-permute-start | bytes 688136 | tf_op jit(solution)/shard_map/ppermute | solution.py:369
  7.0 19.5 %collective-permute-start.1 = (bf16[64,1792]{1,0:T(8,128)(2,1)S(1)}, bf16[64,1792]{1,0:T(8,128)(2,1)S(1)}, u32[]{:S(2)}, u32[]{:S(2)}) collective-permute-start(bf16[64,1792]{1,0:T(8,128)(2,1)S(1)} %get-tuple-element.61), channel_id=1, source_target_pairs={{0,2},{1,3},{2,0},{3,1},{4,6},{5,7},{6,4},{7,5},{8,10},{9,11},{10,... | collective-permute-start | bytes 688136 | tf_op jit(solution)/shard_map/ppermute | solution.py:369
  7.0 19.5 %collective-permute-start.2 = (bf16[64,1792]{1,0:T(8,128)(2,1)S(1)}, bf16[64,1792]{1,0:T(8,128)(2,1)S(1)}, u32[]{:S(2)}, u32[]{:S(2)}) collective-permute-start(bf16[64,1792]{1,0:T(8,128)(2,1)S(1)} %get-tuple-element.60), channel_id=1, source_target_pairs={{0,1},{1,0},{2,3},{3,2},{4,5},{5,4},{6,7},{7,6},{8,9},{9,8},{10,11... | collective-permute-start | bytes 688136 | tf_op jit(solution)/shard_map/ppermute | solution.py:369
  7.7 72.2 %copy-start = (s32[5]{0:T(128)}, s32[5]{0:T(128)S(1)}, u32[]{:S(2)}) copy-start(s32[5]{0:T(128)S(1)} %stack.23.numbers_ref) | copy-start | bytes 64
  7.7 5.2 %copy-start.9 = (bf16[1792]{0:T(1024)(128)(2,1)S(1)}, bf16[1792]{0:T(1024)(128)(2,1)}, u32[]{:S(2)}) copy-start(bf16[1792]{0:T(1024)(128)(2,1)} %param.9) | copy-start | bytes 10756
  7.7 5.2 %copy-start.1 = (s32[64,2]{0,1:T(2,128)S(1)}, s32[64,2]{0,1:T(2,128)}, u32[]{:S(2)}) copy-start(s32[64,2]{0,1:T(2,128)} %param.10) | copy-start | bytes 1540
  7.7 18.8 %copy-start.7 = (bf16[64,1792]{1,0:T(8,128)(2,1)S(1)}, bf16[64,1792]{1,0:T(8,128)(2,1)}, u32[]{:S(2)}) copy-start(bf16[64,1792]{1,0:T(8,128)(2,1)} %param.7) | copy-start | bytes 688132
  10.3 1.3 %copy-start.3 = (bf16[1792,512]{1,0:T(8,128)(2,1)}, bf16[1792,512]{1,0:T(8,128)(2,1)S(1)}, u32[]{:S(2)}) copy-start(bf16[1792,512]{1,0:T(8,128)(2,1)S(1)} %get-tuple-element.35.slab_ref) | copy-start | bytes 5505028
  11.6 1.2 %copy-start.5 = (bf16[1792,512]{1,0:T(8,128)(2,1)}, bf16[1792,512]{1,0:T(8,128)(2,1)S(1)}, u32[]{:S(2)}) copy-start(bf16[1792,512]{1,0:T(8,128)(2,1)S(1)} %get-tuple-element.36.slab_q_ref) | copy-start | bytes 5505028
  28.2 6.3 %collective-permute-start.5 = (bf16[64,1920]{1,0:T(8,128)(2,1)S(1)}, bf16[64,1920]{1,0:T(8,128)(2,1)S(1)}, u32[]{:S(2)}, u32[]{:S(2)}) collective-permute-start(bf16[64,1920]{1,0:T(8,128)(2,1)S(1)} %concatenate.36), channel_id=1, source_target_pairs={{0,8},{4,20},{8,0},{12,28},{16,24},{20,4},{24,16},{28,12},{1,9},{5... | collective-permute-start | bytes 737288 | tf_op jit(solution)/shard_map/ppermute | solution.py:372
  29.7 4.7 %collective-permute-start.6 = (bf16[64,1920]{1,0:T(8,128)(2,1)S(1)}, bf16[64,1920]{1,0:T(8,128)(2,1)S(1)}, u32[]{:S(2)}, u32[]{:S(2)}) collective-permute-start(bf16[64,1920]{1,0:T(8,128)(2,1)S(1)} %concatenate.36), channel_id=1, source_target_pairs={{0,4},{4,0},{8,12},{12,8},{16,20},{20,16},{24,28},{28,24},{1,5},{5... | collective-permute-start | bytes 737288 | tf_op jit(solution)/shard_map/ppermute | solution.py:372
  29.8 14.5 %collective-permute-start.4 = (bf16[64,1920]{1,0:T(8,128)(2,1)S(1)}, bf16[64,1920]{1,0:T(8,128)(2,1)S(1)}, u32[]{:S(2)}, u32[]{:S(2)}) collective-permute-start(bf16[64,1920]{1,0:T(8,128)(2,1)S(1)} %concatenate.36), channel_id=1, source_target_pairs={{0,2},{1,3},{2,0},{3,1},{4,6},{5,7},{6,4},{7,5},{8,10},{9,11},{10,... | collective-permute-start | bytes 737288 | tf_op jit(solution)/shard_map/ppermute | solution.py:369
  29.8 14.6 %collective-permute-start.3 = (bf16[64,1920]{1,0:T(8,128)(2,1)S(1)}, bf16[64,1920]{1,0:T(8,128)(2,1)S(1)}, u32[]{:S(2)}, u32[]{:S(2)}) collective-permute-start(bf16[64,1920]{1,0:T(8,128)(2,1)S(1)} %concatenate.36), channel_id=1, source_target_pairs={{0,1},{1,0},{2,3},{3,2},{4,5},{5,4},{6,7},{7,6},{8,9},{9,8},{10,11... | collective-permute-start | bytes 737288 | tf_op jit(solution)/shard_map/ppermute | solution.py:369
  34.5 10.0 %collective-permute-start.7 = (bf16[64,1920]{1,0:T(8,128)(2,1)S(1)}, bf16[64,1920]{1,0:T(8,128)(2,1)S(1)}, u32[]{:S(2)}, u32[]{:S(2)}) collective-permute-start(bf16[64,1920]{1,0:T(8,128)(2,1)S(1)} %collective-permute-done.6), channel_id=1, source_target_pairs={{0,8},{4,20},{8,0},{12,28},{16,24},{20,4},{24,16},{28,12},{1,9},{5... | collective-permute-start | bytes 737288 | tf_op jit(solution)/shard_map/ppermute | solution.py:372
  35.9 9.2 %collective-permute-start.11 = (bf16[64,1920]{1,0:T(8,128)(2,1)S(1)}, bf16[64,1920]{1,0:T(8,128)(2,1)S(1)}, u32[]{:S(2)}, u32[]{:S(2)}) collective-permute-start(bf16[64,1920]{1,0:T(8,128)(2,1)S(1)} %collective-permute-done.5), channel_id=1, source_target_pairs={{0,4},{4,0},{8,12},{12,8},{16,20},{20,16},{24,28},{28,24},{1,5},{5... | collective-permute-start | bytes 737288 | tf_op jit(solution)/shard_map/ppermute | solution.py:372
  36.0 9.8 %collective-permute-start.13 = (bf16[64,1920]{1,0:T(8,128)(2,1)S(1)}, bf16[64,1920]{1,0:T(8,128)(2,1)S(1)}, u32[]{:S(2)}, u32[]{:S(2)}) collective-permute-start(bf16[64,1920]{1,0:T(8,128)(2,1)S(1)} %collective-permute-done.5), channel_id=1, source_target_pairs={{0,16},{4,12},{8,24},{12,4},{16,0},{20,28},{24,8},{28,20},{1,17},{... | collective-permute-start | bytes 737288 | tf_op jit(solution)/shard_map/ppermute | solution.py:372
  44.2 9.9 %collective-permute-start.20 = (bf16[64,1920]{1,0:T(8,128)(2,1)S(1)}, bf16[64,1920]{1,0:T(8,128)(2,1)S(1)}, u32[]{:S(2)}, u32[]{:S(2)}) collective-permute-start(bf16[64,1920]{1,0:T(8,128)(2,1)S(1)} %collective-permute-done.4), channel_id=1, source_target_pairs={{0,1},{1,0},{2,3},{3,2},{4,5},{5,4},{6,7},{7,6},{8,9},{9,8},{10,11... | collective-permute-start | bytes 737288 | tf_op jit(solution)/shard_map/ppermute | solution.py:369
  44.4 4.3 %copy-start.6 = (bf16[1792,512]{1,0:T(8,128)(2,1)S(1)}, bf16[1792,512]{1,0:T(8,128)(2,1)}, u32[]{:S(2)}) copy-start(bf16[1792,512]{1,0:T(8,128)(2,1)} %copy-done.5) | copy-start | bytes 5505028
  44.4 4.2 %copy-start.4 = (bf16[1792,512]{1,0:T(8,128)(2,1)S(1)}, bf16[1792,512]{1,0:T(8,128)(2,1)}, u32[]{:S(2)}) copy-start(bf16[1792,512]{1,0:T(8,128)(2,1)} %copy-done.3) | copy-start | bytes 5505028
  44.5 6.3 %collective-permute-start.9 = (bf16[128,1920]{1,0:T(8,128)(2,1)S(1)}, bf16[128,1920]{1,0:T(8,128)(2,1)S(1)}, u32[]{:S(2)}, u32[]{:S(2)}) collective-permute-start(bf16[128,1920]{1,0:T(8,128)(2,1)S(1)} %pad_maximum_fusion.2), channel_id=1, source_target_pairs={{0,4},{4,0},{8,12},{12,8},{16,20},{20,16},{24,28},{28,24},{1,5},{5... | collective-permute-start | bytes 1474568 | tf_op jit(solution)/shard_map/ppermute | solution.py:372
  44.6 2.2 %collective-permute-start.12 = (bf16[64,1920]{1,0:T(8,128)(2,1)S(1)}, bf16[64,1920]{1,0:T(8,128)(2,1)S(1)}, u32[]{:S(2)}, u32[]{:S(2)}) collective-permute-start(bf16[64,1920]{1,0:T(8,128)(2,1)S(1)} %collective-permute-done.7), channel_id=1, source_target_pairs={{0,4},{4,0},{8,12},{12,8},{16,20},{20,16},{24,28},{28,24},{1,5},{5... | collective-permute-start | bytes 737288 | tf_op jit(solution)/shard_map/ppermute | solution.py:372
  45.2 8.9 %collective-permute-start.8 = (bf16[128,1920]{1,0:T(8,128)(2,1)S(1)}, bf16[128,1920]{1,0:T(8,128)(2,1)S(1)}, u32[]{:S(2)}, u32[]{:S(2)}) collective-permute-start(bf16[128,1920]{1,0:T(8,128)(2,1)S(1)} %pad_maximum_fusion.2), channel_id=1, source_target_pairs={{0,8},{4,20},{8,0},{12,28},{16,24},{20,4},{24,16},{28,12},{1,9},{5... | collective-permute-start | bytes 1474568 | tf_op jit(solution)/shard_map/ppermute | solution.py:372
  45.8 2.8 %collective-permute-start.14 = (bf16[64,1920]{1,0:T(8,128)(2,1)S(1)}, bf16[64,1920]{1,0:T(8,128)(2,1)S(1)}, u32[]{:S(2)}, u32[]{:S(2)}) collective-permute-start(bf16[64,1920]{1,0:T(8,128)(2,1)S(1)} %collective-permute-done.13), channel_id=1, source_target_pairs={{0,4},{4,0},{8,12},{12,8},{16,20},{20,16},{24,28},{28,24},{1,5},{5... | collective-permute-start | bytes 737288 | tf_op jit(solution)/shard_map/ppermute | solution.py:372
  46.7 14.2 %collective-permute-start.17 = (bf16[64,1920]{1,0:T(8,128)(2,1)S(1)}, bf16[64,1920]{1,0:T(8,128)(2,1)S(1)}, u32[]{:S(2)}, u32[]{:S(2)}) collective-permute-start(bf16[64,1920]{1,0:T(8,128)(2,1)S(1)} %collective-permute-done.13), channel_id=1, source_target_pairs={{0,2},{1,3},{2,0},{3,1},{4,6},{5,7},{6,4},{7,5},{8,10},{9,11},{10,... | collective-permute-start | bytes 737288 | tf_op jit(solution)/shard_map/ppermute | solution.py:369
  50.8 8.9 %collective-permute-start.10 = (bf16[128,1920]{1,0:T(8,128)(2,1)S(1)}, bf16[128,1920]{1,0:T(8,128)(2,1)S(1)}, u32[]{:S(2)}, u32[]{:S(2)}) collective-permute-start(bf16[128,1920]{1,0:T(8,128)(2,1)S(1)} %collective-permute-done.9), channel_id=1, source_target_pairs={{0,8},{4,20},{8,0},{12,28},{16,24},{20,4},{24,16},{28,12},{1,9},{5... | collective-permute-start | bytes 1474568 | tf_op jit(solution)/shard_map/ppermute | solution.py:372
  54.1 9.4 %collective-permute-start.26 = (bf16[128,1920]{1,0:T(8,128)(2,1)S(1)}, bf16[128,1920]{1,0:T(8,128)(2,1)S(1)}, u32[]{:S(2)}, u32[]{:S(2)}) collective-permute-start(bf16[128,1920]{1,0:T(8,128)(2,1)S(1)} %collective-permute-done.8), channel_id=1, source_target_pairs={{0,4},{4,0},{8,12},{12,8},{16,20},{20,16},{24,28},{28,24},{1,5},{5... | collective-permute-start | bytes 1474568 | tf_op jit(solution)/shard_map/ppermute | solution.py:372
  59.7 8.8 %collective-permute-start.21 = (bf16[64,1920]{1,0:T(8,128)(2,1)S(1)}, bf16[64,1920]{1,0:T(8,128)(2,1)S(1)}, u32[]{:S(2)}, u32[]{:S(2)}) collective-permute-start(bf16[64,1920]{1,0:T(8,128)(2,1)S(1)} %collective-permute-done.20), channel_id=1, source_target_pairs={{0,4},{4,0},{8,12},{12,8},{16,20},{20,16},{24,28},{28,24},{1,5},{5... | collective-permute-start | bytes 737288 | tf_op jit(solution)/shard_map/ppermute | solution.py:372
  59.7 10.4 %collective-permute-start.22 = (bf16[64,1920]{1,0:T(8,128)(2,1)S(1)}, bf16[64,1920]{1,0:T(8,128)(2,1)S(1)}, u32[]{:S(2)}, u32[]{:S(2)}) collective-permute-start(bf16[64,1920]{1,0:T(8,128)(2,1)S(1)} %collective-permute-done.20), channel_id=1, source_target_pairs={{0,8},{4,20},{8,0},{12,28},{16,24},{20,4},{24,16},{28,12},{1,9},{5... | collective-permute-start | bytes 737288 | tf_op jit(solution)/shard_map/ppermute | solution.py:372
  60.9 9.2 %collective-permute-start.18 = (bf16[64,1920]{1,0:T(8,128)(2,1)S(1)}, bf16[64,1920]{1,0:T(8,128)(2,1)S(1)}, u32[]{:S(2)}, u32[]{:S(2)}) collective-permute-start(bf16[64,1920]{1,0:T(8,128)(2,1)S(1)} %collective-permute-done.17), channel_id=1, source_target_pairs={{0,1},{1,0},{2,3},{3,2},{4,5},{5,4},{6,7},{7,6},{8,9},{9,8},{10,11... | collective-permute-start | bytes 737288 | tf_op jit(solution)/shard_map/ppermute | solution.py:369
  61.8 13.1 %collective-permute-start.15 = (bf16[128,1920]{1,0:T(8,128)(2,1)S(1)}, bf16[128,1920]{1,0:T(8,128)(2,1)S(1)}, u32[]{:S(2)}, u32[]{:S(2)}) collective-permute-start(bf16[128,1920]{1,0:T(8,128)(2,1)S(1)} %collective-permute-done.8), channel_id=1, source_target_pairs={{0,16},{4,12},{8,24},{12,4},{16,0},{20,28},{24,8},{28,20},{1,17},{... | collective-permute-start | bytes 1474568 | tf_op jit(solution)/shard_map/ppermute | solution.py:372
  63.5 12.0 %collective-permute-start.27 = (bf16[128,1920]{1,0:T(8,128)(2,1)S(1)}, bf16[128,1920]{1,0:T(8,128)(2,1)S(1)}, u32[]{:S(2)}, u32[]{:S(2)}) collective-permute-start(bf16[128,1920]{1,0:T(8,128)(2,1)S(1)} %collective-permute-done.10), channel_id=1, source_target_pairs={{0,4},{4,0},{8,12},{12,8},{16,20},{20,16},{24,28},{28,24},{1,5},{5... | collective-permute-start | bytes 1474568 | tf_op jit(solution)/shard_map/ppermute | solution.py:372
  68.5 6.3 %collective-permute-start.23 = (bf16[64,1920]{1,0:T(8,128)(2,1)S(1)}, bf16[64,1920]{1,0:T(8,128)(2,1)S(1)}, u32[]{:S(2)}, u32[]{:S(2)}) collective-permute-start(bf16[64,1920]{1,0:T(8,128)(2,1)S(1)} %collective-permute-done.21), channel_id=1, source_target_pairs={{0,8},{4,20},{8,0},{12,28},{16,24},{20,4},{24,16},{28,12},{1,9},{5... | collective-permute-start | bytes 737288 | tf_op jit(solution)/shard_map/ppermute | solution.py:372
  70.1 4.8 %collective-permute-start.24 = (bf16[64,1920]{1,0:T(8,128)(2,1)S(1)}, bf16[64,1920]{1,0:T(8,128)(2,1)S(1)}, u32[]{:S(2)}, u32[]{:S(2)}) collective-permute-start(bf16[64,1920]{1,0:T(8,128)(2,1)S(1)} %collective-permute-done.22), channel_id=1, source_target_pairs={{0,4},{4,0},{8,12},{12,8},{16,20},{20,16},{24,28},{28,24},{1,5},{5... | collective-permute-start | bytes 737288 | tf_op jit(solution)/shard_map/ppermute | solution.py:372
  70.2 4.6 %collective-permute-start.19 = (bf16[64,1920]{1,0:T(8,128)(2,1)S(1)}, bf16[64,1920]{1,0:T(8,128)(2,1)S(1)}, u32[]{:S(2)}, u32[]{:S(2)}) collective-permute-start(bf16[64,1920]{1,0:T(8,128)(2,1)S(1)} %collective-permute-done.18), channel_id=1, source_target_pairs={{0,4},{4,0},{8,12},{12,8},{16,20},{20,16},{24,28},{28,24},{1,5},{5... | collective-permute-start | bytes 737288 | tf_op jit(solution)/shard_map/ppermute | solution.py:372
  74.8 1.5 %collective-permute-start.25 = (bf16[64,1920]{1,0:T(8,128)(2,1)S(1)}, bf16[64,1920]{1,0:T(8,128)(2,1)S(1)}, u32[]{:S(2)}, u32[]{:S(2)}) collective-permute-start(bf16[64,1920]{1,0:T(8,128)(2,1)S(1)} %collective-permute-done.23), channel_id=1, source_target_pairs={{0,4},{4,0},{8,12},{12,8},{16,20},{20,16},{24,28},{28,24},{1,5},{5... | collective-permute-start | bytes 737288 | tf_op jit(solution)/shard_map/ppermute | solution.py:372
  74.9 4.8 %collective-permute-start.16 = (bf16[128,1920]{1,0:T(8,128)(2,1)S(1)}, bf16[128,1920]{1,0:T(8,128)(2,1)S(1)}, u32[]{:S(2)}, u32[]{:S(2)}) collective-permute-start(bf16[128,1920]{1,0:T(8,128)(2,1)S(1)} %collective-permute-done.15), channel_id=1, source_target_pairs={{0,4},{4,0},{8,12},{12,8},{16,20},{20,16},{24,28},{28,24},{1,5},{5... | collective-permute-start | bytes 1474568 | tf_op jit(solution)/shard_map/ppermute | solution.py:372
  83.0 10.7 %copy-start.2 = (f32[64,2]{0,1:T(2,128)S(1)}, f32[64,2]{0,1:T(2,128)}, u32[]{:S(2)}) copy-start(f32[64,2]{0,1:T(2,128)} %param.11) | copy-start | bytes 1540
  83.0 10.1 %all-to-all-start = ((f32[32,2,128]{2,1,0:T(2,128)}), f32[32,2,128]{2,1,0:T(2,128)S(1)}, u32[]{:S(2)}, u32[]{:S(2)}) async-start(f32[32,2,128]{2,1,0:T(2,128)} %get-tuple-element.53), calls=%async_computation | async-start | bytes 65536 | tf_op jit(solution)/shard_map/all_to_all | solution.py:441
  93.1 0.6 copy-start.8

commit v6 on v5

--- a/solution.py
+++ b/solution.py
@@ -349,7 +349,7 @@
         in_specs=[SMEM_SPEC] + [VMEM_SPEC] * 3,
         out_specs=[VMEM_SPEC] * 2,
         out_shape=[jax.ShapeDtypeStruct((1, tok), jnp.float32), jax.ShapeDtypeStruct((1, 1), jnp.float32)],
-    )(numbers, in_hbm(back), in_vmem(routes), in_vmem(weights))
+    )(numbers, in_vmem(back), routes, weights)
 
 
 def in_pieces(squares):

time: 95.3 us -> 94.6 us (level)
    unnamed x32 -> x28, local copies, waits for them, and re-layouts: 3.43 us -> 2.81 us
where the time goes in v6:
time: 94.6 us; the launch traced here: 94.4 us
  waiting for transfers between devices  41.7 us (44%)
  starting transfers between devices  26.4 us (28%)
  Pallas kernels  18.6 us (20%)
  local copies, waits for them, and re-layouts  4.99 us (5%)
  other arithmetic  1.64 us (2%)
  between operations  1.04 us (1%)
    ppermute x8, waiting for transfers between devices, over_z(): return lax.ppermute(x, 'tensor', [(i, i ^ k) for i in range(n_z)])  21 us
    ppermute x20, waiting for transfers between devices, in_plane(): lax.ppermute(x, 'expert', [(i, i ^ (one if i & 1 else zero)) for i in ran...  14.7 us
    ppermute x20, starting transfers between devices, in_plane(): lax.ppermute(x, 'expert', [(i, i ^ (one if i & 1 else zero)) for i in ran...  12.1 us
    ppermute x8, starting transfers between devices, over_z(): return lax.ppermute(x, 'tensor', [(i, i ^ k) for i in range(n_z)])  11.5 us
    all_to_all x1, waiting for transfers between devices, line_device(): lax.all_to_all(payload, ('expert', 'tensor'), split_axis=0, concat_axis=0...  6.07 us
    pallas_call x1, Pallas kernels, add_product(): pl.pallas_call(kernel, in_specs=[SMEM_SPEC, HBM_SPEC, HBM_SPEC] + [VMEM_S...  4.81 us
    pallas_call x1, Pallas kernels, early_stats(): pl.pallas_call(kernel, in_specs=[SMEM_SPEC] + [VMEM_SPEC] * len(args), ou...  3.44 us
    pallas_call x1, Pallas kernels, late_stats(): pl.pallas_call(kernel, in_specs=[SMEM_SPEC] + [VMEM_SPEC] * (3 * quarters...  3.11 us
  transfers between devices with their start and end apart: 29, of which 12 were waited for; matrix products, arithmetic and copies ran while one was open for 1% of the time, Pallas kernels for 15%

profile of v6, /device:TPU:0, one launch (start us, length us, event | category | flops | bytes accessed | tf_op | source)
XLA Modules:
  0.0 94.4 jit_solution(7435850374463108784)
XLA Ops:
  0.7 1.2 %dynamic-slice_bitcast_fusion.2 = (bf16[64,1792]{1,0:T(8,128)(2,1)S(1)}, bf16[64,1792]{1,0:T(8,128)(2,1)S(1)}, bf16[64,1792]{1,0:T(8,128)(2,1)S(1)}) fusion(bf16[1,64,7168]{2,1,0:T(8,128)(2,1)} %param.8, s32[]{:T(128)S(6)} %select_n.13, s32[]{:T(128)S(6)} %select_n.15, s32[]{:T(128)S(6)} %select_n.14), kind=kLoop, calls=%fused_computation.16 | loop fusion | bytes 1376268 | tf_op jit(solution)/shard_map/dynamic_slice | solution.py:375
  1.9 5.1 %collective-permute-start = (bf16[64,1792]{1,0:T(8,128)(2,1)S(1)}, bf16[64,1792]{1,0:T(8,128)(2,1)S(1)}, u32[]{:S(2)}, u32[]{:S(2)}) collective-permute-start(bf16[64,1792]{1,0:T(8,128)(2,1)S(1)} %get-tuple-element.59), channel_id=1, source_target_pairs={{0,3},{1,2},{2,1},{3,0},{4,7},{5,6},{6,5},{7,4},{8,11},{9,10},{10,... | collective-permute-start | bytes 688136 | tf_op jit(solution)/shard_map/ppermute | solution.py:369
  7.0 0.0 collective-permute-start.1
  7.0 0.6 collective-permute-start.2
  7.6 0.1 stack.23.numbers_ref
  7.7 2.6 %shard_map.94 = (bf16[1792,512]{1,0:T(8,128)(2,1)S(1)}, bf16[1792,512]{1,0:T(8,128)(2,1)S(1)}) custom-call(s32[5]{0:T(128)S(1)} %stack.23.numbers_ref, bf16[7168,512]{1,0:T(8,128)(2,1)} %bitcast.28, bf16[7168,512]{1,0:T(8,128)(2,1)} %bitcast.30), custom_call_target="tpu_custom_call" | custom-call | bytes 3670016 | tf_op jit(solution)/shard_map/pallas_call | solution.py:109
  10.4 1.3 %copy-done.1 = bf16[1792,512]{1,0:T(8,128)(2,1)} copy-done((bf16[1792,512]{1,0:T(8,128)(2,1)}, bf16[1792,512]{1,0:T(8,128)(2,1)S(1)}, u32[]{:S(2)}) %copy-start.1) | copy-done | bytes 1835032
  11.6 1.2 %copy-done.3 = bf16[1792,512]{1,0:T(8,128)(2,1)} copy-done((bf16[1792,512]{1,0:T(8,128)(2,1)}, bf16[1792,512]{1,0:T(8,128)(2,1)S(1)}, u32[]{:S(2)}) %copy-start.3) | copy-done | bytes 1835032
  12.9 0.1 copy.16
  13.0 0.6 collective-permute-done
  13.6 12.9 %collective-permute-done.1 = bf16[64,1792]{1,0:T(8,128)(2,1)S(1)} collective-permute-done((bf16[64,1792]{1,0:T(8,128)(2,1)S(1)}, bf16[64,1792]{1,0:T(8,128)(2,1)S(1)}, u32[]{:S(2)}, u32[]{:S(2)}) %collective-permute-start.1) | collective-permute-done | bytes 229408 | tf_op jit(solution)/shard_map/ppermute | solution.py:369
  26.5 0.0 collective-permute-done.2
  26.5 1.2 %multiply_reduce_fusion = (f32[64]{0:T(128)S(1)}, bf16[64,1792]{1,0:T(8,128)(2,1)S(1)}) fusion(bf16[64,1792]{1,0:T(8,128)(2,1)S(1)} %collective-permute-done.2, bf16[64,1792]{1,0:T(8,128)(2,1)S(1)} %collective-permute-done.1, bf16[64,1792]{1,0:T(8,128)(2,1)S(1)} %collective-permute-done, bf16[1,64,7168]{2,1,0:T(8,128)(2,1)} %param.8, s32[]{:T(128)S(6)} %select_n.12, ...), kind=kLoop, calls=%fused_computation.12 | loop fusion | flops 1490880 | bytes 1383684 | tf_op jit(solution)/shard_map/reduce_sum | solution.py:386
  27.7 0.1 copy.14
  27.8 0.1 copy.13
  27.9 0.1 copy.15
  28.1 0.1 concatenate.36
  28.2 1.6 %collective-permute-start.5 = (bf16[64,1920]{1,0:T(8,128)(2,1)S(1)}, bf16[64,1920]{1,0:T(8,128)(2,1)S(1)}, u32[]{:S(2)}, u32[]{:S(2)}) collective-permute-start(bf16[64,1920]{1,0:T(8,128)(2,1)S(1)} %concatenate.36), channel_id=1, source_target_pairs={{0,8},{4,20},{8,0},{12,28},{16,24},{20,4},{24,16},{28,12},{1,9},{5... | collective-permute-start | bytes 737288 | tf_op jit(solution)/shard_map/ppermute | solution.py:372
  29.8 3.0 %collective-permute-start.3 = (bf16[64,1920]{1,0:T(8,128)(2,1)S(1)}, bf16[64,1920]{1,0:T(8,128)(2,1)S(1)}, u32[]{:S(2)}, u32[]{:S(2)}) collective-permute-start(bf16[64,1920]{1,0:T(8,128)(2,1)S(1)} %concatenate.36), channel_id=1, source_target_pairs={{0,1},{1,0},{2,3},{3,2},{4,5},{5,4},{6,7},{7,6},{8,9},{9,8},{10,11... | collective-permute-start | bytes 737288 | tf_op jit(solution)/shard_map/ppermute | solution.py:369
  32.8 1.6 %collective-permute-done.5 = bf16[64,1920]{1,0:T(8,128)(2,1)S(1)} collective-permute-done((bf16[64,1920]{1,0:T(8,128)(2,1)S(1)}, bf16[64,1920]{1,0:T(8,128)(2,1)S(1)}, u32[]{:S(2)}, u32[]{:S(2)}) %collective-permute-start.5) | collective-permute-done | bytes 245792 | tf_op jit(solution)/shard_map/ppermute | solution.py:372
  34.5 0.0 collective-permute-done.6
  34.5 1.5 %collective-permute-start.7 = (bf16[64,1920]{1,0:T(8,128)(2,1)S(1)}, bf16[64,1920]{1,0:T(8,128)(2,1)S(1)}, u32[]{:S(2)}, u32[]{:S(2)}) collective-permute-start(bf16[64,1920]{1,0:T(8,128)(2,1)S(1)} %collective-permute-done.6), channel_id=1, source_target_pairs={{0,8},{4,20},{8,0},{12,28},{16,24},{20,4},{24,16},{28,12},{1,9},{5... | collective-permute-start | bytes 737288 | tf_op jit(solution)/shard_map/ppermute | solution.py:372
  36.0 1.5 %collective-permute-start.13 = (bf16[64,1920]{1,0:T(8,128)(2,1)S(1)}, bf16[64,1920]{1,0:T(8,128)(2,1)S(1)}, u32[]{:S(2)}, u32[]{:S(2)}) collective-permute-start(bf16[64,1920]{1,0:T(8,128)(2,1)S(1)} %collective-permute-done.5), channel_id=1, source_target_pairs={{0,16},{4,12},{8,24},{12,4},{16,0},{20,28},{24,8},{28,20},{1,17},{... | collective-permute-start | bytes 737288 | tf_op jit(solution)/shard_map/ppermute | solution.py:372
  37.5 6.7 %collective-permute-done.4 = bf16[64,1920]{1,0:T(8,128)(2,1)S(1)} collective-permute-done((bf16[64,1920]{1,0:T(8,128)(2,1)S(1)}, bf16[64,1920]{1,0:T(8,128)(2,1)S(1)}, u32[]{:S(2)}, u32[]{:S(2)}) %collective-permute-start.4) | collective-permute-done | bytes 245792 | tf_op jit(solution)/shard_map/ppermute | solution.py:369
  44.2 0.0 collective-permute-start.20
  44.3 0.1 collective-permute-done.3
  44.4 0.0 collective-permute-done.7
  44.5 0.1 collective-permute-start.9
  44.6 0.6 collective-permute-start.12
  45.2 0.0 collective-permute-done.11
  45.2 0.6 collective-permute-start.8
  45.8 0.0 collective-permute-done.13
  45.8 0.7 collective-permute-start.14
  46.5 0.2 collective-permute-done.12
  46.7 1.8 %collective-permute-start.17 = (bf16[64,1920]{1,0:T(8,128)(2,1)S(1)}, bf16[64,1920]{1,0:T(8,128)(2,1)S(1)}, u32[]{:S(2)}, u32[]{:S(2)}) collective-permute-start(bf16[64,1920]{1,0:T(8,128)(2,1)S(1)} %collective-permute-done.13), channel_id=1, source_target_pairs={{0,2},{1,3},{2,0},{3,1},{4,6},{5,7},{6,4},{7,5},{8,10},{9,11},{10,... | collective-permute-start | bytes 737288 | tf_op jit(solution)/shard_map/ppermute | solution.py:369
  48.6 0.0 collective-permute-done.14
  48.7 2.1 %shard_map.95 = (f32[512,512]{1,0:T(8,128)S(1)}, f32[512,512]{1,0:T(8,128)S(1)}, f32[512,128]{1,0:T(8,128)S(1)}) custom-call(bf16[512,1920]{1,0:T(8,128)(2,1)S(1)} %constant_dynamic-update-slice_fusion.rows_ref, bf16[1792,512]{1,0:T(8,128)(2,1)S(1)} %copy-done.2, bf16[1792,512]{1,0:T(8,128)(2,1)S(1)} %copy-done.4), custom_call_target="tpu_custom_call" | custom-call | flops 1879048192 | bytes 3670016 | tf_op jit(solution)/shard_map/pallas_call | solution.py:133
  50.8 0.0 collective-permute-done.9
  50.8 0.7 collective-permute-start.10
  51.5 2.6 %collective-permute-done.8 = bf16[128,1920]{1,0:T(8,128)(2,1)S(1)} collective-permute-done((bf16[128,1920]{1,0:T(8,128)(2,1)S(1)}, bf16[128,1920]{1,0:T(8,128)(2,1)S(1)}, u32[]{:S(2)}, u32[]{:S(2)}) %collective-permute-start.8) | collective-permute-done | bytes 491552 | tf_op jit(solution)/shard_map/ppermute | solution.py:372
  54.1 0.0 collective-permute-start.26
  54.1 5.6 %collective-permute-done.10 = bf16[128,1920]{1,0:T(8,128)(2,1)S(1)} collective-permute-done((bf16[128,1920]{1,0:T(8,128)(2,1)S(1)}, bf16[128,1920]{1,0:T(8,128)(2,1)S(1)}, u32[]{:S(2)}, u32[]{:S(2)}) %collective-permute-start.10) | collective-permute-done | bytes 491552 | tf_op jit(solution)/shard_map/ppermute | solution.py:372
  59.7 0.6 collective-permute-start.22
  60.3 0.6 collective-permute-done.17
  60.9 0.9 collective-permute-start.18
  61.8 1.5 %collective-permute-start.15 = (bf16[128,1920]{1,0:T(8,128)(2,1)S(1)}, bf16[128,1920]{1,0:T(8,128)(2,1)S(1)}, u32[]{:S(2)}, u32[]{:S(2)}) collective-permute-start(bf16[128,1920]{1,0:T(8,128)(2,1)S(1)} %collective-permute-done.8), channel_id=1, source_target_pairs={{0,16},{4,12},{8,24},{12,4},{16,0},{20,28},{24,8},{28,20},{1,17},{... | collective-permute-start | bytes 1474568 | tf_op jit(solution)/shard_map/ppermute | solution.py:372
  63.4 0.1 pad_maximum_fusion.refs_0_
  63.5 0.1 collective-permute-start.27
  63.6 0.1 pad_maximum_fusion.1.refs_1_
  63.7 4.8 %shard_map.96 = (f32[256,512]{1,0:T(8,128)S(1)}, f32[256,512]{1,0:T(8,128)S(1)}, f32[256,128]{1,0:T(8,128)S(1)}, bf16[1792,512]{1,0:T(8,128)(2,1)S(1)}, bf16[179...) custom-call(s32[5]{0:T(128)S(1)} %stack.23.numbers_ref, ...), custom_call_target="tpu_custom_call" | custom-call | flops 1879048192 | bytes 3670016 | tf_op jit(solution)/shard_map/pallas_call | solution.py:174
  68.5 1.6 %collective-permute-start.23 = (bf16[64,1920]{1,0:T(8,128)(2,1)S(1)}, bf16[64,1920]{1,0:T(8,128)(2,1)S(1)}, u32[]{:S(2)}, u32[]{:S(2)}) collective-permute-start(bf16[64,1920]{1,0:T(8,128)(2,1)S(1)} %collective-permute-done.21), channel_id=1, source_target_pairs={{0,8},{4,20},{8,0},{12,28},{16,24},{20,4},{24,16},{28,12},{1,9},{5... | collective-permute-start | bytes 737288 | tf_op jit(solution)/shard_map/ppermute | solution.py:372
  70.1 0.1 collective-permute-start.24
  70.2 0.5 collective-permute-start.19
  70.7 4.1 %collective-permute-done.23 = bf16[64,1920]{1,0:T(8,128)(2,1)S(1)} collective-permute-done((bf16[64,1920]{1,0:T(8,128)(2,1)S(1)}, bf16[64,1920]{1,0:T(8,128)(2,1)S(1)}, u32[]{:S(2)}, u32[]{:S(2)}) %collective-permute-start.23) | collective-permute-done | bytes 245792 | tf_op jit(solution)/shard_map/ppermute | solution.py:372
  74.9 0.6 collective-permute-start.16
  75.6 0.1 pad_maximum_fusion.6
  75.7 0.6 collective-permute-done.25
  76.3 3.4 %shard_map.97.refs_12_.early_ref = f32[8,384]{1,0:T(8,128)S(1)} custom-call(s32[5]{0:T(128)S(1)} %stack.23.numbers_ref, bf16[384,1920]{1,0:T(8,128)(2,1)S(1)} %constant_dynamic-update-slice_fusion.8.rows_ref, bf16[128,1920]{1,0:T(8,128)(2,1)S(1)} %get-tuple-element.84.refs_0_, bf16[128,1920]{1,0:T(8,128)(2,1)S(1)} %get-tuple-element.85.refs_1_, ...), custom_call_target="tpu_custom_call" | custom-call | flops 1409286144 | bytes 3670016 | tf_op jit(solution)/shard_map/pallas_call | solution.py:239
  79.8 0.1 pad_maximum_fusion.3
  79.9 3.1 %shard_map.98 = (f32[8,128]{1,0:T(8,128)S(1)}, f32[32,2,128]{2,1,0:T(2,128)}) custom-call(s32[5]{0:T(128)S(1)} %stack.23.numbers_ref, bf16[128,1920]{1,0:T(8,128)(2,1)S(1)} %get-tuple-element.82.refs_0_, bf16[128,1920]{1,0:T(8,128)(2,1)S(1)} %get-tuple-element.83.refs_1_, bf16[128,1920]{1,0:T(8,128)(2,1)S(1)} %pad_maximum_fusion.5.refs_2_, ...), custom_call_target="tpu_custom_call" | custom-call | flops 469762048 | bytes 3670016 | tf_op jit(solution)/shard_map/pallas_call | solution.py:285
  83.0 2.8 %all-to-all-start = ((f32[32,2,128]{2,1,0:T(2,128)}), f32[32,2,128]{2,1,0:T(2,128)S(1)}, u32[]{:S(2)}, u32[]{:S(2)}) async-start(f32[32,2,128]{2,1,0:T(2,128)} %get-tuple-element.53), calls=%async_computation | async-start | bytes 65536 | tf_op jit(solution)/shard_map/all_to_all | solution.py:441
  85.8 1.2 %shard_map.100 = f32[1,1792]{1,0:T(1,128)} custom-call(bf16[512,1920]{1,0:T(8,128)(2,1)S(1)} %constant_dynamic-update-slice_fusion.rows_ref, f32[8,384]{1,0:T(8,128)S(1)} %shard_map.97.refs_12_.early_ref, f32[8,128]{1,0:T(8,128)S(1)} %get-tuple-element.56.late_ref), custom_call_target="tpu_custom_call" | custom-call | flops 3932160 | bytes 1966080 | tf_op jit(solution)/shard_map/pallas_call | solution.py:315
  87.0 6.1 %all-to-all-done.back_ref = f32[32,2,128]{2,1,0:T(2,128)S(1)} async-done(((f32[32,2,128]{2,1,0:T(2,128)}), f32[32,2,128]{2,1,0:T(2,128)S(1)}, u32[]{:S(2)}, u32[]{:S(2)}) %all-to-all-start) | async-done | bytes 32800 | tf_op jit(solution)/shard_map/all_to_all | solution.py:441
  93.1 1.3 %shard_map.99 = (f32[1,64]{1,0:T(1,128)}, f32[1,1]{1,0:T(1,128)}) custom-call(s32[5]{0:T(128)} %copy-done, f32[32,2,128]{2,1,0:T(2,128)S(1)} %all-to-all-done.back_ref, s32[2,64]{1,0:T(2,128)} %bitcast.33, f32[2,64]{1,0:T(2,128)} %bitcast.34), custom_call_target="tpu_custom_call" | custom-call | tf_op jit(solution)/shard_map/pallas_call | solution.py:347
  (58 shorter events, 0.8 us)
Async XLA Ops:
  1.9 11.7 %collective-permute-start = (bf16[64,1792]{1,0:T(8,128)(2,1)S(1)}, bf16[64,1792]{1,0:T(8,128)(2,1)S(1)}, u32[]{:S(2)}, u32[]{:S(2)}) collective-permute-start(bf16[64,1792]{1,0:T(8,128)(2,1)S(1)} %get-tuple-element.59), channel_id=1, source_target_pairs={{0,3},{1,2},{2,1},{3,0},{4,7},{5,6},{6,5},{7,4},{8,11},{9,10},{10,... | collective-permute-start | bytes 688136 | tf_op jit(solution)/shard_map/ppermute | solution.py:369
  7.0 19.5 %collective-permute-start.1 = (bf16[64,1792]{1,0:T(8,128)(2,1)S(1)}, bf16[64,1792]{1,0:T(8,128)(2,1)S(1)}, u32[]{:S(2)}, u32[]{:S(2)}) collective-permute-start(bf16[64,1792]{1,0:T(8,128)(2,1)S(1)} %get-tuple-element.61), channel_id=1, source_target_pairs={{0,2},{1,3},{2,0},{3,1},{4,6},{5,7},{6,4},{7,5},{8,10},{9,11},{10,... | collective-permute-start | bytes 688136 | tf_op jit(solution)/shard_map/ppermute | solution.py:369
  7.0 19.5 %collective-permute-start.2 = (bf16[64,1792]{1,0:T(8,128)(2,1)S(1)}, bf16[64,1792]{1,0:T(8,128)(2,1)S(1)}, u32[]{:S(2)}, u32[]{:S(2)}) collective-permute-start(bf16[64,1792]{1,0:T(8,128)(2,1)S(1)} %get-tuple-element.60), channel_id=1, source_target_pairs={{0,1},{1,0},{2,3},{3,2},{4,5},{5,4},{6,7},{7,6},{8,9},{9,8},{10,11... | collective-permute-start | bytes 688136 | tf_op jit(solution)/shard_map/ppermute | solution.py:369
  7.7 72.2 %copy-start = (s32[5]{0:T(128)}, s32[5]{0:T(128)S(1)}, u32[]{:S(2)}) copy-start(s32[5]{0:T(128)S(1)} %stack.23.numbers_ref) | copy-start | bytes 64
  7.7 5.2 %copy-start.6 = (bf16[1792]{0:T(1024)(128)(2,1)S(1)}, bf16[1792]{0:T(1024)(128)(2,1)}, u32[]{:S(2)}) copy-start(bf16[1792]{0:T(1024)(128)(2,1)} %param.9) | copy-start | bytes 10756
  7.7 5.2 %copy-start.7 = (s32[64,2]{0,1:T(2,128)S(1)}, s32[64,2]{0,1:T(2,128)}, u32[]{:S(2)}) copy-start(s32[64,2]{0,1:T(2,128)} %param.10) | copy-start | bytes 1540
  7.7 18.8 %copy-start.5 = (bf16[64,1792]{1,0:T(8,128)(2,1)S(1)}, bf16[64,1792]{1,0:T(8,128)(2,1)}, u32[]{:S(2)}) copy-start(bf16[64,1792]{1,0:T(8,128)(2,1)} %param.7) | copy-start | bytes 688132
  10.3 1.3 %copy-start.1 = (bf16[1792,512]{1,0:T(8,128)(2,1)}, bf16[1792,512]{1,0:T(8,128)(2,1)S(1)}, u32[]{:S(2)}) copy-start(bf16[1792,512]{1,0:T(8,128)(2,1)S(1)} %get-tuple-element.35.slab_ref) | copy-start | bytes 5505028
  11.6 1.2 %copy-start.3 = (bf16[1792,512]{1,0:T(8,128)(2,1)}, bf16[1792,512]{1,0:T(8,128)(2,1)S(1)}, u32[]{:S(2)}) copy-start(bf16[1792,512]{1,0:T(8,128)(2,1)S(1)} %get-tuple-element.36.slab_q_ref) | copy-start | bytes 5505028
  28.2 6.3 %collective-permute-start.5 = (bf16[64,1920]{1,0:T(8,128)(2,1)S(1)}, bf16[64,1920]{1,0:T(8,128)(2,1)S(1)}, u32[]{:S(2)}, u32[]{:S(2)}) collective-permute-start(bf16[64,1920]{1,0:T(8,128)(2,1)S(1)} %concatenate.36), channel_id=1, source_target_pairs={{0,8},{4,20},{8,0},{12,28},{16,24},{20,4},{24,16},{28,12},{1,9},{5... | collective-permute-start | bytes 737288 | tf_op jit(solution)/shard_map/ppermute | solution.py:372
  29.7 4.7 %collective-permute-start.6 = (bf16[64,1920]{1,0:T(8,128)(2,1)S(1)}, bf16[64,1920]{1,0:T(8,128)(2,1)S(1)}, u32[]{:S(2)}, u32[]{:S(2)}) collective-permute-start(bf16[64,1920]{1,0:T(8,128)(2,1)S(1)} %concatenate.36), channel_id=1, source_target_pairs={{0,4},{4,0},{8,12},{12,8},{16,20},{20,16},{24,28},{28,24},{1,5},{5... | collective-permute-start | bytes 737288 | tf_op jit(solution)/shard_map/ppermute | solution.py:372
  29.8 14.5 %collective-permute-start.4 = (bf16[64,1920]{1,0:T(8,128)(2,1)S(1)}, bf16[64,1920]{1,0:T(8,128)(2,1)S(1)}, u32[]{:S(2)}, u32[]{:S(2)}) collective-permute-start(bf16[64,1920]{1,0:T(8,128)(2,1)S(1)} %concatenate.36), channel_id=1, source_target_pairs={{0,2},{1,3},{2,0},{3,1},{4,6},{5,7},{6,4},{7,5},{8,10},{9,11},{10,... | collective-permute-start | bytes 737288 | tf_op jit(solution)/shard_map/ppermute | solution.py:369
  29.8 14.6 %collective-permute-start.3 = (bf16[64,1920]{1,0:T(8,128)(2,1)S(1)}, bf16[64,1920]{1,0:T(8,128)(2,1)S(1)}, u32[]{:S(2)}, u32[]{:S(2)}) collective-permute-start(bf16[64,1920]{1,0:T(8,128)(2,1)S(1)} %concatenate.36), channel_id=1, source_target_pairs={{0,1},{1,0},{2,3},{3,2},{4,5},{5,4},{6,7},{7,6},{8,9},{9,8},{10,11... | collective-permute-start | bytes 737288 | tf_op jit(solution)/shard_map/ppermute | solution.py:369
  34.5 10.0 %collective-permute-start.7 = (bf16[64,1920]{1,0:T(8,128)(2,1)S(1)}, bf16[64,1920]{1,0:T(8,128)(2,1)S(1)}, u32[]{:S(2)}, u32[]{:S(2)}) collective-permute-start(bf16[64,1920]{1,0:T(8,128)(2,1)S(1)} %collective-permute-done.6), channel_id=1, source_target_pairs={{0,8},{4,20},{8,0},{12,28},{16,24},{20,4},{24,16},{28,12},{1,9},{5... | collective-permute-start | bytes 737288 | tf_op jit(solution)/shard_map/ppermute | solution.py:372
  35.9 9.2 %collective-permute-start.11 = (bf16[64,1920]{1,0:T(8,128)(2,1)S(1)}, bf16[64,1920]{1,0:T(8,128)(2,1)S(1)}, u32[]{:S(2)}, u32[]{:S(2)}) collective-permute-start(bf16[64,1920]{1,0:T(8,128)(2,1)S(1)} %collective-permute-done.5), channel_id=1, source_target_pairs={{0,4},{4,0},{8,12},{12,8},{16,20},{20,16},{24,28},{28,24},{1,5},{5... | collective-permute-start | bytes 737288 | tf_op jit(solution)/shard_map/ppermute | solution.py:372
  36.0 9.8 %collective-permute-start.13 = (bf16[64,1920]{1,0:T(8,128)(2,1)S(1)}, bf16[64,1920]{1,0:T(8,128)(2,1)S(1)}, u32[]{:S(2)}, u32[]{:S(2)}) collective-permute-start(bf16[64,1920]{1,0:T(8,128)(2,1)S(1)} %collective-permute-done.5), channel_id=1, source_target_pairs={{0,16},{4,12},{8,24},{12,4},{16,0},{20,28},{24,8},{28,20},{1,17},{... | collective-permute-start | bytes 737288 | tf_op jit(solution)/shard_map/ppermute | solution.py:372
  44.2 9.9 %collective-permute-start.20 = (bf16[64,1920]{1,0:T(8,128)(2,1)S(1)}, bf16[64,1920]{1,0:T(8,128)(2,1)S(1)}, u32[]{:S(2)}, u32[]{:S(2)}) collective-permute-start(bf16[64,1920]{1,0:T(8,128)(2,1)S(1)} %collective-permute-done.4), channel_id=1, source_target_pairs={{0,1},{1,0},{2,3},{3,2},{4,5},{5,4},{6,7},{7,6},{8,9},{9,8},{10,11... | collective-permute-start | bytes 737288 | tf_op jit(solution)/shard_map/ppermute | solution.py:369
  44.4 4.3 %copy-start.4 = (bf16[1792,512]{1,0:T(8,128)(2,1)S(1)}, bf16[1792,512]{1,0:T(8,128)(2,1)}, u32[]{:S(2)}) copy-start(bf16[1792,512]{1,0:T(8,128)(2,1)} %copy-done.3) | copy-start | bytes 5505028
  44.4 4.2 %copy-start.2 = (bf16[1792,512]{1,0:T(8,128)(2,1)S(1)}, bf16[1792,512]{1,0:T(8,128)(2,1)}, u32[]{:S(2)}) copy-start(bf16[1792,512]{1,0:T(8,128)(2,1)} %copy-done.1) | copy-start | bytes 5505028
  44.5 6.3 %collective-permute-start.9 = (bf16[128,1920]{1,0:T(8,128)(2,1)S(1)}, bf16[128,1920]{1,0:T(8,128)(2,1)S(1)}, u32[]{:S(2)}, u32[]{:S(2)}) collective-permute-start(bf16[128,1920]{1,0:T(8,128)(2,1)S(1)} %pad_maximum_fusion.2), channel_id=1, source_target_pairs={{0,4},{4,0},{8,12},{12,8},{16,20},{20,16},{24,28},{28,24},{1,5},{5... | collective-permute-start | bytes 1474568 | tf_op jit(solution)/shard_map/ppermute | solution.py:372
  44.6 2.2 %collective-permute-start.12 = (bf16[64,1920]{1,0:T(8,128)(2,1)S(1)}, bf16[64,1920]{1,0:T(8,128)(2,1)S(1)}, u32[]{:S(2)}, u32[]{:S(2)}) collective-permute-start(bf16[64,1920]{1,0:T(8,128)(2,1)S(1)} %collective-permute-done.7), channel_id=1, source_target_pairs={{0,4},{4,0},{8,12},{12,8},{16,20},{20,16},{24,28},{28,24},{1,5},{5... | collective-permute-start | bytes 737288 | tf_op jit(solution)/shard_map/ppermute | solution.py:372
  45.2 8.9 %collective-permute-start.8 = (bf16[128,1920]{1,0:T(8,128)(2,1)S(1)}, bf16[128,1920]{1,0:T(8,128)(2,1)S(1)}, u32[]{:S(2)}, u32[]{:S(2)}) collective-permute-start(bf16[128,1920]{1,0:T(8,128)(2,1)S(1)} %pad_maximum_fusion.2), channel_id=1, source_target_pairs={{0,8},{4,20},{8,0},{12,28},{16,24},{20,4},{24,16},{28,12},{1,9},{5... | collective-permute-start | bytes 1474568 | tf_op jit(solution)/shard_map/ppermute | solution.py:372
  45.8 2.8 %collective-permute-start.14 = (bf16[64,1920]{1,0:T(8,128)(2,1)S(1)}, bf16[64,1920]{1,0:T(8,128)(2,1)S(1)}, u32[]{:S(2)}, u32[]{:S(2)}) collective-permute-start(bf16[64,1920]{1,0:T(8,128)(2,1)S(1)} %collective-permute-done.13), channel_id=1, source_target_pairs={{0,4},{4,0},{8,12},{12,8},{16,20},{20,16},{24,28},{28,24},{1,5},{5... | collective-permute-start | bytes 737288 | tf_op jit(solution)/shard_map/ppermute | solution.py:372
  46.7 14.2 %collective-permute-start.17 = (bf16[64,1920]{1,0:T(8,128)(2,1)S(1)}, bf16[64,1920]{1,0:T(8,128)(2,1)S(1)}, u32[]{:S(2)}, u32[]{:S(2)}) collective-permute-start(bf16[64,1920]{1,0:T(8,128)(2,1)S(1)} %collective-permute-done.13), channel_id=1, source_target_pairs={{0,2},{1,3},{2,0},{3,1},{4,6},{5,7},{6,4},{7,5},{8,10},{9,11},{10,... | collective-permute-start | bytes 737288 | tf_op jit(solution)/shard_map/ppermute | solution.py:369
  50.8 8.9 %collective-permute-start.10 = (bf16[128,1920]{1,0:T(8,128)(2,1)S(1)}, bf16[128,1920]{1,0:T(8,128)(2,1)S(1)}, u32[]{:S(2)}, u32[]{:S(2)}) collective-permute-start(bf16[128,1920]{1,0:T(8,128)(2,1)S(1)} %collective-permute-done.9), channel_id=1, source_target_pairs={{0,8},{4,20},{8,0},{12,28},{16,24},{20,4},{24,16},{28,12},{1,9},{5... | collective-permute-start | bytes 1474568 | tf_op jit(solution)/shard_map/ppermute | solution.py:372
  54.1 9.4 %collective-permute-start.26 = (bf16[128,1920]{1,0:T(8,128)(2,1)S(1)}, bf16[128,1920]{1,0:T(8,128)(2,1)S(1)}, u32[]{:S(2)}, u32[]{:S(2)}) collective-permute-start(bf16[128,1920]{1,0:T(8,128)(2,1)S(1)} %collective-permute-done.8), channel_id=1, source_target_pairs={{0,4},{4,0},{8,12},{12,8},{16,20},{20,16},{24,28},{28,24},{1,5},{5... | collective-permute-start | bytes 1474568 | tf_op jit(solution)/shard_map/ppermute | solution.py:372
  59.7 8.8 %collective-permute-start.21 = (bf16[64,1920]{1,0:T(8,128)(2,1)S(1)}, bf16[64,1920]{1,0:T(8,128)(2,1)S(1)}, u32[]{:S(2)}, u32[]{:S(2)}) collective-permute-start(bf16[64,1920]{1,0:T(8,128)(2,1)S(1)} %collective-permute-done.20), channel_id=1, source_target_pairs={{0,4},{4,0},{8,12},{12,8},{16,20},{20,16},{24,28},{28,24},{1,5},{5... | collective-permute-start | bytes 737288 | tf_op jit(solution)/shard_map/ppermute | solution.py:372
  59.7 10.4 %collective-permute-start.22 = (bf16[64,1920]{1,0:T(8,128)(2,1)S(1)}, bf16[64,1920]{1,0:T(8,128)(2,1)S(1)}, u32[]{:S(2)}, u32[]{:S(2)}) collective-permute-start(bf16[64,1920]{1,0:T(8,128)(2,1)S(1)} %collective-permute-done.20), channel_id=1, source_target_pairs={{0,8},{4,20},{8,0},{12,28},{16,24},{20,4},{24,16},{28,12},{1,9},{5... | collective-permute-start | bytes 737288 | tf_op jit(solution)/shard_map/ppermute | solution.py:372
  60.9 9.2 %collective-permute-start.18 = (bf16[64,1920]{1,0:T(8,128)(2,1)S(1)}, bf16[64,1920]{1,0:T(8,128)(2,1)S(1)}, u32[]{:S(2)}, u32[]{:S(2)}) collective-permute-start(bf16[64,1920]{1,0:T(8,128)(2,1)S(1)} %collective-permute-done.17), channel_id=1, source_target_pairs={{0,1},{1,0},{2,3},{3,2},{4,5},{5,4},{6,7},{7,6},{8,9},{9,8},{10,11... | collective-permute-start | bytes 737288 | tf_op jit(solution)/shard_map/ppermute | solution.py:369
  61.8 13.1 %collective-permute-start.15 = (bf16[128,1920]{1,0:T(8,128)(2,1)S(1)}, bf16[128,1920]{1,0:T(8,128)(2,1)S(1)}, u32[]{:S(2)}, u32[]{:S(2)}) collective-permute-start(bf16[128,1920]{1,0:T(8,128)(2,1)S(1)} %collective-permute-done.8), channel_id=1, source_target_pairs={{0,16},{4,12},{8,24},{12,4},{16,0},{20,28},{24,8},{28,20},{1,17},{... | collective-permute-start | bytes 1474568 | tf_op jit(solution)/shard_map/ppermute | solution.py:372
  63.5 12.0 %collective-permute-start.27 = (bf16[128,1920]{1,0:T(8,128)(2,1)S(1)}, bf16[128,1920]{1,0:T(8,128)(2,1)S(1)}, u32[]{:S(2)}, u32[]{:S(2)}) collective-permute-start(bf16[128,1920]{1,0:T(8,128)(2,1)S(1)} %collective-permute-done.10), channel_id=1, source_target_pairs={{0,4},{4,0},{8,12},{12,8},{16,20},{20,16},{24,28},{28,24},{1,5},{5... | collective-permute-start | bytes 1474568 | tf_op jit(solution)/shard_map/ppermute | solution.py:372
  68.5 6.3 %collective-permute-start.23 = (bf16[64,1920]{1,0:T(8,128)(2,1)S(1)}, bf16[64,1920]{1,0:T(8,128)(2,1)S(1)}, u32[]{:S(2)}, u32[]{:S(2)}) collective-permute-start(bf16[64,1920]{1,0:T(8,128)(2,1)S(1)} %collective-permute-done.21), channel_id=1, source_target_pairs={{0,8},{4,20},{8,0},{12,28},{16,24},{20,4},{24,16},{28,12},{1,9},{5... | collective-permute-start | bytes 737288 | tf_op jit(solution)/shard_map/ppermute | solution.py:372
  70.1 4.8 %collective-permute-start.24 = (bf16[64,1920]{1,0:T(8,128)(2,1)S(1)}, bf16[64,1920]{1,0:T(8,128)(2,1)S(1)}, u32[]{:S(2)}, u32[]{:S(2)}) collective-permute-start(bf16[64,1920]{1,0:T(8,128)(2,1)S(1)} %collective-permute-done.22), channel_id=1, source_target_pairs={{0,4},{4,0},{8,12},{12,8},{16,20},{20,16},{24,28},{28,24},{1,5},{5... | collective-permute-start | bytes 737288 | tf_op jit(solution)/shard_map/ppermute | solution.py:372
  70.2 4.6 %collective-permute-start.19 = (bf16[64,1920]{1,0:T(8,128)(2,1)S(1)}, bf16[64,1920]{1,0:T(8,128)(2,1)S(1)}, u32[]{:S(2)}, u32[]{:S(2)}) collective-permute-start(bf16[64,1920]{1,0:T(8,128)(2,1)S(1)} %collective-permute-done.18), channel_id=1, source_target_pairs={{0,4},{4,0},{8,12},{12,8},{16,20},{20,16},{24,28},{28,24},{1,5},{5... | collective-permute-start | bytes 737288 | tf_op jit(solution)/shard_map/ppermute | solution.py:372
  74.8 1.5 %collective-permute-start.25 = (bf16[64,1920]{1,0:T(8,128)(2,1)S(1)}, bf16[64,1920]{1,0:T(8,128)(2,1)S(1)}, u32[]{:S(2)}, u32[]{:S(2)}) collective-permute-start(bf16[64,1920]{1,0:T(8,128)(2,1)S(1)} %collective-permute-done.23), channel_id=1, source_target_pairs={{0,4},{4,0},{8,12},{12,8},{16,20},{20,16},{24,28},{28,24},{1,5},{5... | collective-permute-start | bytes 737288 | tf_op jit(solution)/shard_map/ppermute | solution.py:372
  74.9 4.8 %collective-permute-start.16 = (bf16[128,1920]{1,0:T(8,128)(2,1)S(1)}, bf16[128,1920]{1,0:T(8,128)(2,1)S(1)}, u32[]{:S(2)}, u32[]{:S(2)}) collective-permute-start(bf16[128,1920]{1,0:T(8,128)(2,1)S(1)} %collective-permute-done.15), channel_id=1, source_target_pairs={{0,4},{4,0},{8,12},{12,8},{16,20},{20,16},{24,28},{28,24},{1,5},{5... | collective-permute-start | bytes 1474568 | tf_op jit(solution)/shard_map/ppermute | solution.py:372
  83.0 10.1 %all-to-all-start = ((f32[32,2,128]{2,1,0:T(2,128)}), f32[32,2,128]{2,1,0:T(2,128)S(1)}, u32[]{:S(2)}, u32[]{:S(2)}) async-start(f32[32,2,128]{2,1,0:T(2,128)} %get-tuple-element.53), calls=%async_computation | async-start | bytes 65536 | tf_op jit(solution)/shard_map/all_to_all | solution.py:441

commit v7 on v6

--- a/solution.py
+++ b/solution.py
@@ -426,10 +426,10 @@
     ready[0] = tied(ready[0], z_both)
     slabs, sums = add_product(numbers, w, wq, ready, width, first_sums)
     rest = of_quarters([other_core(x) for x in beside])
-    last = of_quarters((across, other_core(across)))
+    last = of_quarters((across, other_core(tied(across, *sums))))
 
     single = tied(z_both, beside[1])
-    across_far = tied(across_far, beside[1])
+    across_far = tied(across_far, beside[1], *first_sums)
     near = single, other_core(single)
     beside = next_chip(near[0]), next_chip(near[1])
     across = over_z(across_far, 1)

time: 94.6 us -> 94.6 us (level)
  no operation moved by 1% of the time
where the time goes in v7:
time: 94.6 us; the launch traced here: 94.4 us
  waiting for transfers between devices  41.7 us (44%)
  starting transfers between devices  26.4 us (28%)
  Pallas kernels  18.6 us (20%)
  local copies, waits for them, and re-layouts  4.99 us (5%)
  other arithmetic  1.63 us (2%)
  between operations  1.04 us (1%)
    ppermute x8, waiting for transfers between devices, over_z(): return lax.ppermute(x, 'tensor', [(i, i ^ k) for i in range(n_z)])  21 us
    ppermute x20, waiting for transfers between devices, in_plane(): lax.ppermute(x, 'expert', [(i, i ^ (one if i & 1 else zero)) for i in ran...  14.7 us
    ppermute x20, starting transfers between devices, in_plane(): lax.ppermute(x, 'expert', [(i, i ^ (one if i & 1 else zero)) for i in ran...  12.1 us
    ppermute x8, starting transfers between devices, over_z(): return lax.ppermute(x, 'tensor', [(i, i ^ k) for i in range(n_z)])  11.5 us
    all_to_all x1, waiting for transfers between devices, line_device(): lax.all_to_all(payload, ('expert', 'tensor'), split_axis=0, concat_axis=0...  6.07 us
    pallas_call x1, Pallas kernels, add_product(): pl.pallas_call(kernel, in_specs=[SMEM_SPEC, HBM_SPEC, HBM_SPEC] + [VMEM_S...  4.81 us
    pallas_call x1, Pallas kernels, early_stats(): pl.pallas_call(kernel, in_specs=[SMEM_SPEC] + [VMEM_SPEC] * len(args), ou...  3.44 us
    pallas_call x1, Pallas kernels, late_stats(): pl.pallas_call(kernel, in_specs=[SMEM_SPEC] + [VMEM_SPEC] * (3 * quarters...  3.11 us
  transfers between devices with their start and end apart: 29, of which 12 were waited for; matrix products, arithmetic and copies ran while one was open for 1% of the time, Pallas kernels for 15%

profile of v7, /device:TPU:0, one launch (start us, length us, event | category | flops | bytes accessed | tf_op | source)
XLA Modules:
  0.0 94.4 jit_solution(16981875198234898893)
XLA Ops:
  0.7 1.2 %dynamic-slice_bitcast_fusion.2 = (bf16[64,1792]{1,0:T(8,128)(2,1)S(1)}, bf16[64,1792]{1,0:T(8,128)(2,1)S(1)}, bf16[64,1792]{1,0:T(8,128)(2,1)S(1)}) fusion(bf16[1,64,7168]{2,1,0:T(8,128)(2,1)} %param.8, s32[]{:T(128)S(6)} %select_n.13, s32[]{:T(128)S(6)} %select_n.15, s32[]{:T(128)S(6)} %select_n.14), kind=kLoop, calls=%fused_computation.16 | loop fusion | bytes 1376268 | tf_op jit(solution)/shard_map/dynamic_slice | solution.py:375
  1.9 5.1 %collective-permute-start = (bf16[64,1792]{1,0:T(8,128)(2,1)S(1)}, bf16[64,1792]{1,0:T(8,128)(2,1)S(1)}, u32[]{:S(2)}, u32[]{:S(2)}) collective-permute-start(bf16[64,1792]{1,0:T(8,128)(2,1)S(1)} %get-tuple-element.61), channel_id=1, source_target_pairs={{0,3},{1,2},{2,1},{3,0},{4,7},{5,6},{6,5},{7,4},{8,11},{9,10},{10,... | collective-permute-start | bytes 688136 | tf_op jit(solution)/shard_map/ppermute | solution.py:369
  7.0 0.0 collective-permute-start.1
  7.0 0.6 collective-permute-start.2
  7.6 0.1 stack.23.numbers_ref
  7.7 2.6 %shard_map.94 = (bf16[1792,512]{1,0:T(8,128)(2,1)S(1)}, bf16[1792,512]{1,0:T(8,128)(2,1)S(1)}) custom-call(s32[5]{0:T(128)S(1)} %stack.23.numbers_ref, bf16[7168,512]{1,0:T(8,128)(2,1)} %bitcast.28, bf16[7168,512]{1,0:T(8,128)(2,1)} %bitcast.30), custom_call_target="tpu_custom_call" | custom-call | bytes 3670016 | tf_op jit(solution)/shard_map/pallas_call | solution.py:109
  10.4 1.3 %copy-done.1 = bf16[1792,512]{1,0:T(8,128)(2,1)} copy-done((bf16[1792,512]{1,0:T(8,128)(2,1)}, bf16[1792,512]{1,0:T(8,128)(2,1)S(1)}, u32[]{:S(2)}) %copy-start.1) | copy-done | bytes 1835032
  11.6 1.2 %copy-done.3 = bf16[1792,512]{1,0:T(8,128)(2,1)} copy-done((bf16[1792,512]{1,0:T(8,128)(2,1)}, bf16[1792,512]{1,0:T(8,128)(2,1)S(1)}, u32[]{:S(2)}) %copy-start.3) | copy-done | bytes 1835032
  12.9 0.1 copy.16
  13.0 0.6 collective-permute-done
  13.6 12.9 %collective-permute-done.1 = bf16[64,1792]{1,0:T(8,128)(2,1)S(1)} collective-permute-done((bf16[64,1792]{1,0:T(8,128)(2,1)S(1)}, bf16[64,1792]{1,0:T(8,128)(2,1)S(1)}, u32[]{:S(2)}, u32[]{:S(2)}) %collective-permute-start.1) | collective-permute-done | bytes 229408 | tf_op jit(solution)/shard_map/ppermute | solution.py:369
  26.5 0.0 collective-permute-done.2
  26.5 1.2 %multiply_reduce_fusion = (f32[64]{0:T(128)S(1)}, bf16[64,1792]{1,0:T(8,128)(2,1)S(1)}) fusion(bf16[64,1792]{1,0:T(8,128)(2,1)S(1)} %collective-permute-done.2, bf16[64,1792]{1,0:T(8,128)(2,1)S(1)} %collective-permute-done.1, bf16[64,1792]{1,0:T(8,128)(2,1)S(1)} %collective-permute-done, bf16[1,64,7168]{2,1,0:T(8,128)(2,1)} %param.8, s32[]{:T(128)S(6)} %select_n.12, ...), kind=kLoop, calls=%fused_computation.12 | loop fusion | flops 1490880 | bytes 1383684 | tf_op jit(solution)/shard_map/reduce_sum | solution.py:386
  27.7 0.1 copy.14
  27.8 0.1 copy.13
  27.9 0.1 copy.15
  28.1 0.1 concatenate.36
  28.2 1.6 %collective-permute-start.5 = (bf16[64,1920]{1,0:T(8,128)(2,1)S(1)}, bf16[64,1920]{1,0:T(8,128)(2,1)S(1)}, u32[]{:S(2)}, u32[]{:S(2)}) collective-permute-start(bf16[64,1920]{1,0:T(8,128)(2,1)S(1)} %concatenate.36), channel_id=1, source_target_pairs={{0,8},{4,20},{8,0},{12,28},{16,24},{20,4},{24,16},{28,12},{1,9},{5... | collective-permute-start | bytes 737288 | tf_op jit(solution)/shard_map/ppermute | solution.py:372
  29.8 3.0 %collective-permute-start.3 = (bf16[64,1920]{1,0:T(8,128)(2,1)S(1)}, bf16[64,1920]{1,0:T(8,128)(2,1)S(1)}, u32[]{:S(2)}, u32[]{:S(2)}) collective-permute-start(bf16[64,1920]{1,0:T(8,128)(2,1)S(1)} %concatenate.36), channel_id=1, source_target_pairs={{0,1},{1,0},{2,3},{3,2},{4,5},{5,4},{6,7},{7,6},{8,9},{9,8},{10,11... | collective-permute-start | bytes 737288 | tf_op jit(solution)/shard_map/ppermute | solution.py:369
  32.8 1.6 %collective-permute-done.5 = bf16[64,1920]{1,0:T(8,128)(2,1)S(1)} collective-permute-done((bf16[64,1920]{1,0:T(8,128)(2,1)S(1)}, bf16[64,1920]{1,0:T(8,128)(2,1)S(1)}, u32[]{:S(2)}, u32[]{:S(2)}) %collective-permute-start.5) | collective-permute-done | bytes 245792 | tf_op jit(solution)/shard_map/ppermute | solution.py:372
  34.5 0.0 collective-permute-done.6
  34.5 1.5 %collective-permute-start.7 = (bf16[64,1920]{1,0:T(8,128)(2,1)S(1)}, bf16[64,1920]{1,0:T(8,128)(2,1)S(1)}, u32[]{:S(2)}, u32[]{:S(2)}) collective-permute-start(bf16[64,1920]{1,0:T(8,128)(2,1)S(1)} %collective-permute-done.6), channel_id=1, source_target_pairs={{0,8},{4,20},{8,0},{12,28},{16,24},{20,4},{24,16},{28,12},{1,9},{5... | collective-permute-start | bytes 737288 | tf_op jit(solution)/shard_map/ppermute | solution.py:372
  36.0 1.5 %collective-permute-start.13 = (bf16[64,1920]{1,0:T(8,128)(2,1)S(1)}, bf16[64,1920]{1,0:T(8,128)(2,1)S(1)}, u32[]{:S(2)}, u32[]{:S(2)}) collective-permute-start(bf16[64,1920]{1,0:T(8,128)(2,1)S(1)} %collective-permute-done.5), channel_id=1, source_target_pairs={{0,16},{4,12},{8,24},{12,4},{16,0},{20,28},{24,8},{28,20},{1,17},{... | collective-permute-start | bytes 737288 | tf_op jit(solution)/shard_map/ppermute | solution.py:372
  37.5 6.7 %collective-permute-done.4 = bf16[64,1920]{1,0:T(8,128)(2,1)S(1)} collective-permute-done((bf16[64,1920]{1,0:T(8,128)(2,1)S(1)}, bf16[64,1920]{1,0:T(8,128)(2,1)S(1)}, u32[]{:S(2)}, u32[]{:S(2)}) %collective-permute-start.4) | collective-permute-done | bytes 245792 | tf_op jit(solution)/shard_map/ppermute | solution.py:369
  44.2 0.0 collective-permute-start.16
  44.3 0.1 collective-permute-done.3
  44.4 0.0 collective-permute-done.7
  44.5 0.1 collective-permute-start.9
  44.6 0.6 collective-permute-start.12
  45.2 0.6 collective-permute-start.8
  45.8 0.0 collective-permute-done.13
  45.8 0.7 collective-permute-start.14
  46.5 0.2 collective-permute-done.12
  46.7 1.8 %collective-permute-start.18 = (bf16[64,1920]{1,0:T(8,128)(2,1)S(1)}, bf16[64,1920]{1,0:T(8,128)(2,1)S(1)}, u32[]{:S(2)}, u32[]{:S(2)}) collective-permute-start(bf16[64,1920]{1,0:T(8,128)(2,1)S(1)} %collective-permute-done.13), channel_id=1, source_target_pairs={{0,2},{1,3},{2,0},{3,1},{4,6},{5,7},{6,4},{7,5},{8,10},{9,11},{10,... | collective-permute-start | bytes 737288 | tf_op jit(solution)/shard_map/ppermute | solution.py:369
  48.6 0.0 collective-permute-done.14
  48.7 2.1 %shard_map.95 = (f32[512,512]{1,0:T(8,128)S(1)}, f32[512,512]{1,0:T(8,128)S(1)}, f32[512,128]{1,0:T(8,128)S(1)}) custom-call(bf16[512,1920]{1,0:T(8,128)(2,1)S(1)} %constant_dynamic-update-slice_fusion.rows_ref, bf16[1792,512]{1,0:T(8,128)(2,1)S(1)} %copy-done.2, bf16[1792,512]{1,0:T(8,128)(2,1)S(1)} %copy-done.4), custom_call_target="tpu_custom_call" | custom-call | flops 1879048192 | bytes 3670016 | tf_op jit(solution)/shard_map/pallas_call | solution.py:133
  50.8 0.0 collective-permute-done.9
  50.8 0.7 collective-permute-start.10
  51.5 2.5 %collective-permute-done.8 = bf16[128,1920]{1,0:T(8,128)(2,1)S(1)} collective-permute-done((bf16[128,1920]{1,0:T(8,128)(2,1)S(1)}, bf16[128,1920]{1,0:T(8,128)(2,1)S(1)}, u32[]{:S(2)}, u32[]{:S(2)}) %collective-permute-start.8) | collective-permute-done | bytes 491552 | tf_op jit(solution)/shard_map/ppermute | solution.py:372
  54.1 0.0 collective-permute-start.26
  54.1 0.0 collective-permute-done.16
  54.1 5.6 %collective-permute-done.10 = bf16[128,1920]{1,0:T(8,128)(2,1)S(1)} collective-permute-done((bf16[128,1920]{1,0:T(8,128)(2,1)S(1)}, bf16[128,1920]{1,0:T(8,128)(2,1)S(1)}, u32[]{:S(2)}, u32[]{:S(2)}) %collective-permute-start.10) | collective-permute-done | bytes 491552 | tf_op jit(solution)/shard_map/ppermute | solution.py:372
  59.7 0.6 collective-permute-start.22
  60.3 0.6 collective-permute-done.18
  60.9 0.9 collective-permute-start.19
  61.8 1.5 %collective-permute-start.15 = (bf16[128,1920]{1,0:T(8,128)(2,1)S(1)}, bf16[128,1920]{1,0:T(8,128)(2,1)S(1)}, u32[]{:S(2)}, u32[]{:S(2)}) collective-permute-start(bf16[128,1920]{1,0:T(8,128)(2,1)S(1)} %collective-permute-done.8), channel_id=1, source_target_pairs={{0,16},{4,12},{8,24},{12,4},{16,0},{20,28},{24,8},{28,20},{1,17},{... | collective-permute-start | bytes 1474568 | tf_op jit(solution)/shard_map/ppermute | solution.py:372
  63.4 0.1 pad_maximum_fusion.1.refs_1_
  63.5 0.1 collective-permute-start.27
  63.6 0.1 pad_maximum_fusion.refs_0_
  63.7 4.8 %shard_map.96 = (f32[256,512]{1,0:T(8,128)S(1)}, f32[256,512]{1,0:T(8,128)S(1)}, f32[256,128]{1,0:T(8,128)S(1)}, bf16[1792,512]{1,0:T(8,128)(2,1)S(1)}, bf16[179...) custom-call(s32[5]{0:T(128)S(1)} %stack.23.numbers_ref, ...), custom_call_target="tpu_custom_call" | custom-call | flops 1879048192 | bytes 3670016 | tf_op jit(solution)/shard_map/pallas_call | solution.py:174
  68.5 1.6 %collective-permute-start.23 = (bf16[64,1920]{1,0:T(8,128)(2,1)S(1)}, bf16[64,1920]{1,0:T(8,128)(2,1)S(1)}, u32[]{:S(2)}, u32[]{:S(2)}) collective-permute-start(bf16[64,1920]{1,0:T(8,128)(2,1)S(1)} %collective-permute-done.21), channel_id=1, source_target_pairs={{0,8},{4,20},{8,0},{12,28},{16,24},{20,4},{24,16},{28,12},{1,9},{5... | collective-permute-start | bytes 737288 | tf_op jit(solution)/shard_map/ppermute | solution.py:372
  70.1 0.1 collective-permute-start.24
  70.2 0.5 collective-permute-start.20
  70.7 4.1 %collective-permute-done.23 = bf16[64,1920]{1,0:T(8,128)(2,1)S(1)} collective-permute-done((bf16[64,1920]{1,0:T(8,128)(2,1)S(1)}, bf16[64,1920]{1,0:T(8,128)(2,1)S(1)}, u32[]{:S(2)}, u32[]{:S(2)}) %collective-permute-start.23) | collective-permute-done | bytes 245792 | tf_op jit(solution)/shard_map/ppermute | solution.py:372
  74.9 0.6 collective-permute-start.17
  75.6 0.1 pad_maximum_fusion.6
  75.7 0.6 collective-permute-done.25
  76.3 3.4 %shard_map.97.refs_12_.early_ref = f32[8,384]{1,0:T(8,128)S(1)} custom-call(s32[5]{0:T(128)S(1)} %stack.23.numbers_ref, bf16[384,1920]{1,0:T(8,128)(2,1)S(1)} %constant_dynamic-update-slice_fusion.8.rows_ref, bf16[128,1920]{1,0:T(8,128)(2,1)S(1)} %get-tuple-element.86.refs_0_, bf16[128,1920]{1,0:T(8,128)(2,1)S(1)} %get-tuple-element.87.refs_1_, ...), custom_call_target="tpu_custom_call" | custom-call | flops 1409286144 | bytes 3670016 | tf_op jit(solution)/shard_map/pallas_call | solution.py:239
  79.8 0.1 pad_maximum_fusion.3
  79.9 3.1 %shard_map.98 = (f32[8,128]{1,0:T(8,128)S(1)}, f32[32,2,128]{2,1,0:T(2,128)}) custom-call(s32[5]{0:T(128)S(1)} %stack.23.numbers_ref, bf16[128,1920]{1,0:T(8,128)(2,1)S(1)} %get-tuple-element.84.refs_0_, bf16[128,1920]{1,0:T(8,128)(2,1)S(1)} %get-tuple-element.85.refs_1_, bf16[128,1920]{1,0:T(8,128)(2,1)S(1)} %pad_maximum_fusion.5.refs_2_, ...), custom_call_target="tpu_custom_call" | custom-call | flops 469762048 | bytes 3670016 | tf_op jit(solution)/shard_map/pallas_call | solution.py:285
  83.0 2.8 %all-to-all-start = ((f32[32,2,128]{2,1,0:T(2,128)}), f32[32,2,128]{2,1,0:T(2,128)S(1)}, u32[]{:S(2)}, u32[]{:S(2)}) async-start(f32[32,2,128]{2,1,0:T(2,128)} %get-tuple-element.55), calls=%async_computation | async-start | bytes 65536 | tf_op jit(solution)/shard_map/all_to_all | solution.py:441
  85.8 1.2 %shard_map.100 = f32[1,1792]{1,0:T(1,128)} custom-call(bf16[512,1920]{1,0:T(8,128)(2,1)S(1)} %constant_dynamic-update-slice_fusion.rows_ref, f32[8,384]{1,0:T(8,128)S(1)} %shard_map.97.refs_12_.early_ref, f32[8,128]{1,0:T(8,128)S(1)} %get-tuple-element.58.late_ref), custom_call_target="tpu_custom_call" | custom-call | flops 3932160 | bytes 1966080 | tf_op jit(solution)/shard_map/pallas_call | solution.py:315
  87.0 6.1 %all-to-all-done.back_ref = f32[32,2,128]{2,1,0:T(2,128)S(1)} async-done(((f32[32,2,128]{2,1,0:T(2,128)}), f32[32,2,128]{2,1,0:T(2,128)S(1)}, u32[]{:S(2)}, u32[]{:S(2)}) %all-to-all-start) | async-done | bytes 32800 | tf_op jit(solution)/shard_map/all_to_all | solution.py:441
  93.1 1.3 %shard_map.99 = (f32[1,64]{1,0:T(1,128)}, f32[1,1]{1,0:T(1,128)}) custom-call(s32[5]{0:T(128)} %copy-done, f32[32,2,128]{2,1,0:T(2,128)S(1)} %all-to-all-done.back_ref, s32[2,64]{1,0:T(2,128)} %bitcast.33, f32[2,64]{1,0:T(2,128)} %bitcast.34), custom_call_target="tpu_custom_call" | custom-call | tf_op jit(solution)/shard_map/pallas_call | solution.py:347
  (58 shorter events, 0.8 us)
Async XLA Ops:
  1.9 11.7 %collective-permute-start = (bf16[64,1792]{1,0:T(8,128)(2,1)S(1)}, bf16[64,1792]{1,0:T(8,128)(2,1)S(1)}, u32[]{:S(2)}, u32[]{:S(2)}) collective-permute-start(bf16[64,1792]{1,0:T(8,128)(2,1)S(1)} %get-tuple-element.61), channel_id=1, source_target_pairs={{0,3},{1,2},{2,1},{3,0},{4,7},{5,6},{6,5},{7,4},{8,11},{9,10},{10,... | collective-permute-start | bytes 688136 | tf_op jit(solution)/shard_map/ppermute | solution.py:369
  7.0 19.5 %collective-permute-start.1 = (bf16[64,1792]{1,0:T(8,128)(2,1)S(1)}, bf16[64,1792]{1,0:T(8,128)(2,1)S(1)}, u32[]{:S(2)}, u32[]{:S(2)}) collective-permute-start(bf16[64,1792]{1,0:T(8,128)(2,1)S(1)} %get-tuple-element.63), channel_id=1, source_target_pairs={{0,2},{1,3},{2,0},{3,1},{4,6},{5,7},{6,4},{7,5},{8,10},{9,11},{10,... | collective-permute-start | bytes 688136 | tf_op jit(solution)/shard_map/ppermute | solution.py:369
  7.0 19.5 %collective-permute-start.2 = (bf16[64,1792]{1,0:T(8,128)(2,1)S(1)}, bf16[64,1792]{1,0:T(8,128)(2,1)S(1)}, u32[]{:S(2)}, u32[]{:S(2)}) collective-permute-start(bf16[64,1792]{1,0:T(8,128)(2,1)S(1)} %get-tuple-element.62), channel_id=1, source_target_pairs={{0,1},{1,0},{2,3},{3,2},{4,5},{5,4},{6,7},{7,6},{8,9},{9,8},{10,11... | collective-permute-start | bytes 688136 | tf_op jit(solution)/shard_map/ppermute | solution.py:369
  7.7 72.2 %copy-start = (s32[5]{0:T(128)}, s32[5]{0:T(128)S(1)}, u32[]{:S(2)}) copy-start(s32[5]{0:T(128)S(1)} %stack.23.numbers_ref) | copy-start | bytes 64
  7.7 5.2 %copy-start.6 = (bf16[1792]{0:T(1024)(128)(2,1)S(1)}, bf16[1792]{0:T(1024)(128)(2,1)}, u32[]{:S(2)}) copy-start(bf16[1792]{0:T(1024)(128)(2,1)} %param.9) | copy-start | bytes 10756
  7.7 5.2 %copy-start.7 = (s32[64,2]{0,1:T(2,128)S(1)}, s32[64,2]{0,1:T(2,128)}, u32[]{:S(2)}) copy-start(s32[64,2]{0,1:T(2,128)} %param.10) | copy-start | bytes 1540
  7.7 18.8 %copy-start.5 = (bf16[64,1792]{1,0:T(8,128)(2,1)S(1)}, bf16[64,1792]{1,0:T(8,128)(2,1)}, u32[]{:S(2)}) copy-start(bf16[64,1792]{1,0:T(8,128)(2,1)} %param.7) | copy-start | bytes 688132
  10.3 1.3 %copy-start.1 = (bf16[1792,512]{1,0:T(8,128)(2,1)}, bf16[1792,512]{1,0:T(8,128)(2,1)S(1)}, u32[]{:S(2)}) copy-start(bf16[1792,512]{1,0:T(8,128)(2,1)S(1)} %get-tuple-element.36.slab_ref) | copy-start | bytes 5505028
  11.6 1.2 %copy-start.3 = (bf16[1792,512]{1,0:T(8,128)(2,1)}, bf16[1792,512]{1,0:T(8,128)(2,1)S(1)}, u32[]{:S(2)}) copy-start(bf16[1792,512]{1,0:T(8,128)(2,1)S(1)} %get-tuple-element.37.slab_q_ref) | copy-start | bytes 5505028
  28.2 6.3 %collective-permute-start.5 = (bf16[64,1920]{1,0:T(8,128)(2,1)S(1)}, bf16[64,1920]{1,0:T(8,128)(2,1)S(1)}, u32[]{:S(2)}, u32[]{:S(2)}) collective-permute-start(bf16[64,1920]{1,0:T(8,128)(2,1)S(1)} %concatenate.36), channel_id=1, source_target_pairs={{0,8},{4,20},{8,0},{12,28},{16,24},{20,4},{24,16},{28,12},{1,9},{5... | collective-permute-start | bytes 737288 | tf_op jit(solution)/shard_map/ppermute | solution.py:372
  29.7 4.7 %collective-permute-start.6 = (bf16[64,1920]{1,0:T(8,128)(2,1)S(1)}, bf16[64,1920]{1,0:T(8,128)(2,1)S(1)}, u32[]{:S(2)}, u32[]{:S(2)}) collective-permute-start(bf16[64,1920]{1,0:T(8,128)(2,1)S(1)} %concatenate.36), channel_id=1, source_target_pairs={{0,4},{4,0},{8,12},{12,8},{16,20},{20,16},{24,28},{28,24},{1,5},{5... | collective-permute-start | bytes 737288 | tf_op jit(solution)/shard_map/ppermute | solution.py:372
  29.8 14.5 %collective-permute-start.4 = (bf16[64,1920]{1,0:T(8,128)(2,1)S(1)}, bf16[64,1920]{1,0:T(8,128)(2,1)S(1)}, u32[]{:S(2)}, u32[]{:S(2)}) collective-permute-start(bf16[64,1920]{1,0:T(8,128)(2,1)S(1)} %concatenate.36), channel_id=1, source_target_pairs={{0,2},{1,3},{2,0},{3,1},{4,6},{5,7},{6,4},{7,5},{8,10},{9,11},{10,... | collective-permute-start | bytes 737288 | tf_op jit(solution)/shard_map/ppermute | solution.py:369
  29.8 14.6 %collective-permute-start.3 = (bf16[64,1920]{1,0:T(8,128)(2,1)S(1)}, bf16[64,1920]{1,0:T(8,128)(2,1)S(1)}, u32[]{:S(2)}, u32[]{:S(2)}) collective-permute-start(bf16[64,1920]{1,0:T(8,128)(2,1)S(1)} %concatenate.36), channel_id=1, source_target_pairs={{0,1},{1,0},{2,3},{3,2},{4,5},{5,4},{6,7},{7,6},{8,9},{9,8},{10,11... | collective-permute-start | bytes 737288 | tf_op jit(solution)/shard_map/ppermute | solution.py:369
  34.5 10.0 %collective-permute-start.7 = (bf16[64,1920]{1,0:T(8,128)(2,1)S(1)}, bf16[64,1920]{1,0:T(8,128)(2,1)S(1)}, u32[]{:S(2)}, u32[]{:S(2)}) collective-permute-start(bf16[64,1920]{1,0:T(8,128)(2,1)S(1)} %collective-permute-done.6), channel_id=1, source_target_pairs={{0,8},{4,20},{8,0},{12,28},{16,24},{20,4},{24,16},{28,12},{1,9},{5... | collective-permute-start | bytes 737288 | tf_op jit(solution)/shard_map/ppermute | solution.py:372
  35.9 9.2 %collective-permute-start.11 = (bf16[64,1920]{1,0:T(8,128)(2,1)S(1)}, bf16[64,1920]{1,0:T(8,128)(2,1)S(1)}, u32[]{:S(2)}, u32[]{:S(2)}) collective-permute-start(bf16[64,1920]{1,0:T(8,128)(2,1)S(1)} %collective-permute-done.5), channel_id=1, source_target_pairs={{0,4},{4,0},{8,12},{12,8},{16,20},{20,16},{24,28},{28,24},{1,5},{5... | collective-permute-start | bytes 737288 | tf_op jit(solution)/shard_map/ppermute | solution.py:372
  36.0 9.8 %collective-permute-start.13 = (bf16[64,1920]{1,0:T(8,128)(2,1)S(1)}, bf16[64,1920]{1,0:T(8,128)(2,1)S(1)}, u32[]{:S(2)}, u32[]{:S(2)}) collective-permute-start(bf16[64,1920]{1,0:T(8,128)(2,1)S(1)} %collective-permute-done.5), channel_id=1, source_target_pairs={{0,16},{4,12},{8,24},{12,4},{16,0},{20,28},{24,8},{28,20},{1,17},{... | collective-permute-start | bytes 737288 | tf_op jit(solution)/shard_map/ppermute | solution.py:372
  44.2 9.9 %collective-permute-start.16 = (bf16[64,1920]{1,0:T(8,128)(2,1)S(1)}, bf16[64,1920]{1,0:T(8,128)(2,1)S(1)}, u32[]{:S(2)}, u32[]{:S(2)}) collective-permute-start(bf16[64,1920]{1,0:T(8,128)(2,1)S(1)} %collective-permute-done.4), channel_id=1, source_target_pairs={{0,1},{1,0},{2,3},{3,2},{4,5},{5,4},{6,7},{7,6},{8,9},{9,8},{10,11... | collective-permute-start | bytes 737288 | tf_op jit(solution)/shard_map/ppermute | solution.py:369
  44.4 4.3 %copy-start.4 = (bf16[1792,512]{1,0:T(8,128)(2,1)S(1)}, bf16[1792,512]{1,0:T(8,128)(2,1)}, u32[]{:S(2)}) copy-start(bf16[1792,512]{1,0:T(8,128)(2,1)} %copy-done.3) | copy-start | bytes 5505028
  44.4 4.2 %copy-start.2 = (bf16[1792,512]{1,0:T(8,128)(2,1)S(1)}, bf16[1792,512]{1,0:T(8,128)(2,1)}, u32[]{:S(2)}) copy-start(bf16[1792,512]{1,0:T(8,128)(2,1)} %copy-done.1) | copy-start | bytes 5505028
  44.5 6.3 %collective-permute-start.9 = (bf16[128,1920]{1,0:T(8,128)(2,1)S(1)}, bf16[128,1920]{1,0:T(8,128)(2,1)S(1)}, u32[]{:S(2)}, u32[]{:S(2)}) collective-permute-start(bf16[128,1920]{1,0:T(8,128)(2,1)S(1)} %pad_maximum_fusion.2), channel_id=1, source_target_pairs={{0,4},{4,0},{8,12},{12,8},{16,20},{20,16},{24,28},{28,24},{1,5},{5... | collective-permute-start | bytes 1474568 | tf_op jit(solution)/shard_map/ppermute | solution.py:372
  44.6 2.2 %collective-permute-start.12 = (bf16[64,1920]{1,0:T(8,128)(2,1)S(1)}, bf16[64,1920]{1,0:T(8,128)(2,1)S(1)}, u32[]{:S(2)}, u32[]{:S(2)}) collective-permute-start(bf16[64,1920]{1,0:T(8,128)(2,1)S(1)} %collective-permute-done.7), channel_id=1, source_target_pairs={{0,4},{4,0},{8,12},{12,8},{16,20},{20,16},{24,28},{28,24},{1,5},{5... | collective-permute-start | bytes 737288 | tf_op jit(solution)/shard_map/ppermute | solution.py:372
  45.2 8.9 %collective-permute-start.8 = (bf16[128,1920]{1,0:T(8,128)(2,1)S(1)}, bf16[128,1920]{1,0:T(8,128)(2,1)S(1)}, u32[]{:S(2)}, u32[]{:S(2)}) collective-permute-start(bf16[128,1920]{1,0:T(8,128)(2,1)S(1)} %pad_maximum_fusion.2), channel_id=1, source_target_pairs={{0,8},{4,20},{8,0},{12,28},{16,24},{20,4},{24,16},{28,12},{1,9},{5... | collective-permute-start | bytes 1474568 | tf_op jit(solution)/shard_map/ppermute | solution.py:372
  45.8 2.8 %collective-permute-start.14 = (bf16[64,1920]{1,0:T(8,128)(2,1)S(1)}, bf16[64,1920]{1,0:T(8,128)(2,1)S(1)}, u32[]{:S(2)}, u32[]{:S(2)}) collective-permute-start(bf16[64,1920]{1,0:T(8,128)(2,1)S(1)} %collective-permute-done.13), channel_id=1, source_target_pairs={{0,4},{4,0},{8,12},{12,8},{16,20},{20,16},{24,28},{28,24},{1,5},{5... | collective-permute-start | bytes 737288 | tf_op jit(solution)/shard_map/ppermute | solution.py:372
  46.7 14.2 %collective-permute-start.18 = (bf16[64,1920]{1,0:T(8,128)(2,1)S(1)}, bf16[64,1920]{1,0:T(8,128)(2,1)S(1)}, u32[]{:S(2)}, u32[]{:S(2)}) collective-permute-start(bf16[64,1920]{1,0:T(8,128)(2,1)S(1)} %collective-permute-done.13), channel_id=1, source_target_pairs={{0,2},{1,3},{2,0},{3,1},{4,6},{5,7},{6,4},{7,5},{8,10},{9,11},{10,... | collective-permute-start | bytes 737288 | tf_op jit(solution)/shard_map/ppermute | solution.py:369
  50.8 8.9 %collective-permute-start.10 = (bf16[128,1920]{1,0:T(8,128)(2,1)S(1)}, bf16[128,1920]{1,0:T(8,128)(2,1)S(1)}, u32[]{:S(2)}, u32[]{:S(2)}) collective-permute-start(bf16[128,1920]{1,0:T(8,128)(2,1)S(1)} %collective-permute-done.9), channel_id=1, source_target_pairs={{0,8},{4,20},{8,0},{12,28},{16,24},{20,4},{24,16},{28,12},{1,9},{5... | collective-permute-start | bytes 1474568 | tf_op jit(solution)/shard_map/ppermute | solution.py:372
  54.1 9.4 %collective-permute-start.26 = (bf16[128,1920]{1,0:T(8,128)(2,1)S(1)}, bf16[128,1920]{1,0:T(8,128)(2,1)S(1)}, u32[]{:S(2)}, u32[]{:S(2)}) collective-permute-start(bf16[128,1920]{1,0:T(8,128)(2,1)S(1)} %collective-permute-done.8), channel_id=1, source_target_pairs={{0,4},{4,0},{8,12},{12,8},{16,20},{20,16},{24,28},{28,24},{1,5},{5... | collective-permute-start | bytes 1474568 | tf_op jit(solution)/shard_map/ppermute | solution.py:372
  59.7 8.8 %collective-permute-start.21 = (bf16[64,1920]{1,0:T(8,128)(2,1)S(1)}, bf16[64,1920]{1,0:T(8,128)(2,1)S(1)}, u32[]{:S(2)}, u32[]{:S(2)}) collective-permute-start(bf16[64,1920]{1,0:T(8,128)(2,1)S(1)} %collective-permute-done.16), channel_id=1, source_target_pairs={{0,4},{4,0},{8,12},{12,8},{16,20},{20,16},{24,28},{28,24},{1,5},{5... | collective-permute-start | bytes 737288 | tf_op jit(solution)/shard_map/ppermute | solution.py:372
  59.7 10.4 %collective-permute-start.22 = (bf16[64,1920]{1,0:T(8,128)(2,1)S(1)}, bf16[64,1920]{1,0:T(8,128)(2,1)S(1)}, u32[]{:S(2)}, u32[]{:S(2)}) collective-permute-start(bf16[64,1920]{1,0:T(8,128)(2,1)S(1)} %collective-permute-done.16), channel_id=1, source_target_pairs={{0,8},{4,20},{8,0},{12,28},{16,24},{20,4},{24,16},{28,12},{1,9},{5... | collective-permute-start | bytes 737288 | tf_op jit(solution)/shard_map/ppermute | solution.py:372
  60.9 9.2 %collective-permute-start.19 = (bf16[64,1920]{1,0:T(8,128)(2,1)S(1)}, bf16[64,1920]{1,0:T(8,128)(2,1)S(1)}, u32[]{:S(2)}, u32[]{:S(2)}) collective-permute-start(bf16[64,1920]{1,0:T(8,128)(2,1)S(1)} %collective-permute-done.18), channel_id=1, source_target_pairs={{0,1},{1,0},{2,3},{3,2},{4,5},{5,4},{6,7},{7,6},{8,9},{9,8},{10,11... | collective-permute-start | bytes 737288 | tf_op jit(solution)/shard_map/ppermute | solution.py:369
  61.8 13.1 %collective-permute-start.15 = (bf16[128,1920]{1,0:T(8,128)(2,1)S(1)}, bf16[128,1920]{1,0:T(8,128)(2,1)S(1)}, u32[]{:S(2)}, u32[]{:S(2)}) collective-permute-start(bf16[128,1920]{1,0:T(8,128)(2,1)S(1)} %collective-permute-done.8), channel_id=1, source_target_pairs={{0,16},{4,12},{8,24},{12,4},{16,0},{20,28},{24,8},{28,20},{1,17},{... | collective-permute-start | bytes 1474568 | tf_op jit(solution)/shard_map/ppermute | solution.py:372
  63.5 12.0 %collective-permute-start.27 = (bf16[128,1920]{1,0:T(8,128)(2,1)S(1)}, bf16[128,1920]{1,0:T(8,128)(2,1)S(1)}, u32[]{:S(2)}, u32[]{:S(2)}) collective-permute-start(bf16[128,1920]{1,0:T(8,128)(2,1)S(1)} %collective-permute-done.10), channel_id=1, source_target_pairs={{0,4},{4,0},{8,12},{12,8},{16,20},{20,16},{24,28},{28,24},{1,5},{5... | collective-permute-start | bytes 1474568 | tf_op jit(solution)/shard_map/ppermute | solution.py:372
  68.5 6.3 %collective-permute-start.23 = (bf16[64,1920]{1,0:T(8,128)(2,1)S(1)}, bf16[64,1920]{1,0:T(8,128)(2,1)S(1)}, u32[]{:S(2)}, u32[]{:S(2)}) collective-permute-start(bf16[64,1920]{1,0:T(8,128)(2,1)S(1)} %collective-permute-done.21), channel_id=1, source_target_pairs={{0,8},{4,20},{8,0},{12,28},{16,24},{20,4},{24,16},{28,12},{1,9},{5... | collective-permute-start | bytes 737288 | tf_op jit(solution)/shard_map/ppermute | solution.py:372
  70.1 4.8 %collective-permute-start.24 = (bf16[64,1920]{1,0:T(8,128)(2,1)S(1)}, bf16[64,1920]{1,0:T(8,128)(2,1)S(1)}, u32[]{:S(2)}, u32[]{:S(2)}) collective-permute-start(bf16[64,1920]{1,0:T(8,128)(2,1)S(1)} %collective-permute-done.22), channel_id=1, source_target_pairs={{0,4},{4,0},{8,12},{12,8},{16,20},{20,16},{24,28},{28,24},{1,5},{5... | collective-permute-start | bytes 737288 | tf_op jit(solution)/shard_map/ppermute | solution.py:372
  70.2 4.6 %collective-permute-start.20 = (bf16[64,1920]{1,0:T(8,128)(2,1)S(1)}, bf16[64,1920]{1,0:T(8,128)(2,1)S(1)}, u32[]{:S(2)}, u32[]{:S(2)}) collective-permute-start(bf16[64,1920]{1,0:T(8,128)(2,1)S(1)} %collective-permute-done.19), channel_id=1, source_target_pairs={{0,4},{4,0},{8,12},{12,8},{16,20},{20,16},{24,28},{28,24},{1,5},{5... | collective-permute-start | bytes 737288 | tf_op jit(solution)/shard_map/ppermute | solution.py:372
  74.8 1.5 %collective-permute-start.25 = (bf16[64,1920]{1,0:T(8,128)(2,1)S(1)}, bf16[64,1920]{1,0:T(8,128)(2,1)S(1)}, u32[]{:S(2)}, u32[]{:S(2)}) collective-permute-start(bf16[64,1920]{1,0:T(8,128)(2,1)S(1)} %collective-permute-done.23), channel_id=1, source_target_pairs={{0,4},{4,0},{8,12},{12,8},{16,20},{20,16},{24,28},{28,24},{1,5},{5... | collective-permute-start | bytes 737288 | tf_op jit(solution)/shard_map/ppermute | solution.py:372
  74.9 4.8 %collective-permute-start.17 = (bf16[128,1920]{1,0:T(8,128)(2,1)S(1)}, bf16[128,1920]{1,0:T(8,128)(2,1)S(1)}, u32[]{:S(2)}, u32[]{:S(2)}) collective-permute-start(bf16[128,1920]{1,0:T(8,128)(2,1)S(1)} %collective-permute-done.15), channel_id=1, source_target_pairs={{0,4},{4,0},{8,12},{12,8},{16,20},{20,16},{24,28},{28,24},{1,5},{5... | collective-permute-start | bytes 1474568 | tf_op jit(solution)/shard_map/ppermute | solution.py:372
  83.0 10.1 %all-to-all-start = ((f32[32,2,128]{2,1,0:T(2,128)}), f32[32,2,128]{2,1,0:T(2,128)S(1)}, u32[]{:S(2)}, u32[]{:S(2)}) async-start(f32[32,2,128]{2,1,0:T(2,128)} %get-tuple-element.55), calls=%async_computation | async-start | bytes 65536 | tf_op jit(solution)/shard_map/all_to_all | solution.py:441
